TPU v7x, 512 devices: a whole 4x8x8 slice. The times are simulated.
512 devices in a mesh: table: 32 (over x_lo, z, core), dp: 16 (over x_hi, y).
Axes of the slice: x: 4 (x_hi: 2, x_lo: 2; x = x_hi * 2 + x_lo), y: 8, z: 8, core: 2. Of those that a mesh axis runs over, the one named last changes fastest.
Arguments:
- ids: int32 [32, 8192, 128], P('table', 'dp'), may hold values from 0 to 1023
- mults: int32 [32, 8192, 128], P('table', 'dp'), may hold values from 0 to 2
- table: bfloat16 [32768, 128], P('table'), may hold values from -0.625 to 0.625
- user_layer: bfloat16 [1024, 512], replicated, may hold values from -0.1875 to 0.1875
- user_head: bfloat16 [512, 128], replicated, may hold values from -0.25 to 0.25
- item_layer: bfloat16 [1024, 512], replicated, may hold values from -0.1875 to 0.1875
- item_head: bfloat16 [512, 128], replicated, may hold values from -0.25 to 0.25
- counts: int32 [16, 512], P('dp', 'table'), may hold values from 1 to 256
Outputs:
- losses: float32 [16, 512], P('dp', 'table')
- table_change: float32 [32768, 128], P('table')
- user_layer_change: float32 [1024, 512], P('table')
- user_head_change: float32 [512, 128], P('table')
- item_layer_change: float32 [1024, 512], P('table')
- item_head_change: float32 [512, 128], P('table')
All inputs are finite; a program needn't handle non-finite values.
Results may differ from a plain program's by a relative error of at most 0.039.
Values may be sent and summed in bfloat16 or wider, within the bound.
No kernel may reach another device: no remote copies, remote signals or barrier semaphores. Data moves between devices by JAX's collectives and lax.ppermute only.
A program may use at most 64 MiB of HBM per device.

v0:
```python
import jax
import jax.numpy as jnp
from jax import lax
from jax.sharding import PartitionSpec as P

LOOKUPS = 8


INVERSE_TEMP = 20.0
EPSILON = 1e-06


def silu_slope(pre):
    gate = jax.nn.sigmoid(pre)
    return gate * (1.0 + pre * (1.0 - gate))


def run_tower(pooled_in, layer, head):
    pre = jnp.dot(pooled_in, layer, preferred_element_type=jnp.float32)
    hidden = jax.nn.silu(pre).astype(jnp.bfloat16)
    output = jnp.dot(hidden, head, preferred_element_type=jnp.float32)
    scale = lax.rsqrt(jnp.sum(output * output, axis=-1, keepdims=True) + EPSILON)
    return (pre, hidden, output * scale, scale)


def tower_back(d_unit, unit, scale, pre, hidden, pooled_in, head):
    along = jnp.sum(unit * d_unit, axis=-1, keepdims=True)
    d_output = ((d_unit - unit * along) * scale).astype(jnp.bfloat16)
    back = lax.dot_general(
        d_output, head, (((1,), (1,)), ((), ())), preferred_element_type=jnp.float32
    )
    d_hidden = (back * silu_slope(pre)).astype(jnp.bfloat16)
    layer_term = lax.dot_general(
        pooled_in, d_hidden, (((0,), (0,)), ((), ())), preferred_element_type=jnp.float32
    )
    head_term = lax.dot_general(
        hidden, d_output, (((0,), (0,)), ((), ())), preferred_element_type=jnp.float32
    )
    return (d_output, d_hidden, layer_term, head_term)


def input_grads(d_hidden, layer):
    return lax.dot_general(
        d_hidden, layer, (((1,), (1,)), ((), ())), preferred_element_type=jnp.float32
    ).astype(jnp.bfloat16)


def shards(ids, mults, table, user_layer, user_head, item_layer, item_head, counts):
    table_count = lax.axis_size("table")
    rows_dev, emb_width = table.shape
    group_rows = ids.shape[1]
    feature_count = ids.shape[2] // LOOKUPS
    own_rows = group_rows // table_count
    user_width = user_layer.shape[0]
    id_blocks = ids[0].reshape(group_rows, feature_count, LOOKUPS).transpose(1, 0, 2)
    mult_blocks = mults[0].reshape(group_rows, feature_count, LOOKUPS).transpose(1, 0, 2)
    table_rows = lax.broadcasted_iota(jnp.int32, (1, rows_dev), 1)

    def lookup_weights(id_block, mult_block):
        running = jnp.zeros((group_rows, rows_dev), jnp.float32)
        for lookup in range(LOOKUPS):
            hit = id_block[:, lookup : lookup + 1] == table_rows
            running = running + jnp.where(
                hit, mult_block[:, lookup : lookup + 1].astype(jnp.float32), 0.0
            )
        return running.astype(jnp.bfloat16)

    def pool_feature(lookup_pair):
        weights = lookup_weights(lookup_pair[0], lookup_pair[1])
        return jnp.dot(weights, table, preferred_element_type=jnp.float32).astype(jnp.bfloat16)

    partial_value = lax.map(pool_feature, (id_blocks, mult_blocks))
    received = lax.all_to_all(partial_value, "table", split_axis=1, concat_axis=1, tiled=True)
    pooled = jnp.sum(
        received.astype(jnp.float32).reshape(feature_count, table_count, own_rows, emb_width),
        axis=1,
    ).astype(jnp.bfloat16)
    pooled = pooled.transpose(1, 0, 2).reshape(own_rows, feature_count * emb_width)
    user_in = pooled[:, :user_width]
    item_in = pooled[:, user_width:]
    user_pre, user_hidden, user_unit, user_scale = run_tower(user_in, user_layer, user_head)
    item_pre, item_hidden, item_unit, item_scale = run_tower(item_in, item_layer, item_head)
    user_vector = user_unit.astype(jnp.bfloat16)
    item_vector = item_unit.astype(jnp.bfloat16)
    item_rows, item_counts = (
        lax.all_gather(item_vector, "dp", axis=0, tiled=True),
        lax.all_gather(counts[0].astype(jnp.bfloat16), "dp", axis=0, tiled=True),
    )
    log_freq = jnp.log(item_counts.astype(jnp.float32))
    scores = (
        INVERSE_TEMP
        * lax.dot_general(
            user_vector, item_rows, (((1,), (1,)), ((), ())), preferred_element_type=jnp.float32
        )
        - log_freq[None, :]
    )
    lse = jnp.log(jnp.sum(jnp.exp(scores), axis=-1))
    own_index = lax.axis_index("dp") * own_rows + lax.broadcasted_iota(jnp.int32, (own_rows,), 0)
    columns = lax.broadcasted_iota(jnp.int32, scores.shape, 1)
    is_positive = columns == own_index[:, None]
    positive = jnp.sum(jnp.where(is_positive, scores, 0.0), axis=-1)
    losses = (lse - positive)[None, :]
    dscore = (jnp.exp(scores - lse[:, None]) - is_positive.astype(jnp.float32)).astype(jnp.bfloat16)
    d_user = INVERSE_TEMP * jnp.dot(dscore, item_rows, preferred_element_type=jnp.float32)
    item_terms = INVERSE_TEMP * lax.dot_general(
        dscore, user_vector, (((0,), (0,)), ((), ())), preferred_element_type=jnp.float32
    )
    d_item = lax.psum_scatter(
        item_terms.astype(jnp.bfloat16), "dp", scatter_dimension=0, tiled=True
    ).astype(jnp.float32)
    user_dout, user_dhid, user_layer_term, user_head_term = tower_back(
        d_user, user_unit, user_scale, user_pre, user_hidden, user_in, user_head
    )
    item_dout, item_dhid, item_layer_term, item_head_term = tower_back(
        d_item, item_unit, item_scale, item_pre, item_hidden, item_in, item_head
    )
    own_grads = jnp.concatenate(
        [input_grads(user_dhid, user_layer), input_grads(item_dhid, item_layer)], axis=1
    )
    group_grads = lax.all_gather(own_grads, "table", axis=0, tiled=True)

    def add_feature(feature, running):
        weights = lookup_weights(id_blocks[feature], mult_blocks[feature])
        column = lax.dynamic_slice_in_dim(group_grads, feature * emb_width, emb_width, 1)
        return running + lax.dot_general(
            weights, column, (((0,), (0,)), ((), ())), preferred_element_type=jnp.float32
        )

    table_part = lax.fori_loop(
        0, feature_count, add_feature, jnp.zeros((rows_dev, emb_width), jnp.float32)
    )
    layer_rows = (
        lax.psum_scatter(
            user_layer_term.astype(jnp.bfloat16), "table", scatter_dimension=0, tiled=True
        ).astype(jnp.float32),
        lax.psum_scatter(
            user_head_term.astype(jnp.bfloat16), "table", scatter_dimension=0, tiled=True
        ).astype(jnp.float32),
        lax.psum_scatter(
            item_layer_term.astype(jnp.bfloat16), "table", scatter_dimension=0, tiled=True
        ).astype(jnp.float32),
        lax.psum_scatter(
            item_head_term.astype(jnp.bfloat16), "table", scatter_dimension=0, tiled=True
        ).astype(jnp.float32),
    )
    totals = (
        lax.psum(table_part.astype(jnp.bfloat16), "dp").astype(jnp.float32),
        lax.psum(layer_rows[0].astype(jnp.bfloat16), "dp").astype(jnp.float32),
        lax.psum(layer_rows[1].astype(jnp.bfloat16), "dp").astype(jnp.float32),
        lax.psum(layer_rows[2].astype(jnp.bfloat16), "dp").astype(jnp.float32),
        lax.psum(layer_rows[3].astype(jnp.bfloat16), "dp").astype(jnp.float32),
    )
    return (losses, totals[0], totals[1], totals[2], totals[3], totals[4])


def solution(mesh):
    in_specs = (
        P("table", "dp", None),
        P("table", "dp", None),
        P("table", None),
        P(),
        P(),
        P(),
        P(),
        P("dp", "table"),
    )
    out_specs = (
        P("dp", "table"),
        P("table", None),
        P("table", None),
        P("table", None),
        P("table", None),
        P("table", None),
    )
    return jax.shard_map(shards, mesh=mesh, in_specs=in_specs, out_specs=out_specs, check_vma=False)
```

profile of v0, /device:TPU:64, one launch (start us, length us, event | category | flops | bytes accessed | tf_op | source)
XLA Modules:
  0.0 1200.2 jit_solution(2960699495812224737)
XLA Ops:
  10.2 70.1 %while.27 = (s32[]{:T(128)}, bf16[16,512,128]{2,1,0:T(8,128)(2,1)S(1)}, s32[16,512,8]{1,2,0:T(8,128)S(1)}, s32[16,512,8]{1,2,0:T(8,128)}, bf16[1024,128]{1,0:T(8,128)(2,1)}, /*index=5*/s32[]{:T(128)}) while((s32[]{:T(128)}, bf16[16,512,128]{2,1,0:T(8,128)(2,1)S(1)}, s32[16,512,8]{1,2,0:T(8,128)S(1)}, ...), condition=%wide.region_1.2_spmd.clone.clone, body=%wide.region_0.1_spmd.clone.clone.sunk | while | flops 146870272 | bytes 557133 | solution.py:72
  10.9 3.6 fusion.86
  15.3 3.6 fusion.86
  19.7 3.6 fusion.86
  24.1 3.6 fusion.86
  28.4 3.6 fusion.86
  32.8 3.6 fusion.86
  37.2 3.6 fusion.86
  41.6 3.6 fusion.86
  46.0 3.6 fusion.86
  50.4 3.6 fusion.86
  54.7 3.6 fusion.86
  59.1 3.6 fusion.86
  63.5 3.6 fusion.86
  67.9 3.6 fusion.86
  72.3 3.6 fusion.86
  76.7 3.6 fusion.86
  83.0 11.2 all-to-all-start
  96.4 42.9 %all-reduce = bf16[256]{0:T(256)(128)(2,1)S(1)} all-reduce(bf16[256]{0:T(256)(128)(2,1)S(1)} %dynamic-update-slice), channel_id=2, replica_groups=mesh['table'=32,'dp'=16] {'dp'}, use_global_device_ids=true, to_apply=%add | all-reduce | flops 256 | bytes 1024
  139.3 6.3 all-to-all-done
  148.7 41.5 %all_gather.9 = bf16[256,128]{1,0:T(8,128)(2,1)S(1)} all-gather(bf16[16,128]{1,0:T(8,128)(2,1)S(1)} %multiply_convert_fusion.3), channel_id=1, replica_groups=mesh['table'=32,'dp'=16] {'dp'}, dimensions={0}, use_global_device_ids=true | all-gather | bytes 69632 | tf_op jit(solution)/shard_map/all_gather | solution.py:86
  193.9 146.1 %reduce-scatter.6.cloned.1.call-done = bf16[16,128]{1,0:T(8,128)(2,1)} async-done(((bf16[256,128]{1,0:T(8,128)(2,1)}), bf16[16,128]{1,0:T(8,128)(2,1)}) %reduce-scatter.6.cloned.1.call-update) | async-done | bytes 4112 | tf_op jit(solution)/shard_map/reduce_scatter | solution.py:108
  347.4 108.6 %reduce-scatter.10.cloned.1.call-done = bf16[16,128]{1,0:T(8,128)(2,1)} async-done(((bf16[512,128]{1,0:T(8,128)(2,1)}), bf16[16,128]{1,0:T(8,128)(2,1)}) %reduce-scatter.10.cloned.1.call-update) | async-done | bytes 4112 | tf_op jit(solution)/shard_map/reduce_scatter | solution.py:136
  456.1 117.0 %reduce-scatter.14.cloned.1.call-done = bf16[16,128]{1,0:T(8,128)(2,1)} async-done(((bf16[512,128]{1,0:T(8,128)(2,1)}), bf16[16,128]{1,0:T(8,128)(2,1)}) %reduce-scatter.14.cloned.1.call-update) | async-done | bytes 4112 | tf_op jit(solution)/shard_map/reduce_scatter | solution.py:142
  573.1 118.4 %reduce-scatter.8.cloned.1.call-done = bf16[32,512]{1,0:T(8,128)(2,1)} async-done(((bf16[1024,512]{1,0:T(8,128)(2,1)}), bf16[32,512]{1,0:T(8,128)(2,1)}) %reduce-scatter.8.cloned.1.call-update) | async-done | bytes 32784 | tf_op jit(solution)/shard_map/reduce_scatter | solution.py:133
  691.5 118.2 %reduce-scatter.12.cloned.1.call-done = bf16[32,512]{1,0:T(8,128)(2,1)} async-done(((bf16[1024,512]{1,0:T(8,128)(2,1)}), bf16[32,512]{1,0:T(8,128)(2,1)}) %reduce-scatter.12.cloned.1.call-update) | async-done | bytes 32784 | tf_op jit(solution)/shard_map/reduce_scatter | solution.py:139
  809.8 69.1 %all-gather.3.cloned.1.call-done = bf16[512,2048]{1,0:T(8,128)(2,1)} async-done(((bf16[16,2048]{1,0:T(8,128)(2,1)}), bf16[512,2048]{1,0:T(8,128)(2,1)}) %all-gather.3.cloned.1.call-update) | async-done | bytes 2097168 | tf_op jit(solution)/shard_map/all_gather | solution.py:120
  878.9 68.7 %while.28 = (s32[]{:T(128)}, f32[1024,128]{1,0:T(8,128)S(1)}, s32[16,512,8]{1,2,0:T(8,128)S(1)}, s32[16,512,8]{1,2,0:T(8,128)}, bf16[512,2048]{1,0:T(8,128)(2,1)...) while((s32[]{:T(128)}, f32[1024,128]{1,0:T(8,128)S(1)}, ...), condition=%wide.region_11.12_spmd.clone.clone, body=%wide.region_10.11_spmd.clone.clone.sunk | while | flops 147066880 | bytes 1343645 | solution.py:129
  892.6 3.5 convolution_add_fusion.2
  944.1 3.5 convolution_add_fusion.2
  948.4 83.4 %all-reduce.7.cloned.1.call-done = (bf16[32,512]{1,0:T(8,128)(2,1)}, bf16[16,128]{1,0:T(8,128)(2,1)}, bf16[32,512]{1,0:T(8,128)(2,1)}, bf16[16,128]{1,0:T(8,128)(2,1)}) async-done(((bf16[32,512]{1,0:T(8,128)(2,1)}, bf16[16,128]{1,0:T(8,128)(2,1)}, bf16[32,512]{1,0:T(8,128)(2,1)}, bf16[16,128]{1,0:T(8,128)(2,1)}), (bf16[32,512]{1,0:T(8,128)(2,1)}, bf16[16,128]{1,0:T(8,128)(2,1)}, bf16[32,512]{1,0:T(8,128)(2,1)}, ...) | async-done | bytes 73744 | tf_op jit(solution)/shard_map/psum | solution.py:148
  1037.1 154.5 %all-reduce.5.cloned.1.call-done = bf16[1024,128]{1,0:T(8,128)(2,1)} async-done(((bf16[1024,128]{1,0:T(8,128)(2,1)}), bf16[1024,128]{1,0:T(8,128)(2,1)}) %all-reduce.5.cloned.1.call-update) | async-done | bytes 262160 | tf_op jit(solution)/shard_map/psum | solution.py:147
  (178 shorter events, 102.3 us)
Async XLA Ops:
  7.2 183.0 %copy-start = (bf16[1024,512]{1,0:T(8,128)(2,1)S(1)}, bf16[1024,512]{1,0:T(8,128)(2,1)}, u32[]{:S(2)}) copy-start(bf16[1024,512]{1,0:T(8,128)(2,1)} %param.15) | copy-start | bytes 3145732
  83.0 13.2 %copy-start.4 = (s32[1,16]{1,0:T(1,128)S(1)}, s32[1,16]{1,0:T(1,128)}, u32[]{:S(2)}) copy-start(s32[1,16]{1,0:T(1,128)} %param.19) | copy-start | bytes 196
  83.0 62.7 %all-to-all-start = ((bf16[16,512,128]{2,0,1:T(8,128)(2,1)}), bf16[16,512,128]{2,0,1:T(8,128)(2,1)S(1)}, u32[]{:S(2)}, u32[]{:S(2)}) async-start(bf16[16,512,128]{2,0,1:T(8,128)(2,1)} %copy.20), calls=%async_computation | async-start | bytes 4194304 | tf_op jit(solution)/shard_map/all_to_all | solution.py:73
  94.2 245.8 %reduce-scatter.6.cloned.1.call-start = ((), (), s32[]{:S(2)}) async-start(), calls=%async_computation.6 | async-start | bytes 69632 | tf_op jit(solution)/shard_map/reduce_scatter | solution.py:108
  145.9 44.5 %copy-start.2 = (bf16[512,128]{1,0:T(8,128)(2,1)S(1)}, bf16[512,128]{1,0:T(8,128)(2,1)}, u32[]{:S(2)}) copy-start(bf16[512,128]{1,0:T(8,128)(2,1)} %param.16) | copy-start | bytes 393220
  190.4 153.8 %copy-start.3 = (bf16[512,128]{1,0:T(8,128)(2,1)S(1)}, bf16[512,128]{1,0:T(8,128)(2,1)}, u32[]{:S(2)}) copy-start(bf16[512,128]{1,0:T(8,128)(2,1)} %param.18) | copy-start | bytes 393220
  192.8 263.3 %reduce-scatter.10.cloned.1.call-start = ((), (), s32[]{:S(2)}) async-start(), calls=%async_computation.10 | async-start | bytes 135168 | tf_op jit(solution)/shard_map/reduce_scatter | solution.py:136
  193.8 379.2 %reduce-scatter.14.cloned.1.call-start = ((), (), s32[]{:S(2)}) async-start(), calls=%async_computation.12 | async-start | bytes 135168 | tf_op jit(solution)/shard_map/reduce_scatter | solution.py:142
  342.5 349.0 %reduce-scatter.8.cloned.1.call-start = ((), (), s32[]{:S(2)}) async-start(), calls=%async_computation.9 | async-start | bytes 1081344 | tf_op jit(solution)/shard_map/reduce_scatter | solution.py:133
  344.2 2.1 copy-start.1
  344.2 465.5 %reduce-scatter.12.cloned.1.call-start = ((), (), s32[]{:S(2)}) async-start(), calls=%async_computation.11 | async-start | bytes 1081344 | tf_op jit(solution)/shard_map/reduce_scatter | solution.py:139
  345.9 533.1 %all-gather.3.cloned.1.call-start = ((), (), s32[]{:S(2)}) async-start(), calls=%async_computation.7 | async-start | bytes 2162688 | tf_op jit(solution)/shard_map/all_gather | solution.py:120
  347.4 684.4 %all-reduce.7.cloned.1.call-start = ((), (), s32[]{:S(2)}) async-start(), calls=%async_computation.13 | async-start | bytes 147456 | tf_op jit(solution)/shard_map/psum | solution.py:148
  809.7 381.8 %all-reduce.5.cloned.1.call-start = ((), (), s32[]{:S(2)}) async-start(), calls=%async_computation.8 | async-start | bytes 524288 | tf_op jit(solution)/shard_map/psum | solution.py:147
Sparse Core Ops, SparseCore 0:
  192.9 147.0 reduce-scatter.5
  343.0 113.0 reduce-scatter.9
  458.9 114.1 reduce-scatter.13
  576.0 115.5 reduce-scatter.7
  694.1 115.5 reduce-scatter.11
  812.5 66.3 all-gather.2
  882.4 149.2 all-reduce.6
  1035.2 156.3 all-reduce.4
where the time goes:
time: 1200 us
  waiting for transfers between devices  922 us (77%)
  matrix products  124 us (10%)
  blocking collectives  84.4 us (7%)
  local copies, waits for them, and re-layouts  30.9 us (3%)
  between operations  14.9 us (1%)
    psum x1, waiting for transfers between devices, shards(): lax.psum(table_part.astype(jnp.bfloat16), 'dp').astype(jnp.float32)  155 us
    reduce_scatter x1, waiting for transfers between devices, shards(): lax.psum_scatter(item_terms.astype(jnp.bfloat16), 'dp', scatter_dimension...  146 us
    reduce_scatter x1, waiting for transfers between devices, shards(): lax.psum_scatter(user_layer_term.astype(jnp.bfloat16), 'table', scatter_d...  118 us
    reduce_scatter x1, waiting for transfers between devices, shards(): lax.psum_scatter(item_layer_term.astype(jnp.bfloat16), 'table', scatter_d...  118 us
    reduce_scatter x1, waiting for transfers between devices, shards(): lax.psum_scatter(item_head_term.astype(jnp.bfloat16), 'table', scatter_di...  117 us
    reduce_scatter x1, waiting for transfers between devices, shards(): lax.psum_scatter(user_head_term.astype(jnp.bfloat16), 'table', scatter_di...  109 us
    psum x1, waiting for transfers between devices, shards(): lax.psum(layer_rows[0].astype(jnp.bfloat16), 'dp').astype(jnp.float32)  83.4 us
    all_gather x1, waiting for transfers between devices, shards(): group_grads = lax.all_gather(own_grads, 'table', axis=0, tiled=True)  69.1 us
  transfers between devices with their start and end apart: 9, of which 9 were waited for; matrix products, arithmetic and copies ran while one was open for 7% of the time, Pallas kernels for 0%

commit v1 on v0

v1 whole, which is shorter than its diff:
```python
import jax
import jax.numpy as jnp
from jax import lax
from jax.experimental import pallas as pl
from jax.experimental.pallas import tpu as pltpu
from jax.sharding import Mesh
from jax.sharding import PartitionSpec as P

LOOKUPS = 8
INVERSE_TEMP = 20.0
EPSILON = 1e-06

AXES = {"x_lo": 2, "z": 8, "core": 2, "x_hi": 2, "y": 8}
TABLE = ("x_lo", "z", "core")
CHIPS = ("x_lo", "z")
DP = ("x_hi", "y")
N_CHIP = 16
N_DP = 16
OWN = 16
FEATURES = 16
TOWER_FEATURES = 8
ROWS = 1024
EMB = 128
HID = 512
OUT = 128
BLOCK = OWN * FEATURES
IN_WIDTH = TOWER_FEATURES * EMB
GRAD_WIDTH = 12 * 128
COLUMNS_AT = 2 * HID + 2 * OUT
CHUNK = 96

BF16 = jnp.bfloat16
F32 = jnp.float32
PARAMS = pltpu.CompilerParams(vmem_limit_bytes=56 * 1024 * 1024)

NT = (((1,), (1,)), ((), ()))
TN = (((0,), (0,)), ((), ()))


def dot(left, right, dims=(((1,), (0,)), ((), ()))):
    return lax.dot_general(left, right, dims, preferred_element_type=F32)


def whole():
    return pl.BlockSpec(memory_space=pltpu.VMEM)


def pool_kernel(core_ref, ids_ref, mults_ref, table_ref, weights_ref, partial_ref):
    ids = ids_ref[...]
    lane = lax.broadcasted_iota(jnp.int32, ids.shape, 1)
    high = lax.shift_right_logical(ids, 7) * FEATURES + lax.shift_right_logical(lane, 3)
    high = high.astype(F32)
    low = (ids & 127).astype(F32)
    mults = mults_ref[...].astype(F32)
    row = lax.broadcasted_iota(jnp.int32, (128, 128), 0).astype(F32)
    zero = jnp.zeros((128, 128), F32)
    one = jnp.ones((128, 128), F32)
    for n in range(OWN):
        left = jnp.where(high[n : n + 1] == row, mults[n : n + 1], zero).astype(BF16)
        right = jnp.where(low[n : n + 1] == row, one, zero).astype(BF16)
        hits = dot(left, right, NT).astype(BF16)
        for h in range(8):
            weights_ref[n * FEATURES : (n + 1) * FEATURES, h * 128 : (h + 1) * 128] = hits[
                h * FEATURES : (h + 1) * FEATURES
            ]
    partial_ref[...] = dot(weights_ref[...], table_ref[...]).astype(BF16)


def pool(core, ids, mults, table):
    def picked(i, core_ref):
        return (2 * i + core_ref[0], 0)

    def at(i, core_ref):
        return (i, 0)

    return pl.pallas_call(
        pool_kernel,
        grid_spec=pltpu.PrefetchScalarGridSpec(
            num_scalar_prefetch=1,
            grid=(N_CHIP,),
            in_specs=[
                pl.BlockSpec((OWN, 128), picked),
                pl.BlockSpec((OWN, 128), picked),
                pl.BlockSpec((ROWS, EMB), lambda i, core_ref: (0, 0)),
            ],
            out_specs=[pl.BlockSpec((BLOCK, ROWS), at), pl.BlockSpec((BLOCK, EMB), at)],
        ),
        out_shape=[
            jax.ShapeDtypeStruct((N_CHIP * BLOCK, ROWS), BF16),
            jax.ShapeDtypeStruct((N_CHIP * BLOCK, EMB), BF16),
        ],
        compiler_params=PARAMS,
        cost_estimate=pl.CostEstimate(
            flops=2 * N_CHIP * BLOCK * ROWS * EMB * 2, bytes_accessed=10 * 2**20, transcendentals=0
        ),
        name="pool",
    )(core, ids, mults, table)


def column_of(row):
    eye = lax.broadcasted_iota(jnp.int32, (OWN, OWN), 0) == lax.broadcasted_iota(
        jnp.int32, (OWN, OWN), 1
    )
    return jnp.sum(jnp.where(eye, row, 0.0), axis=1, keepdims=True)


def row_of(column):
    eye = lax.broadcasted_iota(jnp.int32, (OWN, OWN), 0) == lax.broadcasted_iota(
        jnp.int32, (OWN, OWN), 1
    )
    return jnp.sum(jnp.where(eye, column, 0.0), axis=0, keepdims=True)


def tower_kernel(
    parts_ref, counts_ref, layer0_ref, head0_ref, layer1_ref, head1_ref,
    pooled_ref, pre_ref, hidden_ref, unit_ref, scale_ref, send_ref, rows_ref,
):
    total = parts_ref[0].astype(F32)
    for s in range(1, N_CHIP):
        total = total + parts_ref[s].astype(F32)
    rows_ref[...] = total
    for f in range(FEATURES):
        pooled_ref[:, f * EMB : (f + 1) * EMB] = rows_ref[
            pl.ds(f, OWN, stride=FEATURES), :
        ].astype(BF16)
    for tower, (layer_ref, head_ref) in enumerate(((layer0_ref, head0_ref), (layer1_ref, head1_ref))):
        pooled = pooled_ref[:, tower * IN_WIDTH : (tower + 1) * IN_WIDTH]
        pre = dot(pooled, layer_ref[...])
        hidden = (pre * (1.0 / (1.0 + jnp.exp(-pre)))).astype(BF16)
        output = dot(hidden, head_ref[...])
        scale = lax.rsqrt(jnp.sum(output * output, axis=-1, keepdims=True) + EPSILON)
        unit = output * scale
        pre_ref[:, tower * HID : (tower + 1) * HID] = pre
        hidden_ref[:, tower * HID : (tower + 1) * HID] = hidden
        unit_ref[:, tower * OUT : (tower + 1) * OUT] = unit
        scale_ref[:, tower * OUT : (tower + 1) * OUT] = jnp.broadcast_to(scale, (OWN, OUT))
        rounded = unit.astype(BF16)
        for d in range(N_DP):
            send_ref[d, tower * OWN : (tower + 1) * OWN, :] = rounded
    counts = column_of(counts_ref[...].astype(F32))
    spread = jnp.broadcast_to(counts, (OWN, 128)).astype(BF16)
    for d in range(N_DP):
        send_ref[d, 2 * OWN : 3 * OWN, :] = spread


def towers(parts, counts, layer0, head0, layer1, head1):
    return pl.pallas_call(
        tower_kernel,
        in_specs=[whole()] * 6,
        out_specs=[whole()] * 6,
        out_shape=[
            jax.ShapeDtypeStruct((OWN, FEATURES * EMB), BF16),
            jax.ShapeDtypeStruct((OWN, 2 * HID), F32),
            jax.ShapeDtypeStruct((OWN, 2 * HID), BF16),
            jax.ShapeDtypeStruct((OWN, 2 * OUT), F32),
            jax.ShapeDtypeStruct((OWN, 2 * OUT), F32),
            jax.ShapeDtypeStruct((N_DP, 3 * OWN, 128), BF16),
        ],
        scratch_shapes=[pltpu.VMEM((BLOCK, EMB), F32)],
        compiler_params=PARAMS,
        name="towers",
    )(parts, counts, layer0, head0, layer1, head1)


def softmax_kernel(
    place_ref, group_ref, counts_ref, pooled_ref, pre_ref, hidden_ref, unit_ref, scale_ref,
    head0_ref, head1_ref, losses_ref, send_ref,
):
    size = N_DP * OWN
    group = group_ref[...]
    users = group[:, :OWN].reshape(size, OUT)
    items = group[:, OWN : 2 * OWN].reshape(size, OUT)
    log_freq = jnp.log(group[:, 2 * OWN :].reshape(size, 128).astype(F32))
    log_row = jnp.transpose(log_freq)[:1]
    own_log = jnp.log(column_of(counts_ref[...].astype(F32)))
    own_user = unit_ref[:, :OUT].astype(BF16)
    own_item = unit_ref[:, OUT:].astype(BF16)
    first = place_ref[0] * OWN
    mine = lax.broadcasted_iota(jnp.int32, (OWN, size), 1) == (
        lax.broadcasted_iota(jnp.int32, (OWN, size), 0) + first
    )
    down = INVERSE_TEMP * dot(items, users, NT) - jnp.concatenate([log_freq, log_freq], axis=1)
    lse_row = jnp.log(jnp.sum(jnp.exp(down), axis=0, keepdims=True))
    scores = INVERSE_TEMP * dot(own_user, items, NT) - log_row
    lse = jnp.log(jnp.sum(jnp.exp(scores), axis=1, keepdims=True))
    positive = jnp.sum(jnp.where(mine, scores, 0.0), axis=1, keepdims=True)
    losses_ref[...] = row_of(lse - positive)
    hot = mine.astype(F32)
    d_user = INVERSE_TEMP * dot((jnp.exp(scores - lse) - hot).astype(BF16), items)
    own_down = INVERSE_TEMP * dot(own_item, users, NT) - own_log
    d_item = INVERSE_TEMP * dot((jnp.exp(own_down - lse_row) - hot).astype(BF16), users)
    common = []
    outputs = []
    for tower, (d_unit, head_ref) in enumerate(((d_user, head0_ref), (d_item, head1_ref))):
        unit = unit_ref[:, tower * OUT : (tower + 1) * OUT]
        scale = scale_ref[:, tower * OUT : (tower + 1) * OUT]
        along = jnp.sum(unit * d_unit, axis=-1, keepdims=True)
        d_output = ((d_unit - unit * along) * scale).astype(BF16)
        pre = pre_ref[:, tower * HID : (tower + 1) * HID]
        gate = 1.0 / (1.0 + jnp.exp(-pre))
        slope = gate * (1.0 + pre * (1.0 - gate))
        common.append((dot(d_output, head_ref[...], NT) * slope).astype(BF16))
        outputs.append(d_output)
    common = jnp.concatenate(common + outputs, axis=1)
    pooled = pooled_ref[...]
    hidden = hidden_ref[...]
    blank = jnp.zeros((OWN, 64), BF16)
    for chip in range(N_CHIP):
        send_ref[chip, :, :COLUMNS_AT] = common
        send_ref[chip, :, COLUMNS_AT:] = jnp.concatenate(
            [
                pooled[:, chip * 64 : chip * 64 + 64],
                pooled[:, IN_WIDTH + chip * 64 : IN_WIDTH + chip * 64 + 64],
                hidden[:, chip * 32 : chip * 32 + 32],
                hidden[:, HID + chip * 32 : HID + chip * 32 + 32],
                blank,
            ],
            axis=1,
        )


def softmax_back(place, group, counts, pooled, pre, hidden, unit, scale, head0, head1):
    return pl.pallas_call(
        softmax_kernel,
        in_specs=[pl.BlockSpec(memory_space=pltpu.SMEM)] + [whole()] * 9,
        out_specs=[whole()] * 2,
        out_shape=[
            jax.ShapeDtypeStruct((1, OWN), F32),
            jax.ShapeDtypeStruct((N_CHIP, OWN, GRAD_WIDTH), BF16),
        ],
        compiler_params=PARAMS,
        name="softmax_back",
    )(place, group, counts, pooled, pre, hidden, unit, scale, head0, head1)


def back_kernel(first, last, *refs):
    if first:
        core_ref, grads_ref, weights_ref, layer0_ref, layer1_ref = refs[:5]
        refs = refs[5:]
    else:
        (core_ref, grads_ref, weights_ref, layer0_ref, layer1_ref, before_ref, layers_before_ref,
         heads_before_ref) = refs[:8]
        refs = refs[8:]
    if last:
        send_ref, total_ref, pooled_ref, layers_ref, heads_ref = refs
    else:
        total_ref, layers_ref, heads_ref, pooled_ref = refs
    step = pl.program_id(0)
    samples = N_CHIP * OWN

    @pl.when(step == 0)
    def _():
        grads = grads_ref[...].reshape(samples, GRAD_WIDTH)
        inputs = grads[:, COLUMNS_AT : COLUMNS_AT + 128]
        hidden = grads[:, COLUMNS_AT + 128 :]
        d_hidden = (grads[:, :HID], grads[:, HID : 2 * HID])
        for f in range(FEATURES):
            tower = f // TOWER_FEATURES
            layer_ref = (layer0_ref, layer1_ref)[tower]
            at = (f % TOWER_FEATURES) * EMB
            pooled_ref[pl.ds(f, samples, stride=FEATURES), :] = dot(
                d_hidden[tower], layer_ref[at : at + EMB, :], NT
            )
        for tower in range(2):
            d_output = grads[:, 2 * HID + tower * OUT : 2 * HID + (tower + 1) * OUT]
            layer_rows = dot(inputs, d_hidden[tower], TN)[tower * 64 : tower * 64 + 64]
            head_rows = dot(hidden, d_output, TN)[tower * 32 : tower * 32 + 32]
            if not first:
                layer_rows = layer_rows + layers_before_ref[tower]
                head_rows = head_rows + heads_before_ref[tower]
            layers_ref[tower] = layer_rows
            heads_ref[tower] = head_rows

    d_pooled = pooled_ref[pl.ds(pl.multiple_of(step * BLOCK, BLOCK), BLOCK), :].astype(BF16)
    term = dot(d_pooled, weights_ref[...], TN)

    @pl.when(step == 0)
    def _():
        total_ref[...] = term if first else before_ref[...] + term

    @pl.when(step > 0)
    def _():
        total_ref[...] += term

    if last:

        @pl.when(step == N_CHIP - 1)
        def _():
            table_rows = jnp.transpose(total_ref[...])
            core = core_ref[0]
            for d in range(N_DP):
                send_ref[d, :64, :] = table_rows[d * 64 : (d + 1) * 64].astype(BF16)
                tower, quarter, half = d // 8, d % 8 // 2, d % 2
                send_ref[d, 64:80, :] = layers_ref[
                    tower,
                    pl.ds(pl.multiple_of(core * 32 + half * 16, 16), 16),
                    quarter * 128 : quarter * 128 + 128,
                ].astype(BF16)
                if d < 2:
                    send_ref[d, 80:, :] = heads_ref[
                        d, pl.ds(pl.multiple_of(core * 16, 16), 16), :
                    ].astype(BF16)
                else:
                    send_ref[d, 80:, :] = jnp.zeros((16, 128), BF16)


def back(core, grads, weights, layer0, layer1, before=None):
    first = last = False
    if before is None:
        first = True
    else:
        last = True

    def fixed(shape):
        return pl.BlockSpec(shape, lambda i: (0,) * len(shape))

    total = jax.ShapeDtypeStruct((EMB, ROWS), F32)
    layers = jax.ShapeDtypeStruct((2, 64, HID), F32)
    heads = jax.ShapeDtypeStruct((2, 32, OUT), F32)
    pooled = pltpu.VMEM((N_CHIP * BLOCK, EMB), F32)
    in_specs = [
        pl.BlockSpec(memory_space=pltpu.SMEM),
        fixed((N_CHIP, OWN, GRAD_WIDTH)),
        pl.BlockSpec((BLOCK, ROWS), lambda i: (i, 0)),
        fixed((IN_WIDTH, HID)),
        fixed((IN_WIDTH, HID)),
    ]
    if last:
        in_specs += [fixed(total.shape), fixed(layers.shape), fixed(heads.shape)]
        out_shape = [jax.ShapeDtypeStruct((N_DP, CHUNK, 128), BF16)]
        scratch = [pltpu.VMEM(total.shape, F32), pooled, pltpu.VMEM(layers.shape, F32), pltpu.VMEM(heads.shape, F32)]
    else:
        out_shape = [total, layers, heads]
        scratch = [pooled]
    return pl.pallas_call(
        lambda *refs: back_kernel(first, last, *refs),
        grid=(N_CHIP,),
        in_specs=in_specs,
        out_specs=[fixed(s.shape) for s in out_shape],
        out_shape=out_shape,
        scratch_shapes=scratch,
        compiler_params=PARAMS,
        cost_estimate=pl.CostEstimate(
            flops=2 * N_CHIP * BLOCK * ROWS * EMB, bytes_accessed=10 * 2**20, transcendentals=0
        ),
        name="back",
    )(core, grads, weights, layer0, layer1, *(before or ()))


def sum_kernel(parts_ref, send_ref):
    total = parts_ref[0].astype(F32)
    for d in range(1, N_DP):
        total = total + parts_ref[d].astype(F32)
    total = total.astype(BF16)
    for d in range(N_DP):
        send_ref[d] = total


def sum_parts(parts):
    return pl.pallas_call(
        sum_kernel,
        in_specs=[whole()],
        out_specs=whole(),
        out_shape=jax.ShapeDtypeStruct(parts.shape, BF16),
        compiler_params=PARAMS,
        name="sum_parts",
    )(parts)


def spread_kernel(sums_ref, table_ref, layer0_ref, head0_ref, layer1_ref, head1_ref):
    for d in range(N_DP):
        table_ref[d * 64 : (d + 1) * 64, :] = sums_ref[d, :64, :].astype(F32)
        tower, quarter, half = d // 8, d % 8 // 2, d % 2
        (layer0_ref, layer1_ref)[tower][
            half * 16 : half * 16 + 16, quarter * 128 : quarter * 128 + 128
        ] = sums_ref[d, 64:80, :].astype(F32)
    head0_ref[...] = sums_ref[0, 80:, :].astype(F32)
    head1_ref[...] = sums_ref[1, 80:, :].astype(F32)


def spread(sums):
    return pl.pallas_call(
        spread_kernel,
        in_specs=[whole()],
        out_specs=[whole()] * 5,
        out_shape=[
            jax.ShapeDtypeStruct((ROWS, EMB), F32),
            jax.ShapeDtypeStruct((32, HID), F32),
            jax.ShapeDtypeStruct((16, OUT), F32),
            jax.ShapeDtypeStruct((32, HID), F32),
            jax.ShapeDtypeStruct((16, OUT), F32),
        ],
        compiler_params=PARAMS,
        name="spread",
    )(sums)


def exchange(values, axes):
    return lax.all_to_all(values, axes, 0, 0, tiled=True)


def to_other_core(values):
    return lax.ppermute(values, "core", [(0, 1), (1, 0)])


def shards(ids, mults, table, user_layer, user_head, item_layer, item_head, counts):
    core = lax.axis_index("core").reshape(1)
    place = lax.axis_index(DP).reshape(1)
    other_weights, other_partial = pool(1 - core, ids[0], mults[0], table)
    arrived = to_other_core(other_partial)
    own_weights, own_partial = pool(core, ids[0], mults[0], table)
    chip_partial = (own_partial.astype(F32) + arrived.astype(F32)).astype(BF16)
    parts = exchange(chip_partial.reshape(N_CHIP, BLOCK, EMB), CHIPS)
    pooled, pre, hidden, unit, scale, units = towers(
        parts, counts, user_layer, user_head, item_layer, item_head
    )
    group = exchange(units, DP)
    losses, grads = softmax_back(
        place, group, counts, pooled, pre, hidden, unit, scale, user_head, item_head
    )
    own_grads = exchange(grads, CHIPS)
    other_grads = to_other_core(own_grads)
    before = back(core, own_grads, own_weights, user_layer, item_layer)
    (terms,) = back(core, other_grads, other_weights, user_layer, item_layer, tuple(before))
    sums = exchange(sum_parts(exchange(terms, DP)), DP)
    table_change, layer0, head0, layer1, head1 = spread(sums)
    return (losses, table_change, layer0, head0, layer1, head1)


def solution(mesh):
    fine = Mesh(mesh.devices.reshape(tuple(AXES.values())), tuple(AXES))
    in_specs = (
        P(TABLE, DP, None),
        P(TABLE, DP, None),
        P(TABLE, None),
        P(),
        P(),
        P(),
        P(),
        P(DP, TABLE),
    )
    out_specs = (P(DP, TABLE),) + (P(TABLE, None),) * 5
    return jax.shard_map(shards, mesh=fine, in_specs=in_specs, out_specs=out_specs, check_vma=False)
```

time: 1200 us -> 200 us (0.17)
  the two profiles are of different devices: /device:TPU:64 before, /device:TPU:8 now
where the time goes in v1:
time: 200 us; the launch traced here: 197 us
  blocking collectives  104 us (52%)
  Pallas kernels  66.2 us (33%)
  starting transfers between devices  13.5 us (7%)
  waiting for transfers between devices  9.94 us (5%)
    all_to_all x4, blocking collectives, exchange(): return lax.all_to_all(values, axes, 0, 0, tiled=True)  104 us
    pallas_call x2, Pallas kernels, back(): pl.pallas_call(lambda *refs: back_kernel(first, last, *refs), grid=(N_CHI...  29.7 us
    pallas_call x2, Pallas kernels, pool(): pl.pallas_call(pool_kernel, grid_spec=pltpu.PrefetchScalarGridSpec(num_sc...  26.6 us
    all_to_all x1, waiting for transfers between devices, exchange(): return lax.all_to_all(values, axes, 0, 0, tiled=True)  9.94 us
    all_to_all x1, starting transfers between devices, exchange(): return lax.all_to_all(values, axes, 0, 0, tiled=True)  9.72 us
  transfers between devices with their start and end apart: 3, of which 1 were waited for; matrix products, arithmetic and copies ran while one was open for 0% of the time, Pallas kernels for 14%

profile of v1, /device:TPU:8, one launch (start us, length us, event | category | flops | bytes accessed | tf_op | source)
XLA Modules:
  0.0 197.0 jit_solution(15232823297853329208)
XLA Ops:
  0.6 13.3 %pool.3 = (bf16[4096,1024]{1,0:T(8,128)(2,1)}, bf16[4096,128]{1,0:T(8,128)(2,1)}) custom-call(s32[1]{0:T(128)S(6)} %sub.3.core_ref, s32[512,128]{1,0:T(8,128)} %bitcast.6, s32[512,128]{1,0:T(8,128)} %bitcast.8, bf16[1024,128]{1,0:T(8,128)(2,1)} %table_ref.3), custom_call_target="tpu_custom_call" | custom-call | flops 2147483648 | bytes 10485760 | tf_op jit(solution)/shard_map/pool/pallas_call | solution.py:76
  13.9 1.9 collective-permute-start
  15.8 13.3 %pool.2 = (bf16[4096,1024]{1,0:T(8,128)(2,1)}, bf16[4096,128]{1,0:T(8,128)(2,1)}) custom-call(s32[1]{0:T(128)} %bitcast.1.core_ref.refs_0_, s32[512,128]{1,0:T(8,128)} %bitcast.7, s32[512,128]{1,0:T(8,128)} %bitcast.9, bf16[1024,128]{1,0:T(8,128)(2,1)} %table_ref.3), custom_call_target="tpu_custom_call" | custom-call | flops 2147483648 | bytes 10485760 | tf_op jit(solution)/shard_map/pool/pallas_call | solution.py:76
  29.1 0.0 collective-permute-done
  29.1 1.5 add_convert_fusion
  30.6 38.6 %all_to_all.25.parts_ref = bf16[16,256,128]{2,1,0:T(8,128)(2,1)} all-to-all(bf16[16,256,128]{2,1,0:T(8,128)(2,1)S(1)} %bitcast.5), channel_id=1, replica_groups=mesh['x_lo'=2,'z'=8,'core'=2,'x_hi'=2,'y'=8] {'x_lo','z'}, dimensions={0} | all-to-all | bytes 2097152 | tf_op jit(solution)/shard_map/all_to_all | solution.py:399
  69.2 3.5 %towers.1 = (bf16[16,2048]{1,0:T(8,128)(2,1)}, f32[16,1024]{1,0:T(8,128)}, bf16[16,1024]{1,0:T(8,128)(2,1)}, f32[16,256]{1,0:T(8,128)}, f32[16,256]{1,0:T(8,128)}, /*index=5*/bf16[16,48,128]{2,1,0:T(8,128)(2,1)}) custom-call(bf16[16,256,128]{2,1,0:T(8,128)(2,1)} %all_to_all.25.parts_ref, s32[1,16]{1,0:T(1,128)} %counts_ref.3, bf16[1024,512]{1,0:T(8,128)(2,1)} %refs_3_.3, ...), custom_call_target="tpu_custom_call" | custom-call | tf_op jit(solution)/shard_map/towers/pallas_call | solution.py:147
  72.7 9.7 %all-to-all-start.1 = ((bf16[16,48,128]{2,1,0:T(8,128)(2,1)}), bf16[16,48,128]{2,1,0:T(8,128)(2,1)S(1)}, u32[]{:S(2)}, u32[]{:S(2)}) async-start(bf16[16,48,128]{2,1,0:T(8,128)(2,1)} %get-tuple-element.28), calls=%async_computation.1 | async-start | bytes 393216 | tf_op jit(solution)/shard_map/all_to_all | solution.py:399
  82.4 9.9 %all-to-all-done.1.group_ref = bf16[16,48,128]{2,1,0:T(8,128)(2,1)S(1)} async-done(((bf16[16,48,128]{2,1,0:T(8,128)(2,1)}), bf16[16,48,128]{2,1,0:T(8,128)(2,1)S(1)}, u32[]{:S(2)}, u32[]{:S(2)}) %all-to-all-start.1) | async-done | bytes 196640 | tf_op jit(solution)/shard_map/all_to_all | solution.py:399
  92.3 0.0 copy-start.2
  92.3 0.7 copy-done.2
  93.0 2.8 %softmax_back.1 = (f32[1,16]{1,0:T(1,128)}, bf16[16,16,1536]{2,1,0:T(8,128)(2,1)}) custom-call(s32[1]{0:T(128)} %bitcast.place_ref, bf16[16,48,128]{2,1,0:T(8,128)(2,1)} %copy-done.2, s32[1,16]{1,0:T(1,128)} %counts_ref.3, bf16[16,2048]{1,0:T(8,128)(2,1)} %get-tuple-element.29.pooled_ref, f32[16,1024]{1,0:T(8,128)} %get-tuple-element.30.pre_ref, ...), custom_call_target="tpu_custom_call" | custom-call | tf_op jit(solution)/shard_map/softmax_back/pallas_call | solution.py:223
  95.8 25.1 %all_to_all.26.refs_1_ = bf16[16,16,1536]{2,1,0:T(8,128)(2,1)S(1)} all-to-all(bf16[16,16,1536]{2,1,0:T(8,128)(2,1)} %get-tuple-element.35), channel_id=1, replica_groups=mesh['x_lo'=2,'z'=8,'core'=2,'x_hi'=2,'y'=8] {'x_lo','z'}, dimensions={0} | all-to-all | bytes 1572864 | tf_op jit(solution)/shard_map/all_to_all | solution.py:399
  121.0 0.0 copy-start
  121.0 1.9 collective-permute-start.1
  122.9 0.0 copy-done
  122.9 14.7 %back.2 = (f32[128,1024]{1,0:T(8,128)}, f32[2,64,512]{2,1,0:T(8,128)}, f32[2,32,128]{2,1,0:T(8,128)}) custom-call(s32[1]{0:T(128)} %bitcast.1.core_ref.refs_0_, bf16[16,16,1536]{2,1,0:T(8,128)(2,1)} %copy-done, bf16[4096,1024]{1,0:T(8,128)(2,1)} %get-tuple-element.37.refs_2_, bf16[1024,512]{1,0:T(8,128)(2,1)} %refs_3_.3, bf16[1024,512]{1,0:T(8,128)(2,1)} %refs_4_.3), custom_call_target="tpu_custom_call" | custom-call | flops 1073741824 | bytes 10485760 | tf_op jit(solution)/shard_map/back/pallas_call | solution.py:335
  137.6 0.0 collective-permute-done.1.refs_1_
  137.6 0.0 copy-start.1
  137.6 0.9 copy-done.1
  138.5 15.0 %back.3 = bf16[16,96,128]{2,1,0:T(8,128)(2,1)} custom-call(s32[1]{0:T(128)} %bitcast.1.core_ref.refs_0_, bf16[16,16,1536]{2,1,0:T(8,128)(2,1)} %copy-done.1, bf16[4096,1024]{1,0:T(8,128)(2,1)} %get-tuple-element.36.refs_2_, bf16[1024,512]{1,0:T(8,128)(2,1)} %refs_3_.3, bf16[1024,512]{1,0:T(8,128)(2,1)} %refs_4_.3, f32[128,1024]{1,0:T(8,128)} %get-tuple-element.38.refs_5_, ...), custom_call_target="tpu_custom_call" | custom-call | flops 1073741824 | bytes 10485760 | tf_op jit(solution)/shard_map/back/pallas_call | solution.py:335
  153.5 20.2 %all_to_all.27.parts_ref = bf16[16,96,128]{2,1,0:T(8,128)(2,1)} all-to-all(bf16[16,96,128]{2,1,0:T(8,128)(2,1)} %back.3), channel_id=1, replica_groups=mesh['x_lo'=2,'z'=8,'core'=2,'x_hi'=2,'y'=8] {'x_hi','y'}, dimensions={0} | all-to-all | bytes 786432 | tf_op jit(solution)/shard_map/all_to_all | solution.py:399
  173.7 1.8 sum_parts.1
  175.5 19.7 %all_to_all.28.sums_ref = bf16[16,96,128]{2,1,0:T(8,128)(2,1)} all-to-all(bf16[16,96,128]{2,1,0:T(8,128)(2,1)} %sum_parts.1), channel_id=1, replica_groups=mesh['x_lo'=2,'z'=8,'core'=2,'x_hi'=2,'y'=8] {'x_hi','y'}, dimensions={0} | all-to-all | bytes 786432 | tf_op jit(solution)/shard_map/all_to_all | solution.py:399
  195.2 1.8 spread.1
Async XLA Ops:
  13.9 15.2 %collective-permute-start = (bf16[4096,128]{1,0:T(8,128)(2,1)}, bf16[4096,128]{1,0:T(8,128)(2,1)S(1)}, u32[]{:S(2)}, u32[]{:S(2)}) collective-permute-start(bf16[4096,128]{1,0:T(8,128)(2,1)} %get-tuple-element.27), channel_id=1, source_target_pairs={{0,16},{16,0},{1,17},{17,1},{2,18},{18,2},{3,19},{19,3},{4,20},{20... | collective-permute-start | bytes 3145736 | tf_op jit(solution)/shard_map/ppermute | solution.py:403
  72.7 19.7 %all-to-all-start.1 = ((bf16[16,48,128]{2,1,0:T(8,128)(2,1)}), bf16[16,48,128]{2,1,0:T(8,128)(2,1)S(1)}, u32[]{:S(2)}, u32[]{:S(2)}) async-start(bf16[16,48,128]{2,1,0:T(8,128)(2,1)} %get-tuple-element.28), calls=%async_computation.1 | async-start | bytes 393216 | tf_op jit(solution)/shard_map/all_to_all | solution.py:399
  92.3 0.7 copy-start.2
  121.0 1.9 copy-start
  121.0 16.6 %collective-permute-start.1 = (bf16[16,16,1536]{2,1,0:T(8,128)(2,1)S(1)}, bf16[16,16,1536]{2,1,0:T(8,128)(2,1)S(1)}, u32[]{:S(2)}, u32[]{:S(2)}) collective-permute-start(bf16[16,16,1536]{2,1,0:T(8,128)(2,1)S(1)} %all_to_all.26.refs_1_), channel_id=1, source_target_pairs={{0,16},{16,0},{1,17},{17,1},{2,18},{18,2},{3,19},{19,3},{4,20},{20... | collective-permute-start | bytes 2359304 | tf_op jit(solution)/shard_map/ppermute | solution.py:403
  137.6 1.0 copy-start.1

commit v2 on v1

--- a/solution.py
+++ b/solution.py
@@ -27,6 +27,8 @@
 IN_WIDTH = TOWER_FEATURES * EMB
 GRAD_WIDTH = 12 * 128
 COLUMNS_AT = 2 * HID + 2 * OUT
+POOL_SAMPLES = 64
+BACK_PARTS = 4
 CHUNK = 96
 
 BF16 = jnp.bfloat16
@@ -45,56 +47,76 @@
     return pl.BlockSpec(memory_space=pltpu.VMEM)
 
 
-def pool_kernel(core_ref, ids_ref, mults_ref, table_ref, weights_ref, partial_ref):
-    ids = ids_ref[...]
+def lookup_weights(ids, mults, weights_ref, first):
     lane = lax.broadcasted_iota(jnp.int32, ids.shape, 1)
     high = lax.shift_right_logical(ids, 7) * FEATURES + lax.shift_right_logical(lane, 3)
     high = high.astype(F32)
-    low = (ids & 127).astype(F32)
-    mults = mults_ref[...].astype(F32)
-    row = lax.broadcasted_iota(jnp.int32, (128, 128), 0).astype(F32)
-    zero = jnp.zeros((128, 128), F32)
-    one = jnp.ones((128, 128), F32)
-    for n in range(OWN):
-        left = jnp.where(high[n : n + 1] == row, mults[n : n + 1], zero).astype(BF16)
-        right = jnp.where(low[n : n + 1] == row, one, zero).astype(BF16)
-        hits = dot(left, right, NT).astype(BF16)
+    low = jnp.transpose((ids & 127).astype(F32))
+    mults = mults.astype(F32)
+    down = lax.broadcasted_iota(jnp.int32, (128, 128), 0).astype(F32).astype(BF16)
+    across = lax.broadcasted_iota(jnp.int32, (128, 128), 1).astype(F32).astype(BF16)
+    zero = jnp.zeros((128, 128), BF16)
+    one = jnp.ones((128, 128), BF16)
+
+    def spread_row(values, n):
+        row = jnp.broadcast_to(values[n : n + 1], (16, 128)).astype(BF16)
+        return jnp.concatenate([row] * 8, axis=0)
+
+    for n in range(ids.shape[0]):
+        left = jnp.where(spread_row(high, n) == down, spread_row(mults, n), zero)
+        spread_low = jnp.broadcast_to(low[:, n : n + 1], (128, 128)).astype(BF16)
+        right = jnp.where(spread_low == across, one, zero)
+        hits = dot(left, right).astype(BF16)
+        at = first + n * FEATURES
         for h in range(8):
-            weights_ref[n * FEATURES : (n + 1) * FEATURES, h * 128 : (h + 1) * 128] = hits[
+            weights_ref[at : at + FEATURES, h * 128 : (h + 1) * 128] = hits[
                 h * FEATURES : (h + 1) * FEATURES
             ]
-    partial_ref[...] = dot(weights_ref[...], table_ref[...]).astype(BF16)
-
-
-def pool(core, ids, mults, table):
-    def picked(i, core_ref):
-        return (2 * i + core_ref[0], 0)
-
-    def at(i, core_ref):
-        return (i, 0)
-
+
+
+def pool_kernel(ids_ref, mults_ref, table_ref, out_ref, partial_ref, weights_ref, sems):
+    parts = N_CHIP * OWN // POOL_SAMPLES
+    rows = POOL_SAMPLES * FEATURES
+
+    def copy(part):
+        at = pl.ds(part * rows, rows)
+        return pltpu.make_async_copy(weights_ref.at[at, :], out_ref.at[at, :], sems.at[part])
+
+    def sum_part(part):
+        at = pl.ds(part * rows, rows)
+        partial_ref[at, :] = dot(weights_ref[at, :], table_ref[...]).astype(BF16)
+
+    for part in range(parts):
+        at = pl.ds(part * POOL_SAMPLES, POOL_SAMPLES)
+        lookup_weights(ids_ref[at, :], mults_ref[at, :], weights_ref, part * rows)
+        copy(part).start()
+        if part > 0:
+            sum_part(part - 1)
+    sum_part(parts - 1)
+    for part in range(parts):
+        copy(part).wait()
+
+
+def pool(ids, mults, table):
+    parts = N_CHIP * OWN // POOL_SAMPLES
     return pl.pallas_call(
         pool_kernel,
-        grid_spec=pltpu.PrefetchScalarGridSpec(
-            num_scalar_prefetch=1,
-            grid=(N_CHIP,),
-            in_specs=[
-                pl.BlockSpec((OWN, 128), picked),
-                pl.BlockSpec((OWN, 128), picked),
-                pl.BlockSpec((ROWS, EMB), lambda i, core_ref: (0, 0)),
-            ],
-            out_specs=[pl.BlockSpec((BLOCK, ROWS), at), pl.BlockSpec((BLOCK, EMB), at)],
-        ),
+        in_specs=[whole()] * 3,
+        out_specs=[pl.BlockSpec(memory_space=pl.ANY), whole()],
         out_shape=[
             jax.ShapeDtypeStruct((N_CHIP * BLOCK, ROWS), BF16),
             jax.ShapeDtypeStruct((N_CHIP * BLOCK, EMB), BF16),
         ],
+        scratch_shapes=[
+            pltpu.VMEM((N_CHIP * BLOCK, ROWS), BF16),
+            pltpu.SemaphoreType.DMA((parts,)),
+        ],
         compiler_params=PARAMS,
         cost_estimate=pl.CostEstimate(
             flops=2 * N_CHIP * BLOCK * ROWS * EMB * 2, bytes_accessed=10 * 2**20, transcendentals=0
         ),
         name="pool",
-    )(core, ids, mults, table)
+    )(ids, mults, table)
 
 
 def column_of(row):
@@ -233,118 +255,98 @@
     )(place, group, counts, pooled, pre, hidden, unit, scale, head0, head1)
 
 
-def back_kernel(first, last, *refs):
+def back_kernel(first, *refs):
+    core_ref, grads_ref, weights_ref, layer0_ref, layer1_ref = refs[:5]
     if first:
-        core_ref, grads_ref, weights_ref, layer0_ref, layer1_ref = refs[:5]
-        refs = refs[5:]
+        total_ref, layers_ref, heads_ref, pooled_ref, here_ref, sems = refs[5:]
     else:
-        (core_ref, grads_ref, weights_ref, layer0_ref, layer1_ref, before_ref, layers_before_ref,
-         heads_before_ref) = refs[:8]
-        refs = refs[8:]
-    if last:
-        send_ref, total_ref, pooled_ref, layers_ref, heads_ref = refs
-    else:
-        total_ref, layers_ref, heads_ref, pooled_ref = refs
-    step = pl.program_id(0)
+        before_ref, layers_before_ref, heads_before_ref = refs[5:8]
+        send_ref, pooled_ref, here_ref, layers_ref, heads_ref, sems = refs[8:]
     samples = N_CHIP * OWN
-
-    @pl.when(step == 0)
-    def _():
-        grads = grads_ref[...].reshape(samples, GRAD_WIDTH)
-        inputs = grads[:, COLUMNS_AT : COLUMNS_AT + 128]
-        hidden = grads[:, COLUMNS_AT + 128 :]
-        d_hidden = (grads[:, :HID], grads[:, HID : 2 * HID])
-        for f in range(FEATURES):
-            tower = f // TOWER_FEATURES
-            layer_ref = (layer0_ref, layer1_ref)[tower]
-            at = (f % TOWER_FEATURES) * EMB
-            pooled_ref[pl.ds(f, samples, stride=FEATURES), :] = dot(
-                d_hidden[tower], layer_ref[at : at + EMB, :], NT
-            )
-        for tower in range(2):
-            d_output = grads[:, 2 * HID + tower * OUT : 2 * HID + (tower + 1) * OUT]
-            layer_rows = dot(inputs, d_hidden[tower], TN)[tower * 64 : tower * 64 + 64]
-            head_rows = dot(hidden, d_output, TN)[tower * 32 : tower * 32 + 32]
-            if not first:
-                layer_rows = layer_rows + layers_before_ref[tower]
-                head_rows = head_rows + heads_before_ref[tower]
-            layers_ref[tower] = layer_rows
-            heads_ref[tower] = head_rows
-
-    d_pooled = pooled_ref[pl.ds(pl.multiple_of(step * BLOCK, BLOCK), BLOCK), :].astype(BF16)
-    term = dot(d_pooled, weights_ref[...], TN)
-
-    @pl.when(step == 0)
-    def _():
-        total_ref[...] = term if first else before_ref[...] + term
-
-    @pl.when(step > 0)
-    def _():
-        total_ref[...] += term
-
-    if last:
-
-        @pl.when(step == N_CHIP - 1)
-        def _():
-            table_rows = jnp.transpose(total_ref[...])
-            core = core_ref[0]
-            for d in range(N_DP):
-                send_ref[d, :64, :] = table_rows[d * 64 : (d + 1) * 64].astype(BF16)
-                tower, quarter, half = d // 8, d % 8 // 2, d % 2
-                send_ref[d, 64:80, :] = layers_ref[
-                    tower,
-                    pl.ds(pl.multiple_of(core * 32 + half * 16, 16), 16),
-                    quarter * 128 : quarter * 128 + 128,
-                ].astype(BF16)
-                if d < 2:
-                    send_ref[d, 80:, :] = heads_ref[
-                        d, pl.ds(pl.multiple_of(core * 16, 16), 16), :
-                    ].astype(BF16)
-                else:
-                    send_ref[d, 80:, :] = jnp.zeros((16, 128), BF16)
+    rows = samples * FEATURES // BACK_PARTS
+
+    def copy(part):
+        at = pl.ds(part * rows, rows)
+        return pltpu.make_async_copy(weights_ref.at[at, :], here_ref.at[at, :], sems.at[part])
+
+    for part in range(BACK_PARTS):
+        copy(part).start()
+    grads = grads_ref[...].reshape(samples, GRAD_WIDTH)
+    inputs = grads[:, COLUMNS_AT : COLUMNS_AT + 128]
+    hidden = grads[:, COLUMNS_AT + 128 :]
+    d_hidden = (grads[:, :HID], grads[:, HID : 2 * HID])
+    for f in range(FEATURES):
+        tower = f // TOWER_FEATURES
+        layer_ref = (layer0_ref, layer1_ref)[tower]
+        at = (f % TOWER_FEATURES) * EMB
+        pooled_ref[pl.ds(f, samples, stride=FEATURES), :] = dot(
+            d_hidden[tower], layer_ref[at : at + EMB, :], NT
+        )
+    for tower in range(2):
+        d_output = grads[:, 2 * HID + tower * OUT : 2 * HID + (tower + 1) * OUT]
+        layer_rows = dot(inputs, d_hidden[tower], TN)[tower * 64 : tower * 64 + 64]
+        head_rows = dot(hidden, d_output, TN)[tower * 32 : tower * 32 + 32]
+        if not first:
+            layer_rows = layer_rows + layers_before_ref[tower]
+            head_rows = head_rows + heads_before_ref[tower]
+        layers_ref[tower] = layer_rows
+        heads_ref[tower] = head_rows
+    total = None if first else before_ref[...]
+    for part in range(BACK_PARTS):
+        copy(part).wait()
+        at = pl.ds(part * rows, rows)
+        term = dot(pooled_ref[at, :].astype(BF16), here_ref[at, :], TN)
+        total = term if total is None else total + term
+    if first:
+        total_ref[...] = total
+        return
+    table_rows = jnp.transpose(total)
+    core = core_ref[0]
+    for d in range(N_DP):
+        send_ref[d, :64, :] = table_rows[d * 64 : (d + 1) * 64].astype(BF16)
+        tower, quarter, half = d // 8, d % 8 // 2, d % 2
+        send_ref[d, 64:80, :] = layers_ref[
+            tower,
+            pl.ds(pl.multiple_of(core * 32 + half * 16, 16), 16),
+            quarter * 128 : quarter * 128 + 128,
+        ].astype(BF16)
+        if d < 2:
+            send_ref[d, 80:, :] = heads_ref[d, pl.ds(pl.multiple_of(core * 16, 16), 16), :].astype(BF16)
+        else:
+            send_ref[d, 80:, :] = jnp.zeros((16, 128), BF16)
 
 
 def back(core, grads, weights, layer0, layer1, before=None):
-    first = last = False
-    if before is None:
-        first = True
-    else:
-        last = True
-
-    def fixed(shape):
-        return pl.BlockSpec(shape, lambda i: (0,) * len(shape))
-
+    first = before is None
     total = jax.ShapeDtypeStruct((EMB, ROWS), F32)
     layers = jax.ShapeDtypeStruct((2, 64, HID), F32)
     heads = jax.ShapeDtypeStruct((2, 32, OUT), F32)
-    pooled = pltpu.VMEM((N_CHIP * BLOCK, EMB), F32)
-    in_specs = [
-        pl.BlockSpec(memory_space=pltpu.SMEM),
-        fixed((N_CHIP, OWN, GRAD_WIDTH)),
-        pl.BlockSpec((BLOCK, ROWS), lambda i: (i, 0)),
-        fixed((IN_WIDTH, HID)),
-        fixed((IN_WIDTH, HID)),
-    ]
-    if last:
-        in_specs += [fixed(total.shape), fixed(layers.shape), fixed(heads.shape)]
+    scratch = [pltpu.VMEM((N_CHIP * BLOCK, EMB), F32), pltpu.VMEM((N_CHIP * BLOCK, ROWS), BF16)]
+    if first:
+        out_shape = [total, layers, heads]
+    else:
         out_shape = [jax.ShapeDtypeStruct((N_DP, CHUNK, 128), BF16)]
-        scratch = [pltpu.VMEM(total.shape, F32), pooled, pltpu.VMEM(layers.shape, F32), pltpu.VMEM(heads.shape, F32)]
-    else:
-        out_shape = [total, layers, heads]
-        scratch = [pooled]
-    return pl.pallas_call(
-        lambda *refs: back_kernel(first, last, *refs),
-        grid=(N_CHIP,),
-        in_specs=in_specs,
-        out_specs=[fixed(s.shape) for s in out_shape],
+        scratch += [pltpu.VMEM(layers.shape, F32), pltpu.VMEM(heads.shape, F32)]
+    before = before or ()
+    return pl.pallas_call(
+        lambda *refs: back_kernel(first, *refs),
+        in_specs=[
+            pl.BlockSpec(memory_space=pltpu.SMEM),
+            whole(),
+            pl.BlockSpec(memory_space=pl.ANY),
+            whole(),
+            whole(),
+        ]
+        + [whole()] * len(before),
+        out_specs=[whole()] * len(out_shape),
         out_shape=out_shape,
-        scratch_shapes=scratch,
+        scratch_shapes=scratch + [pltpu.SemaphoreType.DMA((BACK_PARTS,))],
         compiler_params=PARAMS,
         cost_estimate=pl.CostEstimate(
             flops=2 * N_CHIP * BLOCK * ROWS * EMB, bytes_accessed=10 * 2**20, transcendentals=0
         ),
         name="back",
-    )(core, grads, weights, layer0, layer1, *(before or ()))
+    )(core, grads, weights, layer0, layer1, *before)
 
 
 def sum_kernel(parts_ref, send_ref):
@@ -406,9 +408,15 @@
 def shards(ids, mults, table, user_layer, user_head, item_layer, item_head, counts):
     core = lax.axis_index("core").reshape(1)
     place = lax.axis_index(DP).reshape(1)
-    other_weights, other_partial = pool(1 - core, ids[0], mults[0], table)
+    ids = ids[0].reshape(N_CHIP, 2, OWN, 128)
+    mults = mults[0].reshape(N_CHIP, 2, OWN, 128)
+
+    def of_core(values, which):
+        return lax.dynamic_index_in_dim(values, which, 1, False).reshape(N_CHIP * OWN, 128)
+
+    other_weights, other_partial = pool(of_core(ids, 1 - core[0]), of_core(mults, 1 - core[0]), table)
     arrived = to_other_core(other_partial)
-    own_weights, own_partial = pool(core, ids[0], mults[0], table)
+    own_weights, own_partial = pool(of_core(ids, core[0]), of_core(mults, core[0]), table)
     chip_partial = (own_partial.astype(F32) + arrived.astype(F32)).astype(BF16)
     parts = exchange(chip_partial.reshape(N_CHIP, BLOCK, EMB), CHIPS)
     pooled, pre, hidden, unit, scale, units = towers(

time: 200 us -> 172 us (0.86)
  Pallas kernels: 66.2 us -> 38.2 us
    pallas_call x4, Pallas kernels: 56.2 us -> 28.2 us  [the longest x2 14.9 us: pool(): pl.pallas_call(pool_kernel, in_specs=[whole()] * 3, out_specs=[pl.BlockSp...]
  transfers between devices with their start and end apart: 3 -> 3, of which waited for: 1 -> 1; matrix products, arithmetic and copies ran while one was open for 0% -> 0% of each run, Pallas kernels for 14% -> 8%
where the time goes in v2:
time: 172 us; the launch traced here: 171 us
  blocking collectives  104 us (60%)
  Pallas kernels  38.2 us (22%)
  starting transfers between devices  13.6 us (8%)
  waiting for transfers between devices  9.94 us (6%)
  local copies, waits for them, and re-layouts  3.52 us (2%)
    all_to_all x4, blocking collectives, exchange(): return lax.all_to_all(values, axes, 0, 0, tiled=True)  104 us
    pallas_call x2, Pallas kernels, pool(): pl.pallas_call(pool_kernel, in_specs=[whole()] * 3, out_specs=[pl.BlockSp...  14.9 us
    pallas_call x2, Pallas kernels, back(): pl.pallas_call(lambda *refs: back_kernel(first, *refs), in_specs=[pl.Bloc...  13.3 us
    all_to_all x1, waiting for transfers between devices, exchange(): return lax.all_to_all(values, axes, 0, 0, tiled=True)  9.94 us
    all_to_all x1, starting transfers between devices, exchange(): return lax.all_to_all(values, axes, 0, 0, tiled=True)  9.74 us
    ppermute x2, starting transfers between devices, to_other_core(): return lax.ppermute(values, 'core', [(0, 1), (1, 0)])  3.83 us
    pallas_call x1, Pallas kernels, towers(): pl.pallas_call(tower_kernel, in_specs=[whole()] * 6, out_specs=[whole()]...  3.47 us
  transfers between devices with their start and end apart: 3, of which 1 were waited for; matrix products, arithmetic and copies ran while one was open for 0% of the time, Pallas kernels for 8%

profile of v2, /device:TPU:8, one launch (start us, length us, event | category | flops | bytes accessed | tf_op | source)
XLA Modules:
  0.0 171.0 jit_solution(6279823688629596503)
XLA Ops:
  0.6 1.9 %constant_dynamic-slice_fusion.2 = (s32[16,1,16,128]{3,2,1,0:T(8,128)}, s32[16,1,16,128]{3,2,1,0:T(8,128)}, s32[16,1,16,128]{3,2,1,0:T(8,128)}, s32[16,1,16,128]{3,2,1,0:T(8,128)}) fusion(s32[16,2,16,128]{3,2,1,0:T(8,128)} %bitcast.18, s32[]{:T(128)S(6)} %select_n.9, s32[]{:T(128)S(6)} %select_n.10, s32[16,2,16,128]{3,2,1,0:T(8,128)} %bitcast.19), kind=kLoop, calls=%fused_computation.3 | loop fusion | bytes 1048584 | tf_op jit(solution)/shard_map/jit(dynamic_index_in_dim)/dynamic_slice | solution.py:415
  2.5 7.4 %pool.3 = (bf16[4096,1024]{1,0:T(8,128)(2,1)}, bf16[4096,128]{1,0:T(8,128)(2,1)}) custom-call(s32[256,128]{1,0:T(8,128)} %bitcast.23, s32[256,128]{1,0:T(8,128)} %bitcast.22, bf16[1024,128]{1,0:T(8,128)(2,1)} %table_ref.3), custom_call_target="tpu_custom_call" | custom-call | flops 2147483648 | bytes 10485760 | tf_op jit(solution)/shard_map/pool/pallas_call | solution.py:102
  10.0 1.9 %collective-permute-start = (bf16[4096,128]{1,0:T(8,128)(2,1)}, bf16[4096,128]{1,0:T(8,128)(2,1)S(1)}, u32[]{:S(2)}, u32[]{:S(2)}) collective-permute-start(bf16[4096,128]{1,0:T(8,128)(2,1)} %get-tuple-element.27), channel_id=1, source_target_pairs={{0,16},{16,0},{1,17},{17,1},{2,18},{18,2},{3,19},{19,3},{4,20},{20... | collective-permute-start | bytes 3145736 | tf_op jit(solution)/shard_map/ppermute | solution.py:405
  11.9 7.4 %pool.2 = (bf16[4096,1024]{1,0:T(8,128)(2,1)}, bf16[4096,128]{1,0:T(8,128)(2,1)}) custom-call(s32[256,128]{1,0:T(8,128)} %bitcast.21, s32[256,128]{1,0:T(8,128)} %bitcast.20, bf16[1024,128]{1,0:T(8,128)(2,1)} %table_ref.3), custom_call_target="tpu_custom_call" | custom-call | flops 2147483648 | bytes 10485760 | tf_op jit(solution)/shard_map/pool/pallas_call | solution.py:102
  19.3 0.0 collective-permute-done
  19.4 1.5 add_convert_fusion
  20.9 38.6 %all_to_all.25.parts_ref = bf16[16,256,128]{2,1,0:T(8,128)(2,1)} all-to-all(bf16[16,256,128]{2,1,0:T(8,128)(2,1)S(1)} %bitcast.17), channel_id=1, replica_groups=mesh['x_lo'=2,'z'=8,'core'=2,'x_hi'=2,'y'=8] {'x_lo','z'}, dimensions={0} | all-to-all | bytes 2097152 | tf_op jit(solution)/shard_map/all_to_all | solution.py:401
  59.4 3.5 %towers.1 = (bf16[16,2048]{1,0:T(8,128)(2,1)}, f32[16,1024]{1,0:T(8,128)}, bf16[16,1024]{1,0:T(8,128)(2,1)}, f32[16,256]{1,0:T(8,128)}, f32[16,256]{1,0:T(8,128)}, /*index=5*/bf16[16,48,128]{2,1,0:T(8,128)(2,1)}) custom-call(bf16[16,256,128]{2,1,0:T(8,128)(2,1)} %all_to_all.25.parts_ref, s32[1,16]{1,0:T(1,128)} %counts_ref.3, bf16[1024,512]{1,0:T(8,128)(2,1)} %refs_3_.3, ...), custom_call_target="tpu_custom_call" | custom-call | tf_op jit(solution)/shard_map/towers/pallas_call | solution.py:169
  62.9 9.7 %all-to-all-start.1 = ((bf16[16,48,128]{2,1,0:T(8,128)(2,1)}), bf16[16,48,128]{2,1,0:T(8,128)(2,1)S(1)}, u32[]{:S(2)}, u32[]{:S(2)}) async-start(bf16[16,48,128]{2,1,0:T(8,128)(2,1)} %get-tuple-element.28), calls=%async_computation.1 | async-start | bytes 393216 | tf_op jit(solution)/shard_map/all_to_all | solution.py:401
  72.6 9.9 %all-to-all-done.1.group_ref = bf16[16,48,128]{2,1,0:T(8,128)(2,1)S(1)} async-done(((bf16[16,48,128]{2,1,0:T(8,128)(2,1)}), bf16[16,48,128]{2,1,0:T(8,128)(2,1)S(1)}, u32[]{:S(2)}, u32[]{:S(2)}) %all-to-all-start.1) | async-done | bytes 196640 | tf_op jit(solution)/shard_map/all_to_all | solution.py:401
  82.6 0.0 copy-start.2
  82.6 0.7 copy-done.2
  83.2 2.8 %softmax_back.1 = (f32[1,16]{1,0:T(1,128)}, bf16[16,16,1536]{2,1,0:T(8,128)(2,1)}) custom-call(s32[1]{0:T(128)} %bitcast.place_ref, bf16[16,48,128]{2,1,0:T(8,128)(2,1)} %copy-done.2, s32[1,16]{1,0:T(1,128)} %counts_ref.3, bf16[16,2048]{1,0:T(8,128)(2,1)} %get-tuple-element.29.pooled_ref, f32[16,1024]{1,0:T(8,128)} %get-tuple-element.30.pre_ref, ...), custom_call_target="tpu_custom_call" | custom-call | tf_op jit(solution)/shard_map/softmax_back/pallas_call | solution.py:245
  86.1 25.1 %all_to_all.26.refs_1_ = bf16[16,16,1536]{2,1,0:T(8,128)(2,1)S(1)} all-to-all(bf16[16,16,1536]{2,1,0:T(8,128)(2,1)} %get-tuple-element.35), channel_id=1, replica_groups=mesh['x_lo'=2,'z'=8,'core'=2,'x_hi'=2,'y'=8] {'x_lo','z'}, dimensions={0} | all-to-all | bytes 1572864 | tf_op jit(solution)/shard_map/all_to_all | solution.py:401
  111.2 0.0 copy-start
  111.2 1.9 %collective-permute-start.1 = (bf16[16,16,1536]{2,1,0:T(8,128)(2,1)S(1)}, bf16[16,16,1536]{2,1,0:T(8,128)(2,1)S(1)}, u32[]{:S(2)}, u32[]{:S(2)}) collective-permute-start(bf16[16,16,1536]{2,1,0:T(8,128)(2,1)S(1)} %all_to_all.26.refs_1_), channel_id=1, source_target_pairs={{0,16},{16,0},{1,17},{17,1},{2,18},{18,2},{3,19},{19,3},{4,20},{20... | collective-permute-start | bytes 2359304 | tf_op jit(solution)/shard_map/ppermute | solution.py:405
  113.1 0.0 copy-done
  113.1 6.6 %back.2 = (f32[128,1024]{1,0:T(8,128)}, f32[2,64,512]{2,1,0:T(8,128)}, f32[2,32,128]{2,1,0:T(8,128)}) custom-call(s32[1]{0:T(128)} %bitcast.8.refs_0_, bf16[16,16,1536]{2,1,0:T(8,128)(2,1)} %copy-done, bf16[4096,1024]{1,0:T(8,128)(2,1)} %get-tuple-element.37.refs_2_, bf16[1024,512]{1,0:T(8,128)(2,1)} %refs_3_.3, bf16[1024,512]{1,0:T(8,128)(2,1)} %refs_4_.3), custom_call_target="tpu_custom_call" | custom-call | flops 1073741824 | bytes 10485760 | tf_op jit(solution)/shard_map/back/pallas_call | solution.py:331
  119.7 0.0 collective-permute-done.1.refs_1_
  119.7 0.0 copy-start.1
  119.7 1.0 copy-done.1
  120.7 6.8 %back.3 = bf16[16,96,128]{2,1,0:T(8,128)(2,1)} custom-call(s32[1]{0:T(128)} %bitcast.8.refs_0_, bf16[16,16,1536]{2,1,0:T(8,128)(2,1)} %copy-done.1, bf16[4096,1024]{1,0:T(8,128)(2,1)} %get-tuple-element.36.refs_2_, bf16[1024,512]{1,0:T(8,128)(2,1)} %refs_3_.3, bf16[1024,512]{1,0:T(8,128)(2,1)} %refs_4_.3, f32[128,1024]{1,0:T(8,128)} %get-tuple-element.38.refs_5_, ...), custom_call_target="tpu_custom_call" | custom-call | flops 1073741824 | bytes 10485760 | tf_op jit(solution)/shard_map/back/pallas_call | solution.py:331
  127.5 20.2 %all_to_all.27.parts_ref = bf16[16,96,128]{2,1,0:T(8,128)(2,1)} all-to-all(bf16[16,96,128]{2,1,0:T(8,128)(2,1)} %back.3), channel_id=1, replica_groups=mesh['x_lo'=2,'z'=8,'core'=2,'x_hi'=2,'y'=8] {'x_hi','y'}, dimensions={0} | all-to-all | bytes 786432 | tf_op jit(solution)/shard_map/all_to_all | solution.py:401
  147.7 1.8 %sum_parts.1 = bf16[16,96,128]{2,1,0:T(8,128)(2,1)} custom-call(bf16[16,96,128]{2,1,0:T(8,128)(2,1)} %all_to_all.27.parts_ref), custom_call_target="tpu_custom_call" | custom-call | tf_op jit(solution)/shard_map/sum_parts/pallas_call | solution.py:362
  149.5 19.7 %all_to_all.28.sums_ref = bf16[16,96,128]{2,1,0:T(8,128)(2,1)} all-to-all(bf16[16,96,128]{2,1,0:T(8,128)(2,1)} %sum_parts.1), channel_id=1, replica_groups=mesh['x_lo'=2,'z'=8,'core'=2,'x_hi'=2,'y'=8] {'x_hi','y'}, dimensions={0} | all-to-all | bytes 786432 | tf_op jit(solution)/shard_map/all_to_all | solution.py:401
  169.2 1.8 %spread.1 = (f32[1024,128]{1,0:T(8,128)}, f32[32,512]{1,0:T(8,128)}, f32[16,128]{1,0:T(8,128)}, f32[32,512]{1,0:T(8,128)}, f32[16,128]{1,0:T(8,128)}) custom-call(bf16[16,96,128]{2,1,0:T(8,128)(2,1)} %all_to_all.28.sums_ref), custom_call_target="tpu_custom_call" | custom-call | tf_op jit(solution)/shard_map/spread/pallas_call | solution.py:384
Async XLA Ops:
  10.0 9.4 %collective-permute-start = (bf16[4096,128]{1,0:T(8,128)(2,1)}, bf16[4096,128]{1,0:T(8,128)(2,1)S(1)}, u32[]{:S(2)}, u32[]{:S(2)}) collective-permute-start(bf16[4096,128]{1,0:T(8,128)(2,1)} %get-tuple-element.27), channel_id=1, source_target_pairs={{0,16},{16,0},{1,17},{17,1},{2,18},{18,2},{3,19},{19,3},{4,20},{20... | collective-permute-start | bytes 3145736 | tf_op jit(solution)/shard_map/ppermute | solution.py:405
  62.9 19.7 %all-to-all-start.1 = ((bf16[16,48,128]{2,1,0:T(8,128)(2,1)}), bf16[16,48,128]{2,1,0:T(8,128)(2,1)S(1)}, u32[]{:S(2)}, u32[]{:S(2)}) async-start(bf16[16,48,128]{2,1,0:T(8,128)(2,1)} %get-tuple-element.28), calls=%async_computation.1 | async-start | bytes 393216 | tf_op jit(solution)/shard_map/all_to_all | solution.py:401
  82.6 0.7 copy-start.2
  111.2 1.9 %copy-start = (bf16[16,16,1536]{2,1,0:T(8,128)(2,1)}, bf16[16,16,1536]{2,1,0:T(8,128)(2,1)S(1)}, u32[]{:S(2)}) copy-start(bf16[16,16,1536]{2,1,0:T(8,128)(2,1)S(1)} %all_to_all.26.refs_1_) | copy-start | bytes 2359300
  111.2 8.5 %collective-permute-start.1 = (bf16[16,16,1536]{2,1,0:T(8,128)(2,1)S(1)}, bf16[16,16,1536]{2,1,0:T(8,128)(2,1)S(1)}, u32[]{:S(2)}, u32[]{:S(2)}) collective-permute-start(bf16[16,16,1536]{2,1,0:T(8,128)(2,1)S(1)} %all_to_all.26.refs_1_), channel_id=1, source_target_pairs={{0,16},{16,0},{1,17},{17,1},{2,18},{18,2},{3,19},{19,3},{4,20},{20... | collective-permute-start | bytes 2359304 | tf_op jit(solution)/shard_map/ppermute | solution.py:405
  119.7 1.0 copy-start.1

commit v3 on v2

--- a/solution.py
+++ b/solution.py
@@ -29,11 +29,10 @@
 COLUMNS_AT = 2 * HID + 2 * OUT
 POOL_SAMPLES = 64
 BACK_PARTS = 4
-CHUNK = 96
+CHUNK = 88
 
 BF16 = jnp.bfloat16
 F32 = jnp.float32
-PARAMS = pltpu.CompilerParams(vmem_limit_bytes=56 * 1024 * 1024)
 
 NT = (((1,), (1,)), ((), ()))
 TN = (((0,), (0,)), ((), ()))
@@ -41,6 +40,10 @@
 
 def dot(left, right, dims=(((1,), (0,)), ((), ()))):
     return lax.dot_general(left, right, dims, preferred_element_type=F32)
+
+
+def room(mib):
+    return pltpu.CompilerParams(vmem_limit_bytes=mib * 2**20)
 
 
 def whole():
@@ -74,49 +77,40 @@
             ]
 
 
-def pool_kernel(ids_ref, mults_ref, table_ref, out_ref, partial_ref, weights_ref, sems):
+def pool_kernel(other, place_ref, lookups_ref, table_ref, weights_ref, partial_ref):
+    core = place_ref[0] ^ other
     parts = N_CHIP * OWN // POOL_SAMPLES
     rows = POOL_SAMPLES * FEATURES
-
-    def copy(part):
-        at = pl.ds(part * rows, rows)
-        return pltpu.make_async_copy(weights_ref.at[at, :], out_ref.at[at, :], sems.at[part])
 
     def sum_part(part):
         at = pl.ds(part * rows, rows)
         partial_ref[at, :] = dot(weights_ref[at, :], table_ref[...]).astype(BF16)
 
     for part in range(parts):
-        at = pl.ds(part * POOL_SAMPLES, POOL_SAMPLES)
-        lookup_weights(ids_ref[at, :], mults_ref[at, :], weights_ref, part * rows)
-        copy(part).start()
+        chips = range(part * POOL_SAMPLES // OWN, (part + 1) * POOL_SAMPLES // OWN)
+        starts = [pl.multiple_of((2 * chip + core) * OWN, OWN) for chip in chips]
+        lookups = jnp.concatenate([lookups_ref[pl.ds(start, OWN), :] for start in starts], axis=0)
+        lookup_weights(lookups & 1023, lax.shift_right_logical(lookups, 10), weights_ref, part * rows)
         if part > 0:
             sum_part(part - 1)
     sum_part(parts - 1)
-    for part in range(parts):
-        copy(part).wait()
-
-
-def pool(ids, mults, table):
-    parts = N_CHIP * OWN // POOL_SAMPLES
-    return pl.pallas_call(
-        pool_kernel,
-        in_specs=[whole()] * 3,
-        out_specs=[pl.BlockSpec(memory_space=pl.ANY), whole()],
+
+
+def pool(other, place, lookups, table):
+    return pl.pallas_call(
+        lambda *refs: pool_kernel(other, *refs),
+        in_specs=[pl.BlockSpec(memory_space=pltpu.SMEM)] + [whole()] * 2,
+        out_specs=[whole()] * 2,
         out_shape=[
             jax.ShapeDtypeStruct((N_CHIP * BLOCK, ROWS), BF16),
             jax.ShapeDtypeStruct((N_CHIP * BLOCK, EMB), BF16),
         ],
-        scratch_shapes=[
-            pltpu.VMEM((N_CHIP * BLOCK, ROWS), BF16),
-            pltpu.SemaphoreType.DMA((parts,)),
-        ],
-        compiler_params=PARAMS,
+        compiler_params=room(8),
         cost_estimate=pl.CostEstimate(
             flops=2 * N_CHIP * BLOCK * ROWS * EMB * 2, bytes_accessed=10 * 2**20, transcendentals=0
         ),
         name="pool",
-    )(ids, mults, table)
+    )(place, lookups, table)
 
 
 def column_of(row):
@@ -179,7 +173,7 @@
             jax.ShapeDtypeStruct((N_DP, 3 * OWN, 128), BF16),
         ],
         scratch_shapes=[pltpu.VMEM((BLOCK, EMB), F32)],
-        compiler_params=PARAMS,
+        compiler_params=room(8),
         name="towers",
     )(parts, counts, layer0, head0, layer1, head1)
 
@@ -197,7 +191,7 @@
     own_log = jnp.log(column_of(counts_ref[...].astype(F32)))
     own_user = unit_ref[:, :OUT].astype(BF16)
     own_item = unit_ref[:, OUT:].astype(BF16)
-    first = place_ref[0] * OWN
+    first = place_ref[1] * OWN
     mine = lax.broadcasted_iota(jnp.int32, (OWN, size), 1) == (
         lax.broadcasted_iota(jnp.int32, (OWN, size), 0) + first
     )
@@ -250,27 +244,20 @@
             jax.ShapeDtypeStruct((1, OWN), F32),
             jax.ShapeDtypeStruct((N_CHIP, OWN, GRAD_WIDTH), BF16),
         ],
-        compiler_params=PARAMS,
+        compiler_params=room(6),
         name="softmax_back",
     )(place, group, counts, pooled, pre, hidden, unit, scale, head0, head1)
 
 
 def back_kernel(first, *refs):
-    core_ref, grads_ref, weights_ref, layer0_ref, layer1_ref = refs[:5]
+    place_ref, grads_ref, weights_ref, layer0_ref, layer1_ref = refs[:5]
     if first:
-        total_ref, layers_ref, heads_ref, pooled_ref, here_ref, sems = refs[5:]
+        total_ref, layers_ref, heads_ref, pooled_ref = refs[5:]
     else:
         before_ref, layers_before_ref, heads_before_ref = refs[5:8]
-        send_ref, pooled_ref, here_ref, layers_ref, heads_ref, sems = refs[8:]
+        send_ref, pooled_ref, layers_ref, heads_ref = refs[8:]
     samples = N_CHIP * OWN
     rows = samples * FEATURES // BACK_PARTS
-
-    def copy(part):
-        at = pl.ds(part * rows, rows)
-        return pltpu.make_async_copy(weights_ref.at[at, :], here_ref.at[at, :], sems.at[part])
-
-    for part in range(BACK_PARTS):
-        copy(part).start()
     grads = grads_ref[...].reshape(samples, GRAD_WIDTH)
     inputs = grads[:, COLUMNS_AT : COLUMNS_AT + 128]
     hidden = grads[:, COLUMNS_AT + 128 :]
@@ -293,15 +280,14 @@
         heads_ref[tower] = head_rows
     total = None if first else before_ref[...]
     for part in range(BACK_PARTS):
-        copy(part).wait()
         at = pl.ds(part * rows, rows)
-        term = dot(pooled_ref[at, :].astype(BF16), here_ref[at, :], TN)
+        term = dot(pooled_ref[at, :].astype(BF16), weights_ref[at, :], TN)
         total = term if total is None else total + term
     if first:
         total_ref[...] = total
         return
     table_rows = jnp.transpose(total)
-    core = core_ref[0]
+    core = place_ref[0]
     for d in range(N_DP):
         send_ref[d, :64, :] = table_rows[d * 64 : (d + 1) * 64].astype(BF16)
         tower, quarter, half = d // 8, d % 8 // 2, d % 2
@@ -310,18 +296,19 @@
             pl.ds(pl.multiple_of(core * 32 + half * 16, 16), 16),
             quarter * 128 : quarter * 128 + 128,
         ].astype(BF16)
-        if d < 2:
-            send_ref[d, 80:, :] = heads_ref[d, pl.ds(pl.multiple_of(core * 16, 16), 16), :].astype(BF16)
+        if d < 4:
+            at = pl.multiple_of(core * 16 + d % 2 * 8, 8)
+            send_ref[d, 80:, :] = heads_ref[d // 2, pl.ds(at, 8), :].astype(BF16)
         else:
-            send_ref[d, 80:, :] = jnp.zeros((16, 128), BF16)
-
-
-def back(core, grads, weights, layer0, layer1, before=None):
+            send_ref[d, 80:, :] = jnp.zeros((8, 128), BF16)
+
+
+def back(place, grads, weights, layer0, layer1, before=None):
     first = before is None
     total = jax.ShapeDtypeStruct((EMB, ROWS), F32)
     layers = jax.ShapeDtypeStruct((2, 64, HID), F32)
     heads = jax.ShapeDtypeStruct((2, 32, OUT), F32)
-    scratch = [pltpu.VMEM((N_CHIP * BLOCK, EMB), F32), pltpu.VMEM((N_CHIP * BLOCK, ROWS), BF16)]
+    scratch = [pltpu.VMEM((N_CHIP * BLOCK, EMB), F32)]
     if first:
         out_shape = [total, layers, heads]
     else:
@@ -332,21 +319,17 @@
         lambda *refs: back_kernel(first, *refs),
         in_specs=[
             pl.BlockSpec(memory_space=pltpu.SMEM),
-            whole(),
-            pl.BlockSpec(memory_space=pl.ANY),
-            whole(),
-            whole(),
         ]
-        + [whole()] * len(before),
+        + [whole()] * (4 + len(before)),
         out_specs=[whole()] * len(out_shape),
         out_shape=out_shape,
-        scratch_shapes=scratch + [pltpu.SemaphoreType.DMA((BACK_PARTS,))],
-        compiler_params=PARAMS,
+        scratch_shapes=scratch,
+        compiler_params=room(12),
         cost_estimate=pl.CostEstimate(
             flops=2 * N_CHIP * BLOCK * ROWS * EMB, bytes_accessed=10 * 2**20, transcendentals=0
         ),
         name="back",
-    )(core, grads, weights, layer0, layer1, *before)
+    )(place, grads, weights, layer0, layer1, *before)
 
 
 def sum_kernel(parts_ref, send_ref):
@@ -364,7 +347,7 @@
         in_specs=[whole()],
         out_specs=whole(),
         out_shape=jax.ShapeDtypeStruct(parts.shape, BF16),
-        compiler_params=PARAMS,
+        compiler_params=room(2),
         name="sum_parts",
     )(parts)
 
@@ -376,8 +359,8 @@
         (layer0_ref, layer1_ref)[tower][
             half * 16 : half * 16 + 16, quarter * 128 : quarter * 128 + 128
         ] = sums_ref[d, 64:80, :].astype(F32)
-    head0_ref[...] = sums_ref[0, 80:, :].astype(F32)
-    head1_ref[...] = sums_ref[1, 80:, :].astype(F32)
+    for d in range(4):
+        (head0_ref, head1_ref)[d // 2][d % 2 * 8 : d % 2 * 8 + 8, :] = sums_ref[d, 80:, :].astype(F32)
 
 
 def spread(sums):
@@ -392,7 +375,7 @@
             jax.ShapeDtypeStruct((32, HID), F32),
             jax.ShapeDtypeStruct((16, OUT), F32),
         ],
-        compiler_params=PARAMS,
+        compiler_params=room(4),
         name="spread",
     )(sums)
 
@@ -406,17 +389,11 @@
 
 
 def shards(ids, mults, table, user_layer, user_head, item_layer, item_head, counts):
-    core = lax.axis_index("core").reshape(1)
-    place = lax.axis_index(DP).reshape(1)
-    ids = ids[0].reshape(N_CHIP, 2, OWN, 128)
-    mults = mults[0].reshape(N_CHIP, 2, OWN, 128)
-
-    def of_core(values, which):
-        return lax.dynamic_index_in_dim(values, which, 1, False).reshape(N_CHIP * OWN, 128)
-
-    other_weights, other_partial = pool(of_core(ids, 1 - core[0]), of_core(mults, 1 - core[0]), table)
+    place = jnp.stack([lax.axis_index("core"), lax.axis_index(DP)])
+    lookups = ids[0] + 1024 * mults[0]
+    other_weights, other_partial = pool(1, place, lookups, table)
     arrived = to_other_core(other_partial)
-    own_weights, own_partial = pool(of_core(ids, core[0]), of_core(mults, core[0]), table)
+    own_weights, own_partial = pool(0, place, lookups, table)
     chip_partial = (own_partial.astype(F32) + arrived.astype(F32)).astype(BF16)
     parts = exchange(chip_partial.reshape(N_CHIP, BLOCK, EMB), CHIPS)
     pooled, pre, hidden, unit, scale, units = towers(
@@ -428,8 +405,8 @@
     )
     own_grads = exchange(grads, CHIPS)
     other_grads = to_other_core(own_grads)
-    before = back(core, own_grads, own_weights, user_layer, item_layer)
-    (terms,) = back(core, other_grads, other_weights, user_layer, item_layer, tuple(before))
+    before = back(place, own_grads, own_weights, user_layer, item_layer)
+    (terms,) = back(place, other_grads, other_weights, user_layer, item_layer, tuple(before))
     sums = exchange(sum_parts(exchange(terms, DP)), DP)
     table_change, layer0, head0, layer1, head1 = spread(sums)
     return (losses, table_change, layer0, head0, layer1, head1)

time: 172 us -> 150 us (0.87)
  Pallas kernels: 38.2 us -> 21.2 us
  blocking collectives: 104 us -> 121 us
  waiting for transfers between devices: 9.94 us -> 0.01 us
  starting transfers between devices: 13.6 us -> 3.83 us
  local copies, waits for them, and re-layouts: 3.52 us -> 0.98 us
    all_to_all x4 -> x5, blocking collectives: 104 us -> 121 us  [exchange(): return lax.all_to_all(values, axes, 0, 0, tiled=True)]
    all_to_all x1 -> x0, waiting for transfers between devices: 9.94 us -> none  [exchange(): return lax.all_to_all(values, axes, 0, 0, tiled=True)]
    all_to_all x1 -> x0, starting transfers between devices: 9.74 us -> none  [exchange(): return lax.all_to_all(values, axes, 0, 0, tiled=True)]
    pallas_call x2, Pallas kernels: 13.3 us -> 6.45 us  [back(): pl.pallas_call(lambda *refs: back_kernel(first, *refs), in_specs=[pl.Bloc...]
    pallas_call x2, Pallas kernels: 14.9 us -> 11.3 us  [pool(): pl.pallas_call(lambda *refs: pool_kernel(other, *refs), in_specs=[pl.Bloc...]
    pallas_call x1, Pallas kernels: 3.47 us -> 0.84 us  [towers(): pl.pallas_call(tower_kernel, in_specs=[whole()] * 6, out_specs=[whole()]...]
    dynamic_slice x1 -> x0, local copies, waits for them, and re-layouts: 1.89 us -> none  [of_core(): lax.dynamic_index_in_dim(values, which, 1, False).reshape(N_CHIP * OWN, 128)]
    pallas_call x1, Pallas kernels: 1.8 us -> 0.06 us  [sum_parts(): pl.pallas_call(sum_kernel, in_specs=[whole()], out_specs=whole(), out_sha...]
  transfers between devices with their start and end apart: 3 -> 2, of which waited for: 1 -> 0; matrix products, arithmetic and copies ran while one was open for 0% -> 0% of each run, Pallas kernels for 8% -> 6%
where the time goes in v3:
time: 150 us; the launch traced here: 149 us
  blocking collectives  121 us (81%)
  Pallas kernels  21.2 us (14%)
  starting transfers between devices  3.83 us (3%)
    all_to_all x5, blocking collectives, exchange(): return lax.all_to_all(values, axes, 0, 0, tiled=True)  121 us
    pallas_call x2, Pallas kernels, pool(): pl.pallas_call(lambda *refs: pool_kernel(other, *refs), in_specs=[pl.Bloc...  11.3 us
    pallas_call x2, Pallas kernels, back(): pl.pallas_call(lambda *refs: back_kernel(first, *refs), in_specs=[pl.Bloc...  6.45 us
    ppermute x2, starting transfers between devices, to_other_core(): return lax.ppermute(values, 'core', [(0, 1), (1, 0)])  3.83 us
  transfers between devices with their start and end apart: 2, of which 0 were waited for; matrix products, arithmetic and copies ran while one was open for 0% of the time, Pallas kernels for 6%

profile of v3, /device:TPU:8, one launch (start us, length us, event | category | flops | bytes accessed | tf_op | source)
XLA Modules:
  0.0 149.2 jit_solution(9772725837218934141)
XLA Ops:
  0.6 0.1 pad_add_fusion.refs_0_.place_ref
  0.7 1.1 add_bitcast_fusion.refs_1_
  1.8 0.0 copy-start.5
  1.8 0.9 copy-done.5
  2.7 5.7 %pool.3 = (bf16[4096,1024]{1,0:T(8,128)(2,1)S(1)}, bf16[4096,128]{1,0:T(8,128)(2,1)S(1)}) custom-call(s32[2]{0:T(128)S(1)} %pad_add_fusion.refs_0_.place_ref, s32[512,128]{1,0:T(8,128)S(1)} %add_bitcast_fusion.refs_1_, bf16[1024,128]{1,0:T(8,128)(2,1)S(1)} %copy-done.5), custom_call_target="tpu_custom_call" | custom-call | flops 2147483648 | bytes 10485760 | tf_op jit(solution)/shard_map/pool/pallas_call | solution.py:100
  8.4 1.9 %collective-permute-start = (bf16[4096,128]{1,0:T(8,128)(2,1)S(1)}, bf16[4096,128]{1,0:T(8,128)(2,1)S(1)}, u32[]{:S(2)}, u32[]{:S(2)}) collective-permute-start(bf16[4096,128]{1,0:T(8,128)(2,1)S(1)} %get-tuple-element.27), channel_id=1, source_target_pairs={{0,16},{16,0},{1,17},{17,1},{2,18},{18,2},{3,19},{19,3},{4,20},{20... | collective-permute-start | bytes 3145736 | tf_op jit(solution)/shard_map/ppermute | solution.py:388
  10.3 5.7 %pool.2 = (bf16[4096,1024]{1,0:T(8,128)(2,1)S(1)}, bf16[4096,128]{1,0:T(8,128)(2,1)S(1)}) custom-call(s32[2]{0:T(128)S(1)} %pad_add_fusion.refs_0_.place_ref, s32[512,128]{1,0:T(8,128)S(1)} %add_bitcast_fusion.refs_1_, bf16[1024,128]{1,0:T(8,128)(2,1)S(1)} %copy-done.5), custom_call_target="tpu_custom_call" | custom-call | flops 2147483648 | bytes 10485760 | tf_op jit(solution)/shard_map/pool/pallas_call | solution.py:100
  16.0 0.0 collective-permute-done
  16.0 0.0 copy-start
  16.0 0.0 copy-start.1
  16.0 0.0 copy-start.2
  16.0 0.0 copy-start.3
  16.0 0.0 copy-start.4
  16.1 0.3 add_convert_fusion
  16.3 38.6 %all_to_all.25.parts_ref = bf16[16,256,128]{2,1,0:T(8,128)(2,1)S(1)} all-to-all(bf16[16,256,128]{2,1,0:T(8,128)(2,1)S(1)} %bitcast.5), channel_id=1, replica_groups=mesh['x_lo'=2,'z'=8,'core'=2,'x_hi'=2,'y'=8] {'x_lo','z'}, dimensions={0} | all-to-all | bytes 2097152 | tf_op jit(solution)/shard_map/all_to_all | solution.py:384
  55.0 0.0 copy-done
  55.0 0.0 copy-done.1
  55.0 0.0 copy-done.2
  55.0 0.0 copy-done.3
  55.0 0.0 copy-done.4
  55.0 0.8 towers.1
  55.8 19.4 %all_to_all.26.group_ref = bf16[16,48,128]{2,1,0:T(8,128)(2,1)S(1)} all-to-all(bf16[16,48,128]{2,1,0:T(8,128)(2,1)S(1)} %get-tuple-element.28), channel_id=1, replica_groups=mesh['x_lo'=2,'z'=8,'core'=2,'x_hi'=2,'y'=8] {'x_hi','y'}, dimensions={0} | all-to-all | bytes 393216 | tf_op jit(solution)/shard_map/all_to_all | solution.py:384
  75.3 1.7 %softmax_back.1 = (f32[1,16]{1,0:T(1,128)}, bf16[16,16,1536]{2,1,0:T(8,128)(2,1)S(1)}) custom-call(s32[2]{0:T(128)S(1)} %pad_add_fusion.refs_0_.place_ref, bf16[16,48,128]{2,1,0:T(8,128)(2,1)S(1)} %all_to_all.26.group_ref, s32[1,16]{1,0:T(1,128)S(1)} %copy-done.4, bf16[16,2048]{1,0:T(8,128)(2,1)S(1)} %get-tuple-element.29.pooled_ref, ...), custom_call_target="tpu_custom_call" | custom-call | tf_op jit(solution)/shard_map/softmax_back/pallas_call | solution.py:239
  77.0 24.9 %all_to_all.27.refs_1_ = bf16[16,16,1536]{2,1,0:T(8,128)(2,1)S(1)} all-to-all(bf16[16,16,1536]{2,1,0:T(8,128)(2,1)S(1)} %get-tuple-element.35), channel_id=1, replica_groups=mesh['x_lo'=2,'z'=8,'core'=2,'x_hi'=2,'y'=8] {'x_lo','z'}, dimensions={0} | all-to-all | bytes 1572864 | tf_op jit(solution)/shard_map/all_to_all | solution.py:384
  101.9 1.9 %collective-permute-start.1 = (bf16[16,16,1536]{2,1,0:T(8,128)(2,1)S(1)}, bf16[16,16,1536]{2,1,0:T(8,128)(2,1)S(1)}, u32[]{:S(2)}, u32[]{:S(2)}) collective-permute-start(bf16[16,16,1536]{2,1,0:T(8,128)(2,1)S(1)} %all_to_all.27.refs_1_), channel_id=1, source_target_pairs={{0,16},{16,0},{1,17},{17,1},{2,18},{18,2},{3,19},{19,3},{4,20},{20... | collective-permute-start | bytes 2359304 | tf_op jit(solution)/shard_map/ppermute | solution.py:388
  103.8 3.2 %back.2 = (f32[128,1024]{1,0:T(8,128)S(1)}, f32[2,64,512]{2,1,0:T(8,128)S(1)}, f32[2,32,128]{2,1,0:T(8,128)S(1)}) custom-call(s32[2]{0:T(128)S(1)} %pad_add_fusion.refs_0_.place_ref, bf16[16,16,1536]{2,1,0:T(8,128)(2,1)S(1)} %all_to_all.27.refs_1_, bf16[4096,1024]{1,0:T(8,128)(2,1)S(1)} %get-tuple-element.37.refs_2_, bf16[1024,512]{1,0:T(8,128)(2,1)S(1)} %copy-done, ...), custom_call_target="tpu_custom_call" | custom-call | flops 1073741824 | bytes 10485760 | tf_op jit(solution)/shard_map/back/pallas_call | solution.py:318
  107.0 0.0 collective-permute-done.1.refs_1_
  107.0 3.3 %back.3 = bf16[16,88,128]{2,1,0:T(8,128)(2,1)S(1)} custom-call(s32[2]{0:T(128)S(1)} %pad_add_fusion.refs_0_.place_ref, bf16[16,16,1536]{2,1,0:T(8,128)(2,1)S(1)} %collective-permute-done.1.refs_1_, bf16[4096,1024]{1,0:T(8,128)(2,1)S(1)} %get-tuple-element.36.refs_2_, bf16[1024,512]{1,0:T(8,128)(2,1)S(1)} %copy-done, bf16[1024,512]{1,0:T(8,128)(2,1)S(1)} %copy-done.1, ...), custom_call_target="tpu_custom_call" | custom-call | flops 1073741824 | bytes 10485760 | tf_op jit(solution)/shard_map/back/pallas_call | solution.py:318
  110.3 19.3 %all_to_all.28.parts_ref = bf16[16,88,128]{2,1,0:T(8,128)(2,1)S(1)} all-to-all(bf16[16,88,128]{2,1,0:T(8,128)(2,1)S(1)} %back.3), channel_id=1, replica_groups=mesh['x_lo'=2,'z'=8,'core'=2,'x_hi'=2,'y'=8] {'x_hi','y'}, dimensions={0} | all-to-all | bytes 720896 | tf_op jit(solution)/shard_map/all_to_all | solution.py:384
  129.6 0.1 sum_parts.1
  129.6 18.6 %all_to_all.29.sums_ref = bf16[16,88,128]{2,1,0:T(8,128)(2,1)S(1)} all-to-all(bf16[16,88,128]{2,1,0:T(8,128)(2,1)S(1)} %sum_parts.1), channel_id=1, replica_groups=mesh['x_lo'=2,'z'=8,'core'=2,'x_hi'=2,'y'=8] {'x_hi','y'}, dimensions={0} | all-to-all | bytes 720896 | tf_op jit(solution)/shard_map/all_to_all | solution.py:384
  148.3 0.9 spread.1
Async XLA Ops:
  1.8 1.0 copy-start.5
  8.4 7.6 %collective-permute-start = (bf16[4096,128]{1,0:T(8,128)(2,1)S(1)}, bf16[4096,128]{1,0:T(8,128)(2,1)S(1)}, u32[]{:S(2)}, u32[]{:S(2)}) collective-permute-start(bf16[4096,128]{1,0:T(8,128)(2,1)S(1)} %get-tuple-element.27), channel_id=1, source_target_pairs={{0,16},{16,0},{1,17},{17,1},{2,18},{18,2},{3,19},{19,3},{4,20},{20... | collective-permute-start | bytes 3145736 | tf_op jit(solution)/shard_map/ppermute | solution.py:388
  16.0 39.0 %copy-start = (bf16[1024,512]{1,0:T(8,128)(2,1)S(1)}, bf16[1024,512]{1,0:T(8,128)(2,1)}, u32[]{:S(2)}) copy-start(bf16[1024,512]{1,0:T(8,128)(2,1)} %refs_3_.3) | copy-start | bytes 3145732
  16.0 39.0 %copy-start.1 = (bf16[1024,512]{1,0:T(8,128)(2,1)S(1)}, bf16[1024,512]{1,0:T(8,128)(2,1)}, u32[]{:S(2)}) copy-start(bf16[1024,512]{1,0:T(8,128)(2,1)} %refs_4_.3) | copy-start | bytes 3145732
  16.0 38.9 %copy-start.2 = (bf16[512,128]{1,0:T(8,128)(2,1)S(1)}, bf16[512,128]{1,0:T(8,128)(2,1)}, u32[]{:S(2)}) copy-start(bf16[512,128]{1,0:T(8,128)(2,1)} %head0_ref.3) | copy-start | bytes 393220
  16.0 38.9 %copy-start.3 = (bf16[512,128]{1,0:T(8,128)(2,1)S(1)}, bf16[512,128]{1,0:T(8,128)(2,1)}, u32[]{:S(2)}) copy-start(bf16[512,128]{1,0:T(8,128)(2,1)} %head1_ref.3) | copy-start | bytes 393220
  16.0 38.9 %copy-start.4 = (s32[1,16]{1,0:T(1,128)S(1)}, s32[1,16]{1,0:T(1,128)}, u32[]{:S(2)}) copy-start(s32[1,16]{1,0:T(1,128)} %counts_ref.3) | copy-start | bytes 196
  101.9 5.1 %collective-permute-start.1 = (bf16[16,16,1536]{2,1,0:T(8,128)(2,1)S(1)}, bf16[16,16,1536]{2,1,0:T(8,128)(2,1)S(1)}, u32[]{:S(2)}, u32[]{:S(2)}) collective-permute-start(bf16[16,16,1536]{2,1,0:T(8,128)(2,1)S(1)} %all_to_all.27.refs_1_), channel_id=1, source_target_pairs={{0,16},{16,0},{1,17},{17,1},{2,18},{18,2},{3,19},{19,3},{4,20},{20... | collective-permute-start | bytes 2359304 | tf_op jit(solution)/shard_map/ppermute | solution.py:388

commit v4 on v3

--- a/solution.py
+++ b/solution.py
@@ -15,6 +15,7 @@
 CHIPS = ("x_lo", "z")
 DP = ("x_hi", "y")
 N_CHIP = 16
+N_Z = 8
 N_DP = 16
 OWN = 16
 FEATURES = 16
@@ -27,8 +28,8 @@
 IN_WIDTH = TOWER_FEATURES * EMB
 GRAD_WIDTH = 12 * 128
 COLUMNS_AT = 2 * HID + 2 * OUT
-POOL_SAMPLES = 64
-BACK_PARTS = 4
+POOL_SAMPLES = 32
+BACK_PARTS = 2
 CHUNK = 88
 
 BF16 = jnp.bfloat16
@@ -77,9 +78,10 @@
             ]
 
 
-def pool_kernel(other, place_ref, lookups_ref, table_ref, weights_ref, partial_ref):
-    core = place_ref[0] ^ other
-    parts = N_CHIP * OWN // POOL_SAMPLES
+def pool_kernel(other_x, other_core, place_ref, lookups_ref, table_ref, weights_ref, partial_ref):
+    core = place_ref[0] ^ other_core
+    x_lo = place_ref[2] ^ other_x
+    parts = N_Z * OWN // POOL_SAMPLES
     rows = POOL_SAMPLES * FEATURES
 
     def sum_part(part):
@@ -88,7 +90,7 @@
 
     for part in range(parts):
         chips = range(part * POOL_SAMPLES // OWN, (part + 1) * POOL_SAMPLES // OWN)
-        starts = [pl.multiple_of((2 * chip + core) * OWN, OWN) for chip in chips]
+        starts = [pl.multiple_of((2 * (x_lo * N_Z + z) + core) * OWN, OWN) for z in chips]
         lookups = jnp.concatenate([lookups_ref[pl.ds(start, OWN), :] for start in starts], axis=0)
         lookup_weights(lookups & 1023, lax.shift_right_logical(lookups, 10), weights_ref, part * rows)
         if part > 0:
@@ -96,18 +98,18 @@
     sum_part(parts - 1)
 
 
-def pool(other, place, lookups, table):
-    return pl.pallas_call(
-        lambda *refs: pool_kernel(other, *refs),
+def pool(other_x, other_core, place, lookups, table):
+    return pl.pallas_call(
+        lambda *refs: pool_kernel(other_x, other_core, *refs),
         in_specs=[pl.BlockSpec(memory_space=pltpu.SMEM)] + [whole()] * 2,
         out_specs=[whole()] * 2,
         out_shape=[
-            jax.ShapeDtypeStruct((N_CHIP * BLOCK, ROWS), BF16),
-            jax.ShapeDtypeStruct((N_CHIP * BLOCK, EMB), BF16),
+            jax.ShapeDtypeStruct((N_Z * BLOCK, ROWS), BF16),
+            jax.ShapeDtypeStruct((N_Z * BLOCK, EMB), BF16),
         ],
         compiler_params=room(8),
         cost_estimate=pl.CostEstimate(
-            flops=2 * N_CHIP * BLOCK * ROWS * EMB * 2, bytes_accessed=10 * 2**20, transcendentals=0
+            flops=2 * N_Z * BLOCK * ROWS * EMB * 2, bytes_accessed=5 * 2**20, transcendentals=0
         ),
         name="pool",
     )(place, lookups, table)
@@ -132,7 +134,7 @@
     pooled_ref, pre_ref, hidden_ref, unit_ref, scale_ref, send_ref, rows_ref,
 ):
     total = parts_ref[0].astype(F32)
-    for s in range(1, N_CHIP):
+    for s in range(1, N_Z):
         total = total + parts_ref[s].astype(F32)
     rows_ref[...] = total
     for f in range(FEATURES):
@@ -250,14 +252,15 @@
 
 
 def back_kernel(first, *refs):
-    place_ref, grads_ref, weights_ref, layer0_ref, layer1_ref = refs[:5]
+    place_ref, grads_ref, here_ref, there_ref, layer0_ref, layer1_ref = refs[:6]
     if first:
-        total_ref, layers_ref, heads_ref, pooled_ref = refs[5:]
+        total_ref, layers_ref, heads_ref, pooled_ref = refs[6:]
     else:
-        before_ref, layers_before_ref, heads_before_ref = refs[5:8]
-        send_ref, pooled_ref, layers_ref, heads_ref = refs[8:]
+        before_ref, layers_before_ref, heads_before_ref = refs[6:9]
+        send_ref, pooled_ref, layers_ref, heads_ref = refs[9:]
     samples = N_CHIP * OWN
-    rows = samples * FEATURES // BACK_PARTS
+    half = samples * FEATURES // 2
+    rows = half // BACK_PARTS
     grads = grads_ref[...].reshape(samples, GRAD_WIDTH)
     inputs = grads[:, COLUMNS_AT : COLUMNS_AT + 128]
     hidden = grads[:, COLUMNS_AT + 128 :]
@@ -279,10 +282,13 @@
         layers_ref[tower] = layer_rows
         heads_ref[tower] = head_rows
     total = None if first else before_ref[...]
-    for part in range(BACK_PARTS):
-        at = pl.ds(part * rows, rows)
-        term = dot(pooled_ref[at, :].astype(BF16), weights_ref[at, :], TN)
-        total = term if total is None else total + term
+    for other_x, weights_ref in enumerate((here_ref, there_ref)):
+        first_row = (place_ref[2] ^ other_x) * half
+        for part in range(BACK_PARTS):
+            at = pl.ds(pl.multiple_of(first_row + part * rows, rows), rows)
+            weights = weights_ref[part * rows : (part + 1) * rows, :]
+            term = dot(pooled_ref[at, :].astype(BF16), weights, TN)
+            total = term if total is None else total + term
     if first:
         total_ref[...] = total
         return
@@ -320,7 +326,7 @@
         in_specs=[
             pl.BlockSpec(memory_space=pltpu.SMEM),
         ]
-        + [whole()] * (4 + len(before)),
+        + [whole()] * (5 + len(before)),
         out_specs=[whole()] * len(out_shape),
         out_shape=out_shape,
         scratch_shapes=scratch,
@@ -329,7 +335,7 @@
             flops=2 * N_CHIP * BLOCK * ROWS * EMB, bytes_accessed=10 * 2**20, transcendentals=0
         ),
         name="back",
-    )(place, grads, weights, layer0, layer1, *before)
+    )(place, grads, *weights, layer0, layer1, *before)
 
 
 def sum_kernel(parts_ref, send_ref):
@@ -384,18 +390,27 @@
     return lax.all_to_all(values, axes, 0, 0, tiled=True)
 
 
-def to_other_core(values):
-    return lax.ppermute(values, "core", [(0, 1), (1, 0)])
+def to_other(values, axis):
+    return lax.ppermute(values, axis, [(0, 1), (1, 0)])
+
+
+def add(*terms):
+    return sum(term.astype(F32) for term in terms).astype(BF16)
 
 
 def shards(ids, mults, table, user_layer, user_head, item_layer, item_head, counts):
-    place = jnp.stack([lax.axis_index("core"), lax.axis_index(DP)])
+    place = jnp.stack([lax.axis_index("core"), lax.axis_index(DP), lax.axis_index("x_lo")])
     lookups = ids[0] + 1024 * mults[0]
-    other_weights, other_partial = pool(1, place, lookups, table)
-    arrived = to_other_core(other_partial)
-    own_weights, own_partial = pool(0, place, lookups, table)
-    chip_partial = (own_partial.astype(F32) + arrived.astype(F32)).astype(BF16)
-    parts = exchange(chip_partial.reshape(N_CHIP, BLOCK, EMB), CHIPS)
+    both_weights, both_partial = pool(1, 1, place, lookups, table)
+    both_arrived = to_other(both_partial, "core")
+    x_weights, x_partial = pool(1, 0, place, lookups, table)
+    x_sum, lookups = lax.optimization_barrier((add(x_partial, both_arrived), lookups))
+    x_arrived = to_other(x_sum, "x_lo")
+    core_weights, core_partial = pool(0, 1, place, lookups, table)
+    core_arrived = to_other(core_partial, "core")
+    own_weights, own_partial = pool(0, 0, place, lookups, table)
+    total_partial = add(own_partial, core_arrived, x_arrived)
+    parts = exchange(total_partial.reshape(N_Z, BLOCK, EMB), "z")
     pooled, pre, hidden, unit, scale, units = towers(
         parts, counts, user_layer, user_head, item_layer, item_head
     )
@@ -404,9 +419,11 @@
         place, group, counts, pooled, pre, hidden, unit, scale, user_head, item_head
     )
     own_grads = exchange(grads, CHIPS)
-    other_grads = to_other_core(own_grads)
-    before = back(place, own_grads, own_weights, user_layer, item_layer)
-    (terms,) = back(place, other_grads, other_weights, user_layer, item_layer, tuple(before))
+    other_grads = to_other(own_grads, "core")
+    before = back(place, own_grads, (own_weights, x_weights), user_layer, item_layer)
+    (terms,) = back(
+        place, other_grads, (core_weights, both_weights), user_layer, item_layer, tuple(before)
+    )
     sums = exchange(sum_parts(exchange(terms, DP)), DP)
     table_change, layer0, head0, layer1, head1 = spread(sums)
     return (losses, table_change, layer0, head0, layer1, head1)

time: 150 us -> 147 us (0.980)
  blocking collectives: 121 us -> 106 us
  starting transfers between devices: 3.83 us -> 9.62 us
  waiting for transfers between devices: 0.01 us -> 3.68 us
  Pallas kernels: 21.2 us -> 23.6 us
    all_to_all x5, blocking collectives: 121 us -> 106 us  [exchange(): return lax.all_to_all(values, axes, 0, 0, tiled=True)]
    ppermute x2 -> x4, starting transfers between devices: 3.83 us -> 9.62 us  [to_other(): return lax.ppermute(values, axis, [(0, 1), (1, 0)])]
    ppermute x2 -> x4, waiting for transfers between devices: 0.01 us -> 3.68 us  [to_other(): return lax.ppermute(values, axis, [(0, 1), (1, 0)])]
    pallas_call x2 -> x4, Pallas kernels: 11.3 us -> 13.6 us  [pool(): pl.pallas_call(lambda *refs: pool_kernel(other_x, other_core, *refs), in_...]
  transfers between devices with their start and end apart: 2 -> 4, of which waited for: 0 -> 1; matrix products, arithmetic and copies ran while one was open for 0% -> 0% of each run, Pallas kernels for 6% -> 9%
where the time goes in v4:
time: 147 us; the launch traced here: 146 us
  blocking collectives  106 us (72%)
  Pallas kernels  23.6 us (16%)
  starting transfers between devices  9.62 us (7%)
  waiting for transfers between devices  3.68 us (3%)
  other arithmetic  1.49 us (1%)
    all_to_all x5, blocking collectives, exchange(): return lax.all_to_all(values, axes, 0, 0, tiled=True)  106 us
    pallas_call x4, Pallas kernels, pool(): pl.pallas_call(lambda *refs: pool_kernel(other_x, other_core, *refs), in_...  13.6 us
    ppermute x4, starting transfers between devices, to_other(): return lax.ppermute(values, axis, [(0, 1), (1, 0)])  9.62 us
    pallas_call x2, Pallas kernels, back(): pl.pallas_call(lambda *refs: back_kernel(first, *refs), in_specs=[pl.Bloc...  6.56 us
    ppermute x4, waiting for transfers between devices, to_other(): return lax.ppermute(values, axis, [(0, 1), (1, 0)])  3.68 us
  transfers between devices with their start and end apart: 4, of which 1 were waited for; matrix products, arithmetic and copies ran while one was open for 0% of the time, Pallas kernels for 9%

profile of v4, /device:TPU:8, one launch (start us, length us, event | category | flops | bytes accessed | tf_op | source)
XLA Modules:
  0.0 146.3 jit_solution(12509946614151868732)
XLA Ops:
  0.6 1.1 add_bitcast_fusion.refs_1_
  1.7 0.1 pad_add_fusion.refs_0_.place_ref
  1.8 0.9 copy-done.5
  2.7 3.4 %pool.5 = (bf16[2048,1024]{1,0:T(8,128)(2,1)S(1)}, bf16[2048,128]{1,0:T(8,128)(2,1)S(1)}) custom-call(s32[3]{0:T(128)S(1)} %pad_add_fusion.refs_0_.place_ref, s32[512,128]{1,0:T(8,128)S(1)} %add_bitcast_fusion.refs_1_, bf16[1024,128]{1,0:T(8,128)(2,1)S(1)} %copy-done.5), custom_call_target="tpu_custom_call" | custom-call | flops 1073741824 | bytes 5242880 | tf_op jit(solution)/shard_map/pool/pallas_call | solution.py:102
  6.1 0.0 copy-start.6
  6.1 2.1 %collective-permute-start = (bf16[2048,128]{1,0:T(8,128)(2,1)S(1)}, bf16[2048,128]{1,0:T(8,128)(2,1)S(1)}, u32[]{:S(2)}, u32[]{:S(2)}) collective-permute-start(bf16[2048,128]{1,0:T(8,128)(2,1)S(1)} %get-tuple-element.33), channel_id=1, source_target_pairs={{0,16},{16,0},{1,17},{17,1},{2,18},{18,2},{3,19},{19,3},{4,20},{20... | collective-permute-start | bytes 1572872 | tf_op jit(solution)/shard_map/ppermute | solution.py:394
  8.2 3.4 %pool.4 = (bf16[2048,1024]{1,0:T(8,128)(2,1)S(1)}, bf16[2048,128]{1,0:T(8,128)(2,1)S(1)}) custom-call(s32[3]{0:T(128)S(1)} %pad_add_fusion.refs_0_.place_ref, s32[512,128]{1,0:T(8,128)S(1)} %add_bitcast_fusion.refs_1_, bf16[1024,128]{1,0:T(8,128)(2,1)S(1)} %copy-done.5), custom_call_target="tpu_custom_call" | custom-call | flops 1073741824 | bytes 5242880 | tf_op jit(solution)/shard_map/pool/pallas_call | solution.py:102
  11.6 0.0 collective-permute-done
  11.6 0.1 add_convert_fusion.1
  11.8 3.4 %collective-permute-start.2 = (bf16[2048,128]{1,0:T(8,128)(2,1)S(1)}, bf16[2048,128]{1,0:T(8,128)(2,1)S(1)}, u32[]{:S(2)}, u32[]{:S(2)}) collective-permute-start(bf16[2048,128]{1,0:T(8,128)(2,1)S(1)} %add_convert_fusion.1), channel_id=1, source_target_pairs={{0,256},{256,0},{1,257},{257,1},{2,258},{258,2},{3,259},{259,3},{4... | collective-permute-start | bytes 1572872 | tf_op jit(solution)/shard_map/ppermute | solution.py:394
  15.2 3.4 %pool.7 = (bf16[2048,1024]{1,0:T(8,128)(2,1)S(1)}, bf16[2048,128]{1,0:T(8,128)(2,1)S(1)}) custom-call(s32[3]{0:T(128)S(1)} %pad_add_fusion.refs_0_.place_ref, s32[512,128]{1,0:T(8,128)S(1)} %add_bitcast_fusion.refs_1_, bf16[1024,128]{1,0:T(8,128)(2,1)S(1)} %copy-done.5), custom_call_target="tpu_custom_call" | custom-call | flops 1073741824 | bytes 5242880 | tf_op jit(solution)/shard_map/pool/pallas_call | solution.py:102
  18.6 0.0 copy-start
  18.6 0.0 copy-start.1
  18.6 0.0 copy-start.2
  18.6 0.0 copy-start.3
  18.6 0.0 copy-start.4
  18.6 2.3 %collective-permute-start.1 = (bf16[2048,128]{1,0:T(8,128)(2,1)S(1)}, bf16[2048,128]{1,0:T(8,128)(2,1)S(1)}, u32[]{:S(2)}, u32[]{:S(2)}) collective-permute-start(bf16[2048,128]{1,0:T(8,128)(2,1)S(1)} %get-tuple-element.36), channel_id=1, source_target_pairs={{0,16},{16,0},{1,17},{17,1},{2,18},{18,2},{3,19},{19,3},{4,20},{20... | collective-permute-start | bytes 1572872 | tf_op jit(solution)/shard_map/ppermute | solution.py:394
  20.9 3.4 %pool.6 = (bf16[2048,1024]{1,0:T(8,128)(2,1)S(1)}, bf16[2048,128]{1,0:T(8,128)(2,1)S(1)}) custom-call(s32[3]{0:T(128)S(1)} %pad_add_fusion.refs_0_.place_ref, s32[512,128]{1,0:T(8,128)S(1)} %add_bitcast_fusion.refs_1_, bf16[1024,128]{1,0:T(8,128)(2,1)S(1)} %copy-done.6), custom_call_target="tpu_custom_call" | custom-call | flops 1073741824 | bytes 5242880 | tf_op jit(solution)/shard_map/pool/pallas_call | solution.py:102
  24.3 3.7 %collective-permute-done.2 = bf16[2048,128]{1,0:T(8,128)(2,1)S(1)} collective-permute-done((bf16[2048,128]{1,0:T(8,128)(2,1)S(1)}, bf16[2048,128]{1,0:T(8,128)(2,1)S(1)}, u32[]{:S(2)}, u32[]{:S(2)}) %collective-permute-start.2) | collective-permute-done | bytes 524320 | tf_op jit(solution)/shard_map/ppermute | solution.py:394
  28.0 0.2 add_convert_fusion
  28.2 27.5 %all_to_all.25.parts_ref = bf16[8,256,128]{2,1,0:T(8,128)(2,1)S(1)} all-to-all(bf16[8,256,128]{2,1,0:T(8,128)(2,1)S(1)} %bitcast.6), channel_id=1, replica_groups=mesh['x_lo'=2,'z'=8,'core'=2,'x_hi'=2,'y'=8] {'z'}, dimensions={0} | all-to-all | bytes 1048576 | tf_op jit(solution)/shard_map/all_to_all | solution.py:390
  55.7 0.8 towers.1
  56.5 20.0 %all_to_all.26.group_ref = bf16[16,48,128]{2,1,0:T(8,128)(2,1)S(1)} all-to-all(bf16[16,48,128]{2,1,0:T(8,128)(2,1)S(1)} %get-tuple-element.38), channel_id=1, replica_groups=mesh['x_lo'=2,'z'=8,'core'=2,'x_hi'=2,'y'=8] {'x_hi','y'}, dimensions={0} | all-to-all | bytes 393216 | tf_op jit(solution)/shard_map/all_to_all | solution.py:390
  76.6 1.7 %softmax_back.1 = (f32[1,16]{1,0:T(1,128)}, bf16[16,16,1536]{2,1,0:T(8,128)(2,1)S(1)}) custom-call(s32[3]{0:T(128)S(1)} %pad_add_fusion.refs_0_.place_ref, bf16[16,48,128]{2,1,0:T(8,128)(2,1)S(1)} %all_to_all.26.group_ref, s32[1,16]{1,0:T(1,128)S(1)} %copy-done.4, bf16[16,2048]{1,0:T(8,128)(2,1)S(1)} %get-tuple-element.39.pooled_ref, ...), custom_call_target="tpu_custom_call" | custom-call | tf_op jit(solution)/shard_map/softmax_back/pallas_call | solution.py:241
  78.3 21.1 %all_to_all.27.refs_1_ = bf16[16,16,1536]{2,1,0:T(8,128)(2,1)S(1)} all-to-all(bf16[16,16,1536]{2,1,0:T(8,128)(2,1)S(1)} %get-tuple-element.45), channel_id=1, replica_groups=mesh['x_lo'=2,'z'=8,'core'=2,'x_hi'=2,'y'=8] {'x_lo','z'}, dimensions={0} | all-to-all | bytes 1572864 | tf_op jit(solution)/shard_map/all_to_all | solution.py:390
  99.3 1.9 %collective-permute-start.3 = (bf16[16,16,1536]{2,1,0:T(8,128)(2,1)S(1)}, bf16[16,16,1536]{2,1,0:T(8,128)(2,1)S(1)}, u32[]{:S(2)}, u32[]{:S(2)}) collective-permute-start(bf16[16,16,1536]{2,1,0:T(8,128)(2,1)S(1)} %all_to_all.27.refs_1_), channel_id=1, source_target_pairs={{0,16},{16,0},{1,17},{17,1},{2,18},{18,2},{3,19},{19,3},{4,20},{20... | collective-permute-start | bytes 2359304 | tf_op jit(solution)/shard_map/ppermute | solution.py:394
  101.2 3.3 %back.2 = (f32[128,1024]{1,0:T(8,128)S(1)}, f32[2,64,512]{2,1,0:T(8,128)S(1)}, f32[2,32,128]{2,1,0:T(8,128)S(1)}) custom-call(s32[3]{0:T(128)S(1)} %pad_add_fusion.refs_0_.place_ref, bf16[16,16,1536]{2,1,0:T(8,128)(2,1)S(1)} %all_to_all.27.refs_1_, bf16[2048,1024]{1,0:T(8,128)(2,1)S(1)} %get-tuple-element.48.refs_2_, ...), custom_call_target="tpu_custom_call" | custom-call | flops 1073741824 | bytes 10485760 | tf_op jit(solution)/shard_map/back/pallas_call | solution.py:324
  104.5 3.3 %back.3 = bf16[16,88,128]{2,1,0:T(8,128)(2,1)S(1)} custom-call(s32[3]{0:T(128)S(1)} %pad_add_fusion.refs_0_.place_ref, bf16[16,16,1536]{2,1,0:T(8,128)(2,1)S(1)} %collective-permute-done.3.refs_1_, bf16[2048,1024]{1,0:T(8,128)(2,1)S(1)} %get-tuple-element.46.refs_2_, bf16[2048,1024]{1,0:T(8,128)(2,1)S(1)} %get-tuple-element.47.refs_3_, ...), custom_call_target="tpu_custom_call" | custom-call | flops 1073741824 | bytes 10485760 | tf_op jit(solution)/shard_map/back/pallas_call | solution.py:324
  107.8 18.8 %all_to_all.28.parts_ref = bf16[16,88,128]{2,1,0:T(8,128)(2,1)S(1)} all-to-all(bf16[16,88,128]{2,1,0:T(8,128)(2,1)S(1)} %back.3), channel_id=1, replica_groups=mesh['x_lo'=2,'z'=8,'core'=2,'x_hi'=2,'y'=8] {'x_hi','y'}, dimensions={0} | all-to-all | bytes 720896 | tf_op jit(solution)/shard_map/all_to_all | solution.py:390
  126.7 0.1 sum_parts.1
  126.7 18.7 %all_to_all.29.sums_ref = bf16[16,88,128]{2,1,0:T(8,128)(2,1)S(1)} all-to-all(bf16[16,88,128]{2,1,0:T(8,128)(2,1)S(1)} %sum_parts.1), channel_id=1, replica_groups=mesh['x_lo'=2,'z'=8,'core'=2,'x_hi'=2,'y'=8] {'x_hi','y'}, dimensions={0} | all-to-all | bytes 720896 | tf_op jit(solution)/shard_map/all_to_all | solution.py:390
  145.4 0.9 spread.1
  (9 shorter events, 0.0 us)
Async XLA Ops:
  1.8 1.0 copy-start.5
  6.1 14.8 %copy-start.6 = (bf16[1024,128]{1,0:T(8,128)(2,1)S(1)}, bf16[1024,128]{1,0:T(8,128)(2,1)}, u32[]{:S(2)}) copy-start(bf16[1024,128]{1,0:T(8,128)(2,1)} %refs_2_.7) | copy-start | bytes 786436
  6.1 5.5 %collective-permute-start = (bf16[2048,128]{1,0:T(8,128)(2,1)S(1)}, bf16[2048,128]{1,0:T(8,128)(2,1)S(1)}, u32[]{:S(2)}, u32[]{:S(2)}) collective-permute-start(bf16[2048,128]{1,0:T(8,128)(2,1)S(1)} %get-tuple-element.33), channel_id=1, source_target_pairs={{0,16},{16,0},{1,17},{17,1},{2,18},{18,2},{3,19},{19,3},{4,20},{20... | collective-permute-start | bytes 1572872 | tf_op jit(solution)/shard_map/ppermute | solution.py:394
  11.8 16.2 %collective-permute-start.2 = (bf16[2048,128]{1,0:T(8,128)(2,1)S(1)}, bf16[2048,128]{1,0:T(8,128)(2,1)S(1)}, u32[]{:S(2)}, u32[]{:S(2)}) collective-permute-start(bf16[2048,128]{1,0:T(8,128)(2,1)S(1)} %add_convert_fusion.1), channel_id=1, source_target_pairs={{0,256},{256,0},{1,257},{257,1},{2,258},{258,2},{3,259},{259,3},{4... | collective-permute-start | bytes 1572872 | tf_op jit(solution)/shard_map/ppermute | solution.py:394
  18.6 37.1 %copy-start = (bf16[1024,512]{1,0:T(8,128)(2,1)S(1)}, bf16[1024,512]{1,0:T(8,128)(2,1)}, u32[]{:S(2)}) copy-start(bf16[1024,512]{1,0:T(8,128)(2,1)} %refs_4_.3) | copy-start | bytes 3145732
  18.6 37.1 %copy-start.1 = (bf16[1024,512]{1,0:T(8,128)(2,1)S(1)}, bf16[1024,512]{1,0:T(8,128)(2,1)}, u32[]{:S(2)}) copy-start(bf16[1024,512]{1,0:T(8,128)(2,1)} %refs_5_.3) | copy-start | bytes 3145732
  18.6 37.1 %copy-start.2 = (bf16[512,128]{1,0:T(8,128)(2,1)S(1)}, bf16[512,128]{1,0:T(8,128)(2,1)}, u32[]{:S(2)}) copy-start(bf16[512,128]{1,0:T(8,128)(2,1)} %head0_ref.3) | copy-start | bytes 393220
  18.6 37.1 %copy-start.3 = (bf16[512,128]{1,0:T(8,128)(2,1)S(1)}, bf16[512,128]{1,0:T(8,128)(2,1)}, u32[]{:S(2)}) copy-start(bf16[512,128]{1,0:T(8,128)(2,1)} %head1_ref.3) | copy-start | bytes 393220
  18.6 37.1 %copy-start.4 = (s32[1,16]{1,0:T(1,128)S(1)}, s32[1,16]{1,0:T(1,128)}, u32[]{:S(2)}) copy-start(s32[1,16]{1,0:T(1,128)} %counts_ref.3) | copy-start | bytes 196
  18.6 9.4 %collective-permute-start.1 = (bf16[2048,128]{1,0:T(8,128)(2,1)S(1)}, bf16[2048,128]{1,0:T(8,128)(2,1)S(1)}, u32[]{:S(2)}, u32[]{:S(2)}) collective-permute-start(bf16[2048,128]{1,0:T(8,128)(2,1)S(1)} %get-tuple-element.36), channel_id=1, source_target_pairs={{0,16},{16,0},{1,17},{17,1},{2,18},{18,2},{3,19},{19,3},{4,20},{20... | collective-permute-start | bytes 1572872 | tf_op jit(solution)/shard_map/ppermute | solution.py:394
  99.3 5.2 %collective-permute-start.3 = (bf16[16,16,1536]{2,1,0:T(8,128)(2,1)S(1)}, bf16[16,16,1536]{2,1,0:T(8,128)(2,1)S(1)}, u32[]{:S(2)}, u32[]{:S(2)}) collective-permute-start(bf16[16,16,1536]{2,1,0:T(8,128)(2,1)S(1)} %all_to_all.27.refs_1_), channel_id=1, source_target_pairs={{0,16},{16,0},{1,17},{17,1},{2,18},{18,2},{3,19},{19,3},{4,20},{20... | collective-permute-start | bytes 2359304 | tf_op jit(solution)/shard_map/ppermute | solution.py:394

commit v5 on v4

--- a/solution.py
+++ b/solution.py
@@ -29,7 +29,7 @@
 GRAD_WIDTH = 12 * 128
 COLUMNS_AT = 2 * HID + 2 * OUT
 POOL_SAMPLES = 32
-BACK_PARTS = 2
+BACK_ROWS = 1024
 CHUNK = 88
 
 BF16 = jnp.bfloat16
@@ -78,10 +78,15 @@
             ]
 
 
-def pool_kernel(other_x, other_core, place_ref, lookups_ref, table_ref, weights_ref, partial_ref):
+def pool_kernel(groups, other_core, place_ref, lookups_ref, table_ref, weights_ref, partial_ref):
     core = place_ref[0] ^ other_core
-    x_lo = place_ref[2] ^ other_x
-    parts = N_Z * OWN // POOL_SAMPLES
+    devices = [(other_x, z) for other_x, low, high in groups for z in range(low, high)]
+    starts = [
+        pl.multiple_of((2 * ((place_ref[2] ^ other_x) * N_Z + z) + core) * OWN, OWN)
+        for other_x, z in devices
+    ]
+    together = POOL_SAMPLES // OWN
+    parts = len(devices) // together
     rows = POOL_SAMPLES * FEATURES
 
     def sum_part(part):
@@ -89,27 +94,27 @@
         partial_ref[at, :] = dot(weights_ref[at, :], table_ref[...]).astype(BF16)
 
     for part in range(parts):
-        chips = range(part * POOL_SAMPLES // OWN, (part + 1) * POOL_SAMPLES // OWN)
-        starts = [pl.multiple_of((2 * (x_lo * N_Z + z) + core) * OWN, OWN) for z in chips]
-        lookups = jnp.concatenate([lookups_ref[pl.ds(start, OWN), :] for start in starts], axis=0)
+        here = starts[part * together : (part + 1) * together]
+        lookups = jnp.concatenate([lookups_ref[pl.ds(start, OWN), :] for start in here], axis=0)
         lookup_weights(lookups & 1023, lax.shift_right_logical(lookups, 10), weights_ref, part * rows)
         if part > 0:
             sum_part(part - 1)
     sum_part(parts - 1)
 
 
-def pool(other_x, other_core, place, lookups, table):
-    return pl.pallas_call(
-        lambda *refs: pool_kernel(other_x, other_core, *refs),
+def pool(groups, other_core, place, lookups, table):
+    rows = sum(high - low for _, low, high in groups) * BLOCK
+    return pl.pallas_call(
+        lambda *refs: pool_kernel(groups, other_core, *refs),
         in_specs=[pl.BlockSpec(memory_space=pltpu.SMEM)] + [whole()] * 2,
         out_specs=[whole()] * 2,
         out_shape=[
-            jax.ShapeDtypeStruct((N_Z * BLOCK, ROWS), BF16),
-            jax.ShapeDtypeStruct((N_Z * BLOCK, EMB), BF16),
+            jax.ShapeDtypeStruct((rows, ROWS), BF16),
+            jax.ShapeDtypeStruct((rows, EMB), BF16),
         ],
         compiler_params=room(8),
         cost_estimate=pl.CostEstimate(
-            flops=2 * N_Z * BLOCK * ROWS * EMB * 2, bytes_accessed=5 * 2**20, transcendentals=0
+            flops=2 * rows * ROWS * EMB * 2, bytes_accessed=rows * ROWS * 2, transcendentals=0
         ),
         name="pool",
     )(place, lookups, table)
@@ -251,16 +256,17 @@
     )(place, group, counts, pooled, pre, hidden, unit, scale, head0, head1)
 
 
-def back_kernel(first, *refs):
-    place_ref, grads_ref, here_ref, there_ref, layer0_ref, layer1_ref = refs[:6]
+def back_kernel(first, spans, *refs):
+    place_ref, grads_ref, layer0_ref, layer1_ref = refs[:4]
+    weights_refs = refs[4 : 4 + len(spans)]
+    refs = refs[4 + len(spans) :]
     if first:
-        total_ref, layers_ref, heads_ref, pooled_ref = refs[6:]
+        total_ref, layers_ref, heads_ref, pooled_ref = refs
     else:
-        before_ref, layers_before_ref, heads_before_ref = refs[6:9]
-        send_ref, pooled_ref, layers_ref, heads_ref = refs[9:]
+        before_ref, layers_before_ref, heads_before_ref = refs[:3]
+        send_ref, pooled_ref, layers_ref, heads_ref = refs[3:]
     samples = N_CHIP * OWN
     half = samples * FEATURES // 2
-    rows = half // BACK_PARTS
     grads = grads_ref[...].reshape(samples, GRAD_WIDTH)
     inputs = grads[:, COLUMNS_AT : COLUMNS_AT + 128]
     hidden = grads[:, COLUMNS_AT + 128 :]
@@ -282,13 +288,16 @@
         layers_ref[tower] = layer_rows
         heads_ref[tower] = head_rows
     total = None if first else before_ref[...]
-    for other_x, weights_ref in enumerate((here_ref, there_ref)):
-        first_row = (place_ref[2] ^ other_x) * half
-        for part in range(BACK_PARTS):
-            at = pl.ds(pl.multiple_of(first_row + part * rows, rows), rows)
-            weights = weights_ref[part * rows : (part + 1) * rows, :]
-            term = dot(pooled_ref[at, :].astype(BF16), weights, TN)
-            total = term if total is None else total + term
+    for groups, weights_ref in zip(spans, weights_refs):
+        here = 0
+        for other_x, low, high in groups:
+            first_row = (place_ref[2] ^ other_x) * half
+            for start in range(low * BLOCK, high * BLOCK, BACK_ROWS):
+                at = pl.ds(pl.multiple_of(first_row + start, BACK_ROWS), BACK_ROWS)
+                weights = weights_ref[here : here + BACK_ROWS, :]
+                term = dot(pooled_ref[at, :].astype(BF16), weights, TN)
+                total = term if total is None else total + term
+                here += BACK_ROWS
     if first:
         total_ref[...] = total
         return
@@ -311,6 +320,7 @@
 
 def back(place, grads, weights, layer0, layer1, before=None):
     first = before is None
+    spans = tuple(weights)
     total = jax.ShapeDtypeStruct((EMB, ROWS), F32)
     layers = jax.ShapeDtypeStruct((2, 64, HID), F32)
     heads = jax.ShapeDtypeStruct((2, 32, OUT), F32)
@@ -322,11 +332,11 @@
         scratch += [pltpu.VMEM(layers.shape, F32), pltpu.VMEM(heads.shape, F32)]
     before = before or ()
     return pl.pallas_call(
-        lambda *refs: back_kernel(first, *refs),
+        lambda *refs: back_kernel(first, spans, *refs),
         in_specs=[
             pl.BlockSpec(memory_space=pltpu.SMEM),
         ]
-        + [whole()] * (5 + len(before)),
+        + [whole()] * (3 + len(spans) + len(before)),
         out_specs=[whole()] * len(out_shape),
         out_shape=out_shape,
         scratch_shapes=scratch,
@@ -335,7 +345,7 @@
             flops=2 * N_CHIP * BLOCK * ROWS * EMB, bytes_accessed=10 * 2**20, transcendentals=0
         ),
         name="back",
-    )(place, grads, *weights, layer0, layer1, *before)
+    )(place, grads, layer0, layer1, *weights.values(), *before)
 
 
 def sum_kernel(parts_ref, send_ref):
@@ -401,15 +411,23 @@
 def shards(ids, mults, table, user_layer, user_head, item_layer, item_head, counts):
     place = jnp.stack([lax.axis_index("core"), lax.axis_index(DP), lax.axis_index("x_lo")])
     lookups = ids[0] + 1024 * mults[0]
-    both_weights, both_partial = pool(1, 1, place, lookups, table)
-    both_arrived = to_other(both_partial, "core")
-    x_weights, x_partial = pool(1, 0, place, lookups, table)
-    x_sum, lookups = lax.optimization_barrier((add(x_partial, both_arrived), lookups))
-    x_arrived = to_other(x_sum, "x_lo")
-    core_weights, core_partial = pool(0, 1, place, lookups, table)
+    half = N_Z // 2 * BLOCK
+    whole_x = N_Z * BLOCK
+    both = ((1, 0, N_Z), (0, 0, N_Z))
+    low, high, own = ((1, 0, N_Z // 2),), ((1, N_Z // 2, N_Z),), ((0, 0, N_Z),)
+    core_weights, core_partial = pool(both, 1, place, lookups, table)
     core_arrived = to_other(core_partial, "core")
-    own_weights, own_partial = pool(0, 0, place, lookups, table)
-    total_partial = add(own_partial, core_arrived, x_arrived)
+    low_weights, low_partial = pool(low, 0, place, lookups, table)
+    low_sum, lookups = lax.optimization_barrier((add(low_partial, core_arrived[:half]), lookups))
+    low_arrived = to_other(low_sum, "x_lo")
+    high_weights, high_partial = pool(high, 0, place, lookups, table)
+    high_sum, lookups = lax.optimization_barrier(
+        (add(high_partial, core_arrived[half:whole_x]), lookups)
+    )
+    high_arrived = to_other(high_sum, "x_lo")
+    own_weights, own_partial = pool(own, 0, place, lookups, table)
+    x_arrived = jnp.concatenate([low_arrived, high_arrived])
+    total_partial = add(own_partial, core_arrived[whole_x:], x_arrived)
     parts = exchange(total_partial.reshape(N_Z, BLOCK, EMB), "z")
     pooled, pre, hidden, unit, scale, units = towers(
         parts, counts, user_layer, user_head, item_layer, item_head
@@ -420,9 +438,10 @@
     )
     own_grads = exchange(grads, CHIPS)
     other_grads = to_other(own_grads, "core")
-    before = back(place, own_grads, (own_weights, x_weights), user_layer, item_layer)
+    weights = {own: own_weights, low: low_weights, high: high_weights}
+    before = back(place, own_grads, weights, user_layer, item_layer)
     (terms,) = back(
-        place, other_grads, (core_weights, both_weights), user_layer, item_layer, tuple(before)
+        place, other_grads, {both: core_weights}, user_layer, item_layer, tuple(before)
     )
     sums = exchange(sum_parts(exchange(terms, DP)), DP)
     table_change, layer0, head0, layer1, head1 = spread(sums)

time: 147 us -> 148 us (level)
  transfers between devices with their start and end apart: 4 -> 4, of which waited for: 1 -> 2; matrix products, arithmetic and copies ran while one was open for 0% -> 0% of each run, Pallas kernels for 9% -> 8%
where the time goes in v5:
time: 148 us; the launch traced here: 147 us
  blocking collectives  106 us (72%)
  Pallas kernels  23.9 us (16%)
  starting transfers between devices  9.8 us (7%)
  waiting for transfers between devices  4.49 us (3%)
  other arithmetic  1.53 us (1%)
    all_to_all x5, blocking collectives, exchange(): return lax.all_to_all(values, axes, 0, 0, tiled=True)  106 us
    pallas_call x4, Pallas kernels, pool(): pl.pallas_call(lambda *refs: pool_kernel(groups, other_core, *refs), in_s...  13.8 us
    ppermute x4, starting transfers between devices, to_other(): return lax.ppermute(values, axis, [(0, 1), (1, 0)])  9.8 us
    pallas_call x2, Pallas kernels, back(): pl.pallas_call(lambda *refs: back_kernel(first, spans, *refs), in_specs=[...  6.62 us
    ppermute x4, waiting for transfers between devices, to_other(): return lax.ppermute(values, axis, [(0, 1), (1, 0)])  4.49 us
  transfers between devices with their start and end apart: 4, of which 2 were waited for; matrix products, arithmetic and copies ran while one was open for 0% of the time, Pallas kernels for 8%

profile of v5, /device:TPU:8, one launch (start us, length us, event | category | flops | bytes accessed | tf_op | source)
XLA Modules:
  0.0 147.2 jit_solution(6887240624641706145)
XLA Ops:
  0.6 0.0 copy-start.6
  0.7 1.1 add_bitcast_fusion.refs_1_
  1.8 0.1 pad_add_fusion.refs_0_.place_ref
  1.8 0.9 copy-done.5
  2.8 5.8 %pool.5 = (bf16[4096,1024]{1,0:T(8,128)(2,1)S(1)}, bf16[4096,128]{1,0:T(8,128)(2,1)S(1)}) custom-call(s32[3]{0:T(128)S(1)} %pad_add_fusion.refs_0_.place_ref, s32[512,128]{1,0:T(8,128)S(1)} %add_bitcast_fusion.refs_1_, bf16[1024,128]{1,0:T(8,128)(2,1)S(1)} %copy-done.5), custom_call_target="tpu_custom_call" | custom-call | flops 2147483648 | bytes 8388608 | tf_op jit(solution)/shard_map/pool/pallas_call | solution.py:107
  8.6 1.9 %collective-permute-start = (bf16[4096,128]{1,0:T(8,128)(2,1)S(1)}, bf16[4096,128]{1,0:T(8,128)(2,1)S(1)}, u32[]{:S(2)}, u32[]{:S(2)}) collective-permute-start(bf16[4096,128]{1,0:T(8,128)(2,1)S(1)} %get-tuple-element.35), channel_id=1, source_target_pairs={{0,16},{16,0},{1,17},{17,1},{2,18},{18,2},{3,19},{19,3},{4,20},{20... | collective-permute-start | bytes 3145736 | tf_op jit(solution)/shard_map/ppermute | solution.py:404
  10.5 2.3 %pool.4 = (bf16[1024,1024]{1,0:T(8,128)(2,1)S(1)}, bf16[1024,128]{1,0:T(8,128)(2,1)S(1)}) custom-call(s32[3]{0:T(128)S(1)} %pad_add_fusion.refs_0_.place_ref, s32[512,128]{1,0:T(8,128)S(1)} %add_bitcast_fusion.refs_1_, bf16[1024,128]{1,0:T(8,128)(2,1)S(1)} %copy-done.6), custom_call_target="tpu_custom_call" | custom-call | flops 536870912 | bytes 2097152 | tf_op jit(solution)/shard_map/pool/pallas_call | solution.py:107
  12.9 0.3 collective-permute-done
  13.2 0.1 add_convert_fusion.2
  13.2 3.4 %collective-permute-start.1 = (bf16[1024,128]{1,0:T(8,128)(2,1)S(1)}, bf16[1024,128]{1,0:T(8,128)(2,1)S(1)}, u32[]{:S(2)}, u32[]{:S(2)}) collective-permute-start(bf16[1024,128]{1,0:T(8,128)(2,1)S(1)} %add_convert_fusion.2), channel_id=1, source_target_pairs={{0,256},{256,0},{1,257},{257,1},{2,258},{258,2},{3,259},{259,3},{4... | collective-permute-start | bytes 786440 | tf_op jit(solution)/shard_map/ppermute | solution.py:404
  16.6 2.3 %pool.6 = (bf16[1024,1024]{1,0:T(8,128)(2,1)S(1)}, bf16[1024,128]{1,0:T(8,128)(2,1)S(1)}) custom-call(s32[3]{0:T(128)S(1)} %pad_add_fusion.refs_0_.place_ref, s32[512,128]{1,0:T(8,128)S(1)} %add_bitcast_fusion.refs_1_, bf16[1024,128]{1,0:T(8,128)(2,1)S(1)} %copy-done.6), custom_call_target="tpu_custom_call" | custom-call | flops 536870912 | bytes 2097152 | tf_op jit(solution)/shard_map/pool/pallas_call | solution.py:107
  19.0 0.0 copy-start
  19.0 0.0 copy-start.1
  19.0 0.0 copy-start.2
  19.0 0.0 copy-start.3
  19.0 0.1 add_convert_fusion.1
  19.1 2.6 %collective-permute-start.2 = (bf16[1024,128]{1,0:T(8,128)(2,1)S(1)}, bf16[1024,128]{1,0:T(8,128)(2,1)S(1)}, u32[]{:S(2)}, u32[]{:S(2)}) collective-permute-start(bf16[1024,128]{1,0:T(8,128)(2,1)S(1)} %add_convert_fusion.1), channel_id=1, source_target_pairs={{0,256},{256,0},{1,257},{257,1},{2,258},{258,2},{3,259},{259,3},{4... | collective-permute-start | bytes 786440 | tf_op jit(solution)/shard_map/ppermute | solution.py:404
  21.7 3.4 %pool.7 = (bf16[2048,1024]{1,0:T(8,128)(2,1)S(1)}, bf16[2048,128]{1,0:T(8,128)(2,1)S(1)}) custom-call(s32[3]{0:T(128)S(1)} %pad_add_fusion.refs_0_.place_ref, s32[512,128]{1,0:T(8,128)S(1)} %add_bitcast_fusion.refs_1_, bf16[1024,128]{1,0:T(8,128)(2,1)S(1)} %copy-done.6), custom_call_target="tpu_custom_call" | custom-call | flops 1073741824 | bytes 4194304 | tf_op jit(solution)/shard_map/pool/pallas_call | solution.py:107
  25.1 4.2 %collective-permute-done.2 = bf16[1024,128]{1,0:T(8,128)(2,1)S(1)} collective-permute-done((bf16[1024,128]{1,0:T(8,128)(2,1)S(1)}, bf16[1024,128]{1,0:T(8,128)(2,1)S(1)}, u32[]{:S(2)}, u32[]{:S(2)}) %collective-permute-start.2) | collective-permute-done | bytes 262176 | tf_op jit(solution)/shard_map/ppermute | solution.py:404
  29.3 0.2 add_convert_fusion
  29.5 26.9 %all_to_all.25.parts_ref = bf16[8,256,128]{2,1,0:T(8,128)(2,1)S(1)} all-to-all(bf16[8,256,128]{2,1,0:T(8,128)(2,1)S(1)} %bitcast.6), channel_id=1, replica_groups=mesh['x_lo'=2,'z'=8,'core'=2,'x_hi'=2,'y'=8] {'z'}, dimensions={0} | all-to-all | bytes 1048576 | tf_op jit(solution)/shard_map/all_to_all | solution.py:400
  56.4 0.8 towers.1
  57.2 19.9 %all_to_all.26.group_ref = bf16[16,48,128]{2,1,0:T(8,128)(2,1)S(1)} all-to-all(bf16[16,48,128]{2,1,0:T(8,128)(2,1)S(1)} %get-tuple-element.42), channel_id=1, replica_groups=mesh['x_lo'=2,'z'=8,'core'=2,'x_hi'=2,'y'=8] {'x_hi','y'}, dimensions={0} | all-to-all | bytes 393216 | tf_op jit(solution)/shard_map/all_to_all | solution.py:400
  77.2 1.7 %softmax_back.1 = (f32[1,16]{1,0:T(1,128)}, bf16[16,16,1536]{2,1,0:T(8,128)(2,1)S(1)}) custom-call(s32[3]{0:T(128)S(1)} %pad_add_fusion.refs_0_.place_ref, bf16[16,48,128]{2,1,0:T(8,128)(2,1)S(1)} %all_to_all.26.group_ref, s32[1,16]{1,0:T(1,128)S(1)} %copy-done.4, bf16[16,2048]{1,0:T(8,128)(2,1)S(1)} %get-tuple-element.43.pooled_ref, ...), custom_call_target="tpu_custom_call" | custom-call | tf_op jit(solution)/shard_map/softmax_back/pallas_call | solution.py:246
  78.8 21.4 %all_to_all.27.refs_1_ = bf16[16,16,1536]{2,1,0:T(8,128)(2,1)S(1)} all-to-all(bf16[16,16,1536]{2,1,0:T(8,128)(2,1)S(1)} %get-tuple-element.49), channel_id=1, replica_groups=mesh['x_lo'=2,'z'=8,'core'=2,'x_hi'=2,'y'=8] {'x_lo','z'}, dimensions={0} | all-to-all | bytes 1572864 | tf_op jit(solution)/shard_map/all_to_all | solution.py:400
  100.2 1.9 %collective-permute-start.3 = (bf16[16,16,1536]{2,1,0:T(8,128)(2,1)S(1)}, bf16[16,16,1536]{2,1,0:T(8,128)(2,1)S(1)}, u32[]{:S(2)}, u32[]{:S(2)}) collective-permute-start(bf16[16,16,1536]{2,1,0:T(8,128)(2,1)S(1)} %all_to_all.27.refs_1_), channel_id=1, source_target_pairs={{0,16},{16,0},{1,17},{17,1},{2,18},{18,2},{3,19},{19,3},{4,20},{20... | collective-permute-start | bytes 2359304 | tf_op jit(solution)/shard_map/ppermute | solution.py:404
  102.2 3.2 %back.2 = (f32[128,1024]{1,0:T(8,128)S(1)}, f32[2,64,512]{2,1,0:T(8,128)S(1)}, f32[2,32,128]{2,1,0:T(8,128)S(1)}) custom-call(s32[3]{0:T(128)S(1)} %pad_add_fusion.refs_0_.place_ref, bf16[16,16,1536]{2,1,0:T(8,128)(2,1)S(1)} %all_to_all.27.refs_1_, bf16[1024,512]{1,0:T(8,128)(2,1)S(1)} %copy-done, bf16[1024,512]{1,0:T(8,128)(2,1)S(1)} %copy-done.1, ...), custom_call_target="tpu_custom_call" | custom-call | flops 1073741824 | bytes 10485760 | tf_op jit(solution)/shard_map/back/pallas_call | solution.py:334
  105.4 3.4 %back.3 = bf16[16,88,128]{2,1,0:T(8,128)(2,1)S(1)} custom-call(s32[3]{0:T(128)S(1)} %pad_add_fusion.refs_0_.place_ref, bf16[16,16,1536]{2,1,0:T(8,128)(2,1)S(1)} %collective-permute-done.3.refs_1_, bf16[1024,512]{1,0:T(8,128)(2,1)S(1)} %copy-done, bf16[1024,512]{1,0:T(8,128)(2,1)S(1)} %copy-done.1, bf16[4096,1024]{1,0:T(8,128)(2,1)S(1)} %get-tuple-element.50.refs_4_, ...), custom_call_target="tpu_custom_call" | custom-call | flops 1073741824 | bytes 10485760 | tf_op jit(solution)/shard_map/back/pallas_call | solution.py:334
  108.8 18.8 %all_to_all.28.parts_ref = bf16[16,88,128]{2,1,0:T(8,128)(2,1)S(1)} all-to-all(bf16[16,88,128]{2,1,0:T(8,128)(2,1)S(1)} %back.3), channel_id=1, replica_groups=mesh['x_lo'=2,'z'=8,'core'=2,'x_hi'=2,'y'=8] {'x_hi','y'}, dimensions={0} | all-to-all | bytes 720896 | tf_op jit(solution)/shard_map/all_to_all | solution.py:400
  127.7 0.1 sum_parts.1
  127.7 18.6 %all_to_all.29.sums_ref = bf16[16,88,128]{2,1,0:T(8,128)(2,1)S(1)} all-to-all(bf16[16,88,128]{2,1,0:T(8,128)(2,1)S(1)} %sum_parts.1), channel_id=1, replica_groups=mesh['x_lo'=2,'z'=8,'core'=2,'x_hi'=2,'y'=8] {'x_hi','y'}, dimensions={0} | all-to-all | bytes 720896 | tf_op jit(solution)/shard_map/all_to_all | solution.py:400
  146.4 0.9 spread.1
  (10 shorter events, 0.0 us)
Async XLA Ops:
  0.6 9.9 %copy-start.6 = (bf16[1024,128]{1,0:T(8,128)(2,1)S(1)}, bf16[1024,128]{1,0:T(8,128)(2,1)}, u32[]{:S(2)}) copy-start(bf16[1024,128]{1,0:T(8,128)(2,1)} %refs_2_.9) | copy-start | bytes 786436
  1.8 1.0 copy-start.5
  8.6 4.6 %collective-permute-start = (bf16[4096,128]{1,0:T(8,128)(2,1)S(1)}, bf16[4096,128]{1,0:T(8,128)(2,1)S(1)}, u32[]{:S(2)}, u32[]{:S(2)}) collective-permute-start(bf16[4096,128]{1,0:T(8,128)(2,1)S(1)} %get-tuple-element.35), channel_id=1, source_target_pairs={{0,16},{16,0},{1,17},{17,1},{2,18},{18,2},{3,19},{19,3},{4,20},{20... | collective-permute-start | bytes 3145736 | tf_op jit(solution)/shard_map/ppermute | solution.py:404
  13.2 11.9 %collective-permute-start.1 = (bf16[1024,128]{1,0:T(8,128)(2,1)S(1)}, bf16[1024,128]{1,0:T(8,128)(2,1)S(1)}, u32[]{:S(2)}, u32[]{:S(2)}) collective-permute-start(bf16[1024,128]{1,0:T(8,128)(2,1)S(1)} %add_convert_fusion.2), channel_id=1, source_target_pairs={{0,256},{256,0},{1,257},{257,1},{2,258},{258,2},{3,259},{259,3},{4... | collective-permute-start | bytes 786440 | tf_op jit(solution)/shard_map/ppermute | solution.py:404
  19.0 37.4 %copy-start = (bf16[1024,512]{1,0:T(8,128)(2,1)S(1)}, bf16[1024,512]{1,0:T(8,128)(2,1)}, u32[]{:S(2)}) copy-start(bf16[1024,512]{1,0:T(8,128)(2,1)} %refs_2_.11) | copy-start | bytes 3145732
  19.0 37.4 %copy-start.1 = (bf16[1024,512]{1,0:T(8,128)(2,1)S(1)}, bf16[1024,512]{1,0:T(8,128)(2,1)}, u32[]{:S(2)}) copy-start(bf16[1024,512]{1,0:T(8,128)(2,1)} %refs_3_.3) | copy-start | bytes 3145732
  19.0 37.4 %copy-start.2 = (bf16[512,128]{1,0:T(8,128)(2,1)S(1)}, bf16[512,128]{1,0:T(8,128)(2,1)}, u32[]{:S(2)}) copy-start(bf16[512,128]{1,0:T(8,128)(2,1)} %head0_ref.3) | copy-start | bytes 393220
  19.0 37.4 %copy-start.3 = (bf16[512,128]{1,0:T(8,128)(2,1)S(1)}, bf16[512,128]{1,0:T(8,128)(2,1)}, u32[]{:S(2)}) copy-start(bf16[512,128]{1,0:T(8,128)(2,1)} %head1_ref.3) | copy-start | bytes 393220
  19.0 37.4 %copy-start.4 = (s32[1,16]{1,0:T(1,128)S(1)}, s32[1,16]{1,0:T(1,128)}, u32[]{:S(2)}) copy-start(s32[1,16]{1,0:T(1,128)} %counts_ref.3) | copy-start | bytes 196
  19.1 10.2 %collective-permute-start.2 = (bf16[1024,128]{1,0:T(8,128)(2,1)S(1)}, bf16[1024,128]{1,0:T(8,128)(2,1)S(1)}, u32[]{:S(2)}, u32[]{:S(2)}) collective-permute-start(bf16[1024,128]{1,0:T(8,128)(2,1)S(1)} %add_convert_fusion.1), channel_id=1, source_target_pairs={{0,256},{256,0},{1,257},{257,1},{2,258},{258,2},{3,259},{259,3},{4... | collective-permute-start | bytes 786440 | tf_op jit(solution)/shard_map/ppermute | solution.py:404
  100.2 5.2 %collective-permute-start.3 = (bf16[16,16,1536]{2,1,0:T(8,128)(2,1)S(1)}, bf16[16,16,1536]{2,1,0:T(8,128)(2,1)S(1)}, u32[]{:S(2)}, u32[]{:S(2)}) collective-permute-start(bf16[16,16,1536]{2,1,0:T(8,128)(2,1)S(1)} %all_to_all.27.refs_1_), channel_id=1, source_target_pairs={{0,16},{16,0},{1,17},{17,1},{2,18},{18,2},{3,19},{19,3},{4,20},{20... | collective-permute-start | bytes 2359304 | tf_op jit(solution)/shard_map/ppermute | solution.py:404

commit v6 on v4

--- a/solution.py
+++ b/solution.py
@@ -136,7 +136,7 @@
     total = parts_ref[0].astype(F32)
     for s in range(1, N_Z):
         total = total + parts_ref[s].astype(F32)
-    rows_ref[...] = total
+    rows_ref[:BLOCK, :] = total
     for f in range(FEATURES):
         pooled_ref[:, f * EMB : (f + 1) * EMB] = rows_ref[
             pl.ds(f, OWN, stride=FEATURES), :
@@ -174,7 +174,7 @@
             jax.ShapeDtypeStruct((OWN, 2 * OUT), F32),
             jax.ShapeDtypeStruct((N_DP, 3 * OWN, 128), BF16),
         ],
-        scratch_shapes=[pltpu.VMEM((BLOCK, EMB), F32)],
+        scratch_shapes=[pltpu.VMEM((BLOCK + FEATURES, EMB), F32)],
         compiler_params=room(8),
         name="towers",
     )(parts, counts, layer0, head0, layer1, head1)
@@ -314,7 +314,7 @@
     total = jax.ShapeDtypeStruct((EMB, ROWS), F32)
     layers = jax.ShapeDtypeStruct((2, 64, HID), F32)
     heads = jax.ShapeDtypeStruct((2, 32, OUT), F32)
-    scratch = [pltpu.VMEM((N_CHIP * BLOCK, EMB), F32)]
+    scratch = [pltpu.VMEM((N_CHIP * BLOCK + FEATURES, EMB), F32)]
     if first:
         out_shape = [total, layers, heads]
     else:

time: 147 us -> 147 us (level)
  no operation moved by 1% of the time
where the time goes in v6:
time: 147 us; the launch traced here: 146 us
  blocking collectives  106 us (72%)
  Pallas kernels  23.6 us (16%)
  starting transfers between devices  9.62 us (7%)
  waiting for transfers between devices  3.68 us (3%)
  other arithmetic  1.49 us (1%)
    all_to_all x5, blocking collectives, exchange(): return lax.all_to_all(values, axes, 0, 0, tiled=True)  106 us
    pallas_call x4, Pallas kernels, pool(): pl.pallas_call(lambda *refs: pool_kernel(other_x, other_core, *refs), in_...  13.6 us
    ppermute x4, starting transfers between devices, to_other(): return lax.ppermute(values, axis, [(0, 1), (1, 0)])  9.62 us
    pallas_call x2, Pallas kernels, back(): pl.pallas_call(lambda *refs: back_kernel(first, *refs), in_specs=[pl.Bloc...  6.56 us
    ppermute x4, waiting for transfers between devices, to_other(): return lax.ppermute(values, axis, [(0, 1), (1, 0)])  3.68 us
  transfers between devices with their start and end apart: 4, of which 1 were waited for; matrix products, arithmetic and copies ran while one was open for 0% of the time, Pallas kernels for 9%

profile of v6, /device:TPU:8, one launch (start us, length us, event | category | flops | bytes accessed | tf_op | source)
XLA Modules:
  0.0 146.3 jit_solution(17019861330691806295)
XLA Ops:
  0.6 1.1 add_bitcast_fusion.refs_1_
  1.7 0.1 pad_add_fusion.refs_0_.place_ref
  1.8 0.9 copy-done.5
  2.7 3.4 %pool.5 = (bf16[2048,1024]{1,0:T(8,128)(2,1)S(1)}, bf16[2048,128]{1,0:T(8,128)(2,1)S(1)}) custom-call(s32[3]{0:T(128)S(1)} %pad_add_fusion.refs_0_.place_ref, s32[512,128]{1,0:T(8,128)S(1)} %add_bitcast_fusion.refs_1_, bf16[1024,128]{1,0:T(8,128)(2,1)S(1)} %copy-done.5), custom_call_target="tpu_custom_call" | custom-call | flops 1073741824 | bytes 5242880 | tf_op jit(solution)/shard_map/pool/pallas_call | solution.py:102
  6.1 0.0 copy-start.6
  6.1 2.1 %collective-permute-start = (bf16[2048,128]{1,0:T(8,128)(2,1)S(1)}, bf16[2048,128]{1,0:T(8,128)(2,1)S(1)}, u32[]{:S(2)}, u32[]{:S(2)}) collective-permute-start(bf16[2048,128]{1,0:T(8,128)(2,1)S(1)} %get-tuple-element.33), channel_id=1, source_target_pairs={{0,16},{16,0},{1,17},{17,1},{2,18},{18,2},{3,19},{19,3},{4,20},{20... | collective-permute-start | bytes 1572872 | tf_op jit(solution)/shard_map/ppermute | solution.py:394
  8.2 3.4 %pool.4 = (bf16[2048,1024]{1,0:T(8,128)(2,1)S(1)}, bf16[2048,128]{1,0:T(8,128)(2,1)S(1)}) custom-call(s32[3]{0:T(128)S(1)} %pad_add_fusion.refs_0_.place_ref, s32[512,128]{1,0:T(8,128)S(1)} %add_bitcast_fusion.refs_1_, bf16[1024,128]{1,0:T(8,128)(2,1)S(1)} %copy-done.5), custom_call_target="tpu_custom_call" | custom-call | flops 1073741824 | bytes 5242880 | tf_op jit(solution)/shard_map/pool/pallas_call | solution.py:102
  11.6 0.0 collective-permute-done
  11.6 0.1 add_convert_fusion.1
  11.8 3.4 %collective-permute-start.2 = (bf16[2048,128]{1,0:T(8,128)(2,1)S(1)}, bf16[2048,128]{1,0:T(8,128)(2,1)S(1)}, u32[]{:S(2)}, u32[]{:S(2)}) collective-permute-start(bf16[2048,128]{1,0:T(8,128)(2,1)S(1)} %add_convert_fusion.1), channel_id=1, source_target_pairs={{0,256},{256,0},{1,257},{257,1},{2,258},{258,2},{3,259},{259,3},{4... | collective-permute-start | bytes 1572872 | tf_op jit(solution)/shard_map/ppermute | solution.py:394
  15.2 3.4 %pool.7 = (bf16[2048,1024]{1,0:T(8,128)(2,1)S(1)}, bf16[2048,128]{1,0:T(8,128)(2,1)S(1)}) custom-call(s32[3]{0:T(128)S(1)} %pad_add_fusion.refs_0_.place_ref, s32[512,128]{1,0:T(8,128)S(1)} %add_bitcast_fusion.refs_1_, bf16[1024,128]{1,0:T(8,128)(2,1)S(1)} %copy-done.5), custom_call_target="tpu_custom_call" | custom-call | flops 1073741824 | bytes 5242880 | tf_op jit(solution)/shard_map/pool/pallas_call | solution.py:102
  18.6 0.0 copy-start
  18.6 0.0 copy-start.1
  18.6 0.0 copy-start.2
  18.6 0.0 copy-start.3
  18.6 0.0 copy-start.4
  18.6 2.3 %collective-permute-start.1 = (bf16[2048,128]{1,0:T(8,128)(2,1)S(1)}, bf16[2048,128]{1,0:T(8,128)(2,1)S(1)}, u32[]{:S(2)}, u32[]{:S(2)}) collective-permute-start(bf16[2048,128]{1,0:T(8,128)(2,1)S(1)} %get-tuple-element.36), channel_id=1, source_target_pairs={{0,16},{16,0},{1,17},{17,1},{2,18},{18,2},{3,19},{19,3},{4,20},{20... | collective-permute-start | bytes 1572872 | tf_op jit(solution)/shard_map/ppermute | solution.py:394
  20.9 3.4 %pool.6 = (bf16[2048,1024]{1,0:T(8,128)(2,1)S(1)}, bf16[2048,128]{1,0:T(8,128)(2,1)S(1)}) custom-call(s32[3]{0:T(128)S(1)} %pad_add_fusion.refs_0_.place_ref, s32[512,128]{1,0:T(8,128)S(1)} %add_bitcast_fusion.refs_1_, bf16[1024,128]{1,0:T(8,128)(2,1)S(1)} %copy-done.6), custom_call_target="tpu_custom_call" | custom-call | flops 1073741824 | bytes 5242880 | tf_op jit(solution)/shard_map/pool/pallas_call | solution.py:102
  24.3 3.7 %collective-permute-done.2 = bf16[2048,128]{1,0:T(8,128)(2,1)S(1)} collective-permute-done((bf16[2048,128]{1,0:T(8,128)(2,1)S(1)}, bf16[2048,128]{1,0:T(8,128)(2,1)S(1)}, u32[]{:S(2)}, u32[]{:S(2)}) %collective-permute-start.2) | collective-permute-done | bytes 524320 | tf_op jit(solution)/shard_map/ppermute | solution.py:394
  28.0 0.2 add_convert_fusion
  28.2 27.5 %all_to_all.25.parts_ref = bf16[8,256,128]{2,1,0:T(8,128)(2,1)S(1)} all-to-all(bf16[8,256,128]{2,1,0:T(8,128)(2,1)S(1)} %bitcast.6), channel_id=1, replica_groups=mesh['x_lo'=2,'z'=8,'core'=2,'x_hi'=2,'y'=8] {'z'}, dimensions={0} | all-to-all | bytes 1048576 | tf_op jit(solution)/shard_map/all_to_all | solution.py:390
  55.7 0.8 towers.1
  56.5 20.0 %all_to_all.26.group_ref = bf16[16,48,128]{2,1,0:T(8,128)(2,1)S(1)} all-to-all(bf16[16,48,128]{2,1,0:T(8,128)(2,1)S(1)} %get-tuple-element.38), channel_id=1, replica_groups=mesh['x_lo'=2,'z'=8,'core'=2,'x_hi'=2,'y'=8] {'x_hi','y'}, dimensions={0} | all-to-all | bytes 393216 | tf_op jit(solution)/shard_map/all_to_all | solution.py:390
  76.6 1.7 %softmax_back.1 = (f32[1,16]{1,0:T(1,128)}, bf16[16,16,1536]{2,1,0:T(8,128)(2,1)S(1)}) custom-call(s32[3]{0:T(128)S(1)} %pad_add_fusion.refs_0_.place_ref, bf16[16,48,128]{2,1,0:T(8,128)(2,1)S(1)} %all_to_all.26.group_ref, s32[1,16]{1,0:T(1,128)S(1)} %copy-done.4, bf16[16,2048]{1,0:T(8,128)(2,1)S(1)} %get-tuple-element.39.pooled_ref, ...), custom_call_target="tpu_custom_call" | custom-call | tf_op jit(solution)/shard_map/softmax_back/pallas_call | solution.py:241
  78.3 21.1 %all_to_all.27.refs_1_ = bf16[16,16,1536]{2,1,0:T(8,128)(2,1)S(1)} all-to-all(bf16[16,16,1536]{2,1,0:T(8,128)(2,1)S(1)} %get-tuple-element.45), channel_id=1, replica_groups=mesh['x_lo'=2,'z'=8,'core'=2,'x_hi'=2,'y'=8] {'x_lo','z'}, dimensions={0} | all-to-all | bytes 1572864 | tf_op jit(solution)/shard_map/all_to_all | solution.py:390
  99.3 1.9 %collective-permute-start.3 = (bf16[16,16,1536]{2,1,0:T(8,128)(2,1)S(1)}, bf16[16,16,1536]{2,1,0:T(8,128)(2,1)S(1)}, u32[]{:S(2)}, u32[]{:S(2)}) collective-permute-start(bf16[16,16,1536]{2,1,0:T(8,128)(2,1)S(1)} %all_to_all.27.refs_1_), channel_id=1, source_target_pairs={{0,16},{16,0},{1,17},{17,1},{2,18},{18,2},{3,19},{19,3},{4,20},{20... | collective-permute-start | bytes 2359304 | tf_op jit(solution)/shard_map/ppermute | solution.py:394
  101.2 3.3 %back.2 = (f32[128,1024]{1,0:T(8,128)S(1)}, f32[2,64,512]{2,1,0:T(8,128)S(1)}, f32[2,32,128]{2,1,0:T(8,128)S(1)}) custom-call(s32[3]{0:T(128)S(1)} %pad_add_fusion.refs_0_.place_ref, bf16[16,16,1536]{2,1,0:T(8,128)(2,1)S(1)} %all_to_all.27.refs_1_, bf16[2048,1024]{1,0:T(8,128)(2,1)S(1)} %get-tuple-element.48.refs_2_, ...), custom_call_target="tpu_custom_call" | custom-call | flops 1073741824 | bytes 10485760 | tf_op jit(solution)/shard_map/back/pallas_call | solution.py:324
  104.5 3.3 %back.3 = bf16[16,88,128]{2,1,0:T(8,128)(2,1)S(1)} custom-call(s32[3]{0:T(128)S(1)} %pad_add_fusion.refs_0_.place_ref, bf16[16,16,1536]{2,1,0:T(8,128)(2,1)S(1)} %collective-permute-done.3.refs_1_, bf16[2048,1024]{1,0:T(8,128)(2,1)S(1)} %get-tuple-element.46.refs_2_, bf16[2048,1024]{1,0:T(8,128)(2,1)S(1)} %get-tuple-element.47.refs_3_, ...), custom_call_target="tpu_custom_call" | custom-call | flops 1073741824 | bytes 10485760 | tf_op jit(solution)/shard_map/back/pallas_call | solution.py:324
  107.8 18.8 %all_to_all.28.parts_ref = bf16[16,88,128]{2,1,0:T(8,128)(2,1)S(1)} all-to-all(bf16[16,88,128]{2,1,0:T(8,128)(2,1)S(1)} %back.3), channel_id=1, replica_groups=mesh['x_lo'=2,'z'=8,'core'=2,'x_hi'=2,'y'=8] {'x_hi','y'}, dimensions={0} | all-to-all | bytes 720896 | tf_op jit(solution)/shard_map/all_to_all | solution.py:390
  126.7 0.1 sum_parts.1
  126.7 18.7 %all_to_all.29.sums_ref = bf16[16,88,128]{2,1,0:T(8,128)(2,1)S(1)} all-to-all(bf16[16,88,128]{2,1,0:T(8,128)(2,1)S(1)} %sum_parts.1), channel_id=1, replica_groups=mesh['x_lo'=2,'z'=8,'core'=2,'x_hi'=2,'y'=8] {'x_hi','y'}, dimensions={0} | all-to-all | bytes 720896 | tf_op jit(solution)/shard_map/all_to_all | solution.py:390
  145.4 0.9 spread.1
  (9 shorter events, 0.0 us)
Async XLA Ops:
  1.8 1.0 copy-start.5
  6.1 14.8 %copy-start.6 = (bf16[1024,128]{1,0:T(8,128)(2,1)S(1)}, bf16[1024,128]{1,0:T(8,128)(2,1)}, u32[]{:S(2)}) copy-start(bf16[1024,128]{1,0:T(8,128)(2,1)} %refs_2_.7) | copy-start | bytes 786436
  6.1 5.5 %collective-permute-start = (bf16[2048,128]{1,0:T(8,128)(2,1)S(1)}, bf16[2048,128]{1,0:T(8,128)(2,1)S(1)}, u32[]{:S(2)}, u32[]{:S(2)}) collective-permute-start(bf16[2048,128]{1,0:T(8,128)(2,1)S(1)} %get-tuple-element.33), channel_id=1, source_target_pairs={{0,16},{16,0},{1,17},{17,1},{2,18},{18,2},{3,19},{19,3},{4,20},{20... | collective-permute-start | bytes 1572872 | tf_op jit(solution)/shard_map/ppermute | solution.py:394
  11.8 16.2 %collective-permute-start.2 = (bf16[2048,128]{1,0:T(8,128)(2,1)S(1)}, bf16[2048,128]{1,0:T(8,128)(2,1)S(1)}, u32[]{:S(2)}, u32[]{:S(2)}) collective-permute-start(bf16[2048,128]{1,0:T(8,128)(2,1)S(1)} %add_convert_fusion.1), channel_id=1, source_target_pairs={{0,256},{256,0},{1,257},{257,1},{2,258},{258,2},{3,259},{259,3},{4... | collective-permute-start | bytes 1572872 | tf_op jit(solution)/shard_map/ppermute | solution.py:394
  18.6 37.1 %copy-start = (bf16[1024,512]{1,0:T(8,128)(2,1)S(1)}, bf16[1024,512]{1,0:T(8,128)(2,1)}, u32[]{:S(2)}) copy-start(bf16[1024,512]{1,0:T(8,128)(2,1)} %refs_4_.3) | copy-start | bytes 3145732
  18.6 37.1 %copy-start.1 = (bf16[1024,512]{1,0:T(8,128)(2,1)S(1)}, bf16[1024,512]{1,0:T(8,128)(2,1)}, u32[]{:S(2)}) copy-start(bf16[1024,512]{1,0:T(8,128)(2,1)} %refs_5_.3) | copy-start | bytes 3145732
  18.6 37.1 %copy-start.2 = (bf16[512,128]{1,0:T(8,128)(2,1)S(1)}, bf16[512,128]{1,0:T(8,128)(2,1)}, u32[]{:S(2)}) copy-start(bf16[512,128]{1,0:T(8,128)(2,1)} %head0_ref.3) | copy-start | bytes 393220
  18.6 37.1 %copy-start.3 = (bf16[512,128]{1,0:T(8,128)(2,1)S(1)}, bf16[512,128]{1,0:T(8,128)(2,1)}, u32[]{:S(2)}) copy-start(bf16[512,128]{1,0:T(8,128)(2,1)} %head1_ref.3) | copy-start | bytes 393220
  18.6 37.1 %copy-start.4 = (s32[1,16]{1,0:T(1,128)S(1)}, s32[1,16]{1,0:T(1,128)}, u32[]{:S(2)}) copy-start(s32[1,16]{1,0:T(1,128)} %counts_ref.3) | copy-start | bytes 196
  18.6 9.4 %collective-permute-start.1 = (bf16[2048,128]{1,0:T(8,128)(2,1)S(1)}, bf16[2048,128]{1,0:T(8,128)(2,1)S(1)}, u32[]{:S(2)}, u32[]{:S(2)}) collective-permute-start(bf16[2048,128]{1,0:T(8,128)(2,1)S(1)} %get-tuple-element.36), channel_id=1, source_target_pairs={{0,16},{16,0},{1,17},{17,1},{2,18},{18,2},{3,19},{19,3},{4,20},{20... | collective-permute-start | bytes 1572872 | tf_op jit(solution)/shard_map/ppermute | solution.py:394
  99.3 5.2 %collective-permute-start.3 = (bf16[16,16,1536]{2,1,0:T(8,128)(2,1)S(1)}, bf16[16,16,1536]{2,1,0:T(8,128)(2,1)S(1)}, u32[]{:S(2)}, u32[]{:S(2)}) collective-permute-start(bf16[16,16,1536]{2,1,0:T(8,128)(2,1)S(1)} %all_to_all.27.refs_1_), channel_id=1, source_target_pairs={{0,16},{16,0},{1,17},{17,1},{2,18},{18,2},{3,19},{19,3},{4,20},{20... | collective-permute-start | bytes 2359304 | tf_op jit(solution)/shard_map/ppermute | solution.py:394

commit v7 on v6

--- a/solution.py
+++ b/solution.py
@@ -156,9 +156,11 @@
         for d in range(N_DP):
             send_ref[d, tower * OWN : (tower + 1) * OWN, :] = rounded
     counts = column_of(counts_ref[...].astype(F32))
-    spread = jnp.broadcast_to(counts, (OWN, 128)).astype(BF16)
+    spread = jnp.broadcast_to(counts, (OWN, 128))
+    left = lax.broadcasted_iota(jnp.int32, (OWN // 2, 128), 1) < 64
+    spread = jnp.where(left, spread[: OWN // 2], spread[OWN // 2 :]).astype(BF16)
     for d in range(N_DP):
-        send_ref[d, 2 * OWN : 3 * OWN, :] = spread
+        send_ref[d, 2 * OWN :, :] = spread
 
 
 def towers(parts, counts, layer0, head0, layer1, head1):
@@ -172,7 +174,7 @@
             jax.ShapeDtypeStruct((OWN, 2 * HID), BF16),
             jax.ShapeDtypeStruct((OWN, 2 * OUT), F32),
             jax.ShapeDtypeStruct((OWN, 2 * OUT), F32),
-            jax.ShapeDtypeStruct((N_DP, 3 * OWN, 128), BF16),
+            jax.ShapeDtypeStruct((N_DP, 2 * OWN + OWN // 2, 128), BF16),
         ],
         scratch_shapes=[pltpu.VMEM((BLOCK + FEATURES, EMB), F32)],
         compiler_params=room(8),
@@ -188,7 +190,9 @@
     group = group_ref[...]
     users = group[:, :OWN].reshape(size, OUT)
     items = group[:, OWN : 2 * OWN].reshape(size, OUT)
-    log_freq = jnp.log(group[:, 2 * OWN :].reshape(size, 128).astype(F32))
+    counts = group[:, 2 * OWN :].astype(F32)
+    counts = [jnp.concatenate([half, half], axis=2) for half in (counts[:, :, :64], counts[:, :, 64:])]
+    log_freq = jnp.log(jnp.concatenate(counts, axis=1).reshape(size, 128))
     log_row = jnp.transpose(log_freq)[:1]
     own_log = jnp.log(column_of(counts_ref[...].astype(F32)))
     own_user = unit_ref[:, :OUT].astype(BF16)

time: 147 us -> 146 us (level)
  no operation moved by 1% of the time
where the time goes in v7:
time: 146 us; the launch traced here: 145 us
  blocking collectives  105 us (72%)
  Pallas kernels  23.6 us (16%)
  starting transfers between devices  9.62 us (7%)
  waiting for transfers between devices  3.68 us (3%)
  other arithmetic  1.49 us (1%)
    all_to_all x5, blocking collectives, exchange(): return lax.all_to_all(values, axes, 0, 0, tiled=True)  105 us
    pallas_call x4, Pallas kernels, pool(): pl.pallas_call(lambda *refs: pool_kernel(other_x, other_core, *refs), in_...  13.6 us
    ppermute x4, starting transfers between devices, to_other(): return lax.ppermute(values, axis, [(0, 1), (1, 0)])  9.62 us
    pallas_call x2, Pallas kernels, back(): pl.pallas_call(lambda *refs: back_kernel(first, *refs), in_specs=[pl.Bloc...  6.56 us
    ppermute x4, waiting for transfers between devices, to_other(): return lax.ppermute(values, axis, [(0, 1), (1, 0)])  3.68 us
  transfers between devices with their start and end apart: 4, of which 1 were waited for; matrix products, arithmetic and copies ran while one was open for 0% of the time, Pallas kernels for 9%

profile of v7, /device:TPU:8, one launch (start us, length us, event | category | flops | bytes accessed | tf_op | source)
XLA Modules:
  0.0 145.4 jit_solution(15391919112498668377)
XLA Ops:
  0.6 1.1 add_bitcast_fusion.refs_1_
  1.7 0.1 pad_add_fusion.refs_0_.place_ref
  1.8 0.9 copy-done.5
  2.7 3.4 %pool.5 = (bf16[2048,1024]{1,0:T(8,128)(2,1)S(1)}, bf16[2048,128]{1,0:T(8,128)(2,1)S(1)}) custom-call(s32[3]{0:T(128)S(1)} %pad_add_fusion.refs_0_.place_ref, s32[512,128]{1,0:T(8,128)S(1)} %add_bitcast_fusion.refs_1_, bf16[1024,128]{1,0:T(8,128)(2,1)S(1)} %copy-done.5), custom_call_target="tpu_custom_call" | custom-call | flops 1073741824 | bytes 5242880 | tf_op jit(solution)/shard_map/pool/pallas_call | solution.py:102
  6.1 0.0 copy-start.6
  6.1 2.1 %collective-permute-start = (bf16[2048,128]{1,0:T(8,128)(2,1)S(1)}, bf16[2048,128]{1,0:T(8,128)(2,1)S(1)}, u32[]{:S(2)}, u32[]{:S(2)}) collective-permute-start(bf16[2048,128]{1,0:T(8,128)(2,1)S(1)} %get-tuple-element.33), channel_id=1, source_target_pairs={{0,16},{16,0},{1,17},{17,1},{2,18},{18,2},{3,19},{19,3},{4,20},{20... | collective-permute-start | bytes 1572872 | tf_op jit(solution)/shard_map/ppermute | solution.py:398
  8.2 3.4 %pool.4 = (bf16[2048,1024]{1,0:T(8,128)(2,1)S(1)}, bf16[2048,128]{1,0:T(8,128)(2,1)S(1)}) custom-call(s32[3]{0:T(128)S(1)} %pad_add_fusion.refs_0_.place_ref, s32[512,128]{1,0:T(8,128)S(1)} %add_bitcast_fusion.refs_1_, bf16[1024,128]{1,0:T(8,128)(2,1)S(1)} %copy-done.5), custom_call_target="tpu_custom_call" | custom-call | flops 1073741824 | bytes 5242880 | tf_op jit(solution)/shard_map/pool/pallas_call | solution.py:102
  11.6 0.0 collective-permute-done
  11.6 0.1 add_convert_fusion.1
  11.8 3.4 %collective-permute-start.2 = (bf16[2048,128]{1,0:T(8,128)(2,1)S(1)}, bf16[2048,128]{1,0:T(8,128)(2,1)S(1)}, u32[]{:S(2)}, u32[]{:S(2)}) collective-permute-start(bf16[2048,128]{1,0:T(8,128)(2,1)S(1)} %add_convert_fusion.1), channel_id=1, source_target_pairs={{0,256},{256,0},{1,257},{257,1},{2,258},{258,2},{3,259},{259,3},{4... | collective-permute-start | bytes 1572872 | tf_op jit(solution)/shard_map/ppermute | solution.py:398
  15.2 3.4 %pool.7 = (bf16[2048,1024]{1,0:T(8,128)(2,1)S(1)}, bf16[2048,128]{1,0:T(8,128)(2,1)S(1)}) custom-call(s32[3]{0:T(128)S(1)} %pad_add_fusion.refs_0_.place_ref, s32[512,128]{1,0:T(8,128)S(1)} %add_bitcast_fusion.refs_1_, bf16[1024,128]{1,0:T(8,128)(2,1)S(1)} %copy-done.5), custom_call_target="tpu_custom_call" | custom-call | flops 1073741824 | bytes 5242880 | tf_op jit(solution)/shard_map/pool/pallas_call | solution.py:102
  18.6 0.0 copy-start
  18.6 0.0 copy-start.1
  18.6 0.0 copy-start.2
  18.6 0.0 copy-start.3
  18.6 0.0 copy-start.4
  18.6 2.3 %collective-permute-start.1 = (bf16[2048,128]{1,0:T(8,128)(2,1)S(1)}, bf16[2048,128]{1,0:T(8,128)(2,1)S(1)}, u32[]{:S(2)}, u32[]{:S(2)}) collective-permute-start(bf16[2048,128]{1,0:T(8,128)(2,1)S(1)} %get-tuple-element.36), channel_id=1, source_target_pairs={{0,16},{16,0},{1,17},{17,1},{2,18},{18,2},{3,19},{19,3},{4,20},{20... | collective-permute-start | bytes 1572872 | tf_op jit(solution)/shard_map/ppermute | solution.py:398
  20.9 3.4 %pool.6 = (bf16[2048,1024]{1,0:T(8,128)(2,1)S(1)}, bf16[2048,128]{1,0:T(8,128)(2,1)S(1)}) custom-call(s32[3]{0:T(128)S(1)} %pad_add_fusion.refs_0_.place_ref, s32[512,128]{1,0:T(8,128)S(1)} %add_bitcast_fusion.refs_1_, bf16[1024,128]{1,0:T(8,128)(2,1)S(1)} %copy-done.6), custom_call_target="tpu_custom_call" | custom-call | flops 1073741824 | bytes 5242880 | tf_op jit(solution)/shard_map/pool/pallas_call | solution.py:102
  24.3 3.7 %collective-permute-done.2 = bf16[2048,128]{1,0:T(8,128)(2,1)S(1)} collective-permute-done((bf16[2048,128]{1,0:T(8,128)(2,1)S(1)}, bf16[2048,128]{1,0:T(8,128)(2,1)S(1)}, u32[]{:S(2)}, u32[]{:S(2)}) %collective-permute-start.2) | collective-permute-done | bytes 524320 | tf_op jit(solution)/shard_map/ppermute | solution.py:398
  28.0 0.2 add_convert_fusion
  28.2 27.5 %all_to_all.25.parts_ref = bf16[8,256,128]{2,1,0:T(8,128)(2,1)S(1)} all-to-all(bf16[8,256,128]{2,1,0:T(8,128)(2,1)S(1)} %bitcast.6), channel_id=1, replica_groups=mesh['x_lo'=2,'z'=8,'core'=2,'x_hi'=2,'y'=8] {'z'}, dimensions={0} | all-to-all | bytes 1048576 | tf_op jit(solution)/shard_map/all_to_all | solution.py:394
  55.7 0.8 towers.1
  56.5 19.8 %all_to_all.26.group_ref = bf16[16,40,128]{2,1,0:T(8,128)(2,1)S(1)} all-to-all(bf16[16,40,128]{2,1,0:T(8,128)(2,1)S(1)} %get-tuple-element.38), channel_id=1, replica_groups=mesh['x_lo'=2,'z'=8,'core'=2,'x_hi'=2,'y'=8] {'x_hi','y'}, dimensions={0} | all-to-all | bytes 327680 | tf_op jit(solution)/shard_map/all_to_all | solution.py:394
  76.4 1.7 %softmax_back.1 = (f32[1,16]{1,0:T(1,128)}, bf16[16,16,1536]{2,1,0:T(8,128)(2,1)S(1)}) custom-call(s32[3]{0:T(128)S(1)} %pad_add_fusion.refs_0_.place_ref, bf16[16,40,128]{2,1,0:T(8,128)(2,1)S(1)} %all_to_all.26.group_ref, s32[1,16]{1,0:T(1,128)S(1)} %copy-done.4, bf16[16,2048]{1,0:T(8,128)(2,1)S(1)} %get-tuple-element.39.pooled_ref, ...), custom_call_target="tpu_custom_call" | custom-call | tf_op jit(solution)/shard_map/softmax_back/pallas_call | solution.py:245
  78.0 21.1 %all_to_all.27.refs_1_ = bf16[16,16,1536]{2,1,0:T(8,128)(2,1)S(1)} all-to-all(bf16[16,16,1536]{2,1,0:T(8,128)(2,1)S(1)} %get-tuple-element.45), channel_id=1, replica_groups=mesh['x_lo'=2,'z'=8,'core'=2,'x_hi'=2,'y'=8] {'x_lo','z'}, dimensions={0} | all-to-all | bytes 1572864 | tf_op jit(solution)/shard_map/all_to_all | solution.py:394
  99.1 1.9 %collective-permute-start.3 = (bf16[16,16,1536]{2,1,0:T(8,128)(2,1)S(1)}, bf16[16,16,1536]{2,1,0:T(8,128)(2,1)S(1)}, u32[]{:S(2)}, u32[]{:S(2)}) collective-permute-start(bf16[16,16,1536]{2,1,0:T(8,128)(2,1)S(1)} %all_to_all.27.refs_1_), channel_id=1, source_target_pairs={{0,16},{16,0},{1,17},{17,1},{2,18},{18,2},{3,19},{19,3},{4,20},{20... | collective-permute-start | bytes 2359304 | tf_op jit(solution)/shard_map/ppermute | solution.py:398
  101.0 3.3 %back.2 = (f32[128,1024]{1,0:T(8,128)S(1)}, f32[2,64,512]{2,1,0:T(8,128)S(1)}, f32[2,32,128]{2,1,0:T(8,128)S(1)}) custom-call(s32[3]{0:T(128)S(1)} %pad_add_fusion.refs_0_.place_ref, bf16[16,16,1536]{2,1,0:T(8,128)(2,1)S(1)} %all_to_all.27.refs_1_, bf16[2048,1024]{1,0:T(8,128)(2,1)S(1)} %get-tuple-element.48.refs_2_, ...), custom_call_target="tpu_custom_call" | custom-call | flops 1073741824 | bytes 10485760 | tf_op jit(solution)/shard_map/back/pallas_call | solution.py:328
  104.3 3.3 %back.3 = bf16[16,88,128]{2,1,0:T(8,128)(2,1)S(1)} custom-call(s32[3]{0:T(128)S(1)} %pad_add_fusion.refs_0_.place_ref, bf16[16,16,1536]{2,1,0:T(8,128)(2,1)S(1)} %collective-permute-done.3.refs_1_, bf16[2048,1024]{1,0:T(8,128)(2,1)S(1)} %get-tuple-element.46.refs_2_, bf16[2048,1024]{1,0:T(8,128)(2,1)S(1)} %get-tuple-element.47.refs_3_, ...), custom_call_target="tpu_custom_call" | custom-call | flops 1073741824 | bytes 10485760 | tf_op jit(solution)/shard_map/back/pallas_call | solution.py:328
  107.6 18.1 %all_to_all.28.parts_ref = bf16[16,88,128]{2,1,0:T(8,128)(2,1)S(1)} all-to-all(bf16[16,88,128]{2,1,0:T(8,128)(2,1)S(1)} %back.3), channel_id=1, replica_groups=mesh['x_lo'=2,'z'=8,'core'=2,'x_hi'=2,'y'=8] {'x_hi','y'}, dimensions={0} | all-to-all | bytes 720896 | tf_op jit(solution)/shard_map/all_to_all | solution.py:394
  125.8 0.1 sum_parts.1
  125.8 18.6 %all_to_all.29.sums_ref = bf16[16,88,128]{2,1,0:T(8,128)(2,1)S(1)} all-to-all(bf16[16,88,128]{2,1,0:T(8,128)(2,1)S(1)} %sum_parts.1), channel_id=1, replica_groups=mesh['x_lo'=2,'z'=8,'core'=2,'x_hi'=2,'y'=8] {'x_hi','y'}, dimensions={0} | all-to-all | bytes 720896 | tf_op jit(solution)/shard_map/all_to_all | solution.py:394
  144.5 0.9 spread.1
  (9 shorter events, 0.0 us)
Async XLA Ops:
  1.8 1.0 copy-start.5
  6.1 14.8 %copy-start.6 = (bf16[1024,128]{1,0:T(8,128)(2,1)S(1)}, bf16[1024,128]{1,0:T(8,128)(2,1)}, u32[]{:S(2)}) copy-start(bf16[1024,128]{1,0:T(8,128)(2,1)} %refs_2_.7) | copy-start | bytes 786436
  6.1 5.5 %collective-permute-start = (bf16[2048,128]{1,0:T(8,128)(2,1)S(1)}, bf16[2048,128]{1,0:T(8,128)(2,1)S(1)}, u32[]{:S(2)}, u32[]{:S(2)}) collective-permute-start(bf16[2048,128]{1,0:T(8,128)(2,1)S(1)} %get-tuple-element.33), channel_id=1, source_target_pairs={{0,16},{16,0},{1,17},{17,1},{2,18},{18,2},{3,19},{19,3},{4,20},{20... | collective-permute-start | bytes 1572872 | tf_op jit(solution)/shard_map/ppermute | solution.py:398
  11.8 16.2 %collective-permute-start.2 = (bf16[2048,128]{1,0:T(8,128)(2,1)S(1)}, bf16[2048,128]{1,0:T(8,128)(2,1)S(1)}, u32[]{:S(2)}, u32[]{:S(2)}) collective-permute-start(bf16[2048,128]{1,0:T(8,128)(2,1)S(1)} %add_convert_fusion.1), channel_id=1, source_target_pairs={{0,256},{256,0},{1,257},{257,1},{2,258},{258,2},{3,259},{259,3},{4... | collective-permute-start | bytes 1572872 | tf_op jit(solution)/shard_map/ppermute | solution.py:398
  18.6 37.1 %copy-start = (bf16[1024,512]{1,0:T(8,128)(2,1)S(1)}, bf16[1024,512]{1,0:T(8,128)(2,1)}, u32[]{:S(2)}) copy-start(bf16[1024,512]{1,0:T(8,128)(2,1)} %refs_4_.3) | copy-start | bytes 3145732
  18.6 37.1 %copy-start.1 = (bf16[1024,512]{1,0:T(8,128)(2,1)S(1)}, bf16[1024,512]{1,0:T(8,128)(2,1)}, u32[]{:S(2)}) copy-start(bf16[1024,512]{1,0:T(8,128)(2,1)} %refs_5_.3) | copy-start | bytes 3145732
  18.6 37.1 %copy-start.2 = (bf16[512,128]{1,0:T(8,128)(2,1)S(1)}, bf16[512,128]{1,0:T(8,128)(2,1)}, u32[]{:S(2)}) copy-start(bf16[512,128]{1,0:T(8,128)(2,1)} %head0_ref.3) | copy-start | bytes 393220
  18.6 37.1 %copy-start.3 = (bf16[512,128]{1,0:T(8,128)(2,1)S(1)}, bf16[512,128]{1,0:T(8,128)(2,1)}, u32[]{:S(2)}) copy-start(bf16[512,128]{1,0:T(8,128)(2,1)} %head1_ref.3) | copy-start | bytes 393220
  18.6 37.1 %copy-start.4 = (s32[1,16]{1,0:T(1,128)S(1)}, s32[1,16]{1,0:T(1,128)}, u32[]{:S(2)}) copy-start(s32[1,16]{1,0:T(1,128)} %counts_ref.3) | copy-start | bytes 196
  18.6 9.4 %collective-permute-start.1 = (bf16[2048,128]{1,0:T(8,128)(2,1)S(1)}, bf16[2048,128]{1,0:T(8,128)(2,1)S(1)}, u32[]{:S(2)}, u32[]{:S(2)}) collective-permute-start(bf16[2048,128]{1,0:T(8,128)(2,1)S(1)} %get-tuple-element.36), channel_id=1, source_target_pairs={{0,16},{16,0},{1,17},{17,1},{2,18},{18,2},{3,19},{19,3},{4,20},{20... | collective-permute-start | bytes 1572872 | tf_op jit(solution)/shard_map/ppermute | solution.py:398
  99.1 5.2 %collective-permute-start.3 = (bf16[16,16,1536]{2,1,0:T(8,128)(2,1)S(1)}, bf16[16,16,1536]{2,1,0:T(8,128)(2,1)S(1)}, u32[]{:S(2)}, u32[]{:S(2)}) collective-permute-start(bf16[16,16,1536]{2,1,0:T(8,128)(2,1)S(1)} %all_to_all.27.refs_1_), channel_id=1, source_target_pairs={{0,16},{16,0},{1,17},{17,1},{2,18},{18,2},{3,19},{19,3},{4,20},{20... | collective-permute-start | bytes 2359304 | tf_op jit(solution)/shard_map/ppermute | solution.py:398
